TPU v7x, 256 devices: a whole 4x4x8 slice. The times are simulated.
256 devices in a mesh: outer: 16 (over z, core), shard: 16 (over x, y).
Axes of the slice: x: 4, y: 4, z: 8, core: 2. Of those that a mesh axis runs over, the one named last changes fastest.
Arguments:
- base: float32 [5120, 1024], P('shard'), may hold values from -16 to 16
- local: bfloat16 [16, 5120, 1024], P('outer', 'shard'), may hold values from -28 to 28
- error: float32 [16, 5120, 1024], P('outer', 'shard'), may hold values from -4 to 4
- momentum: float32 [5120, 1024], P('shard'), may hold values from -4 to 4
- query: float32 [1024, 64], replicated, may hold values from -6 to 6
Outputs:
- new_base: float32 [5120, 1024], P('shard')
- new_error: float32 [16, 5120, 1024], P('outer', 'shard')
- new_momentum: float32 [5120, 1024], P('shard')
All inputs are finite; a program needn't handle non-finite values.
Results may differ from a plain program's by a relative error of at most 0.0003.
Values sent between devices are 32-bit elements; how exact they have to be, the bound alone decides.
No kernel may reach another device: no remote copies, remote signals or barrier semaphores. Data moves between devices by JAX's collectives and lax.ppermute only.
A program may use at most 64 MiB of HBM per device.

v0:
```python
import jax
import jax.numpy as jnp
from jax import lax
from jax.sharding import PartitionSpec as P

ITERS = 2


momentum_decay = 0.9
outer_rate = 0.7


def body(base, local, error, momentum, query):
    replicas = lax.axis_size("outer")
    field = base - local[0].astype(jnp.float32) + error[0]
    right = query
    basis = None
    for step in range(ITERS):
        left_part = jnp.dot(field, right, precision=lax.Precision.HIGHEST)
        left = lax.psum(left_part, "outer") / replicas
        gram_part = jnp.dot(left.T, left, precision=lax.Precision.HIGHEST)
        gram = lax.psum(gram_part, "shard")
        factor = jnp.linalg.cholesky(gram)
        basis = lax.linalg.triangular_solve(
            factor, left, left_side=False, lower=True, transpose_a=True
        )
        right_part = jnp.einsum("dk,dq->kq", field, basis, precision=lax.Precision.HIGHEST)
        right = lax.psum(right_part, ("outer", "shard")) / replicas
    approx = jnp.dot(basis, right.T, precision=lax.Precision.HIGHEST)
    new_error = (field - approx)[None]
    new_momentum = momentum_decay * momentum + approx
    new_base = base - outer_rate * (approx + momentum_decay * new_momentum)
    return (new_base, new_error, new_momentum)


def solution(mesh):
    in_specs = (
        P("shard", None),
        P("outer", "shard", None),
        P("outer", "shard", None),
        P("shard", None),
        P(),
    )
    out_specs = (P("shard", None), P("outer", "shard", None), P("shard", None))
    return jax.shard_map(body, mesh=mesh, in_specs=in_specs, out_specs=out_specs, check_vma=False)
```

profile of v0, /device:TPU:1, one launch (start us, length us, event | category | flops | bytes accessed | tf_op | source)
XLA Modules:
  0.0 913.6 jit_solution(13129653164021942056)
XLA Ops:
  7.2 2.3 fusion
  9.6 1.9 fusion.33
  11.5 107.6 %all-reduce.5.cloned.1.call-done = f32[320,64]{0,1:T(8,128)} async-done(((f32[320,64]{0,1:T(8,128)}), f32[320,64]{0,1:T(8,128)}) %all-reduce.5.cloned.1.call-update) | async-done | bytes 81936 | tf_op jit(solution)/shard_map/psum | solution.py:20
  119.2 1.2 fusion.11
  120.4 60.2 %psum.43 = f32[64,64]{0,1:T(8,128)S(1)} all-reduce(f32[64,64]{0,1:T(8,128)S(1)} %fusion.11), channel_id=1, replica_groups=mesh['outer'=16,'shard'=16] {'shard'}, use_global_device_ids=true, to_apply=%region_1.0 | all-reduce | flops 4096 | bytes 32768 | tf_op jit(solution)/shard_map/psum | solution.py:22
  180.7 5.8 cholesky.44
  186.6 0.6 compare_reduce_fusion.1
  187.3 0.7 fusion.17
  187.9 4.9 custom-call.6
  192.8 1.2 convolution_bitcast_fusion.1
  194.0 3.4 fusion.34
  197.5 259.6 %all-reduce.7.cloned.1.call-done = f32[1024,64]{1,0:T(8,128)} async-done(((f32[1024,64]{1,0:T(8,128)}), f32[1024,64]{1,0:T(8,128)}) %all-reduce.7.cloned.1.call-update) | async-done | bytes 262160 | tf_op jit(solution)/shard_map/psum | solution.py:28
  457.1 2.9 fusion.3
  460.1 104.0 %all-reduce.9.cloned.1.call-done = f32[320,64]{0,1:T(8,128)} async-done(((f32[320,64]{0,1:T(8,128)}), f32[320,64]{0,1:T(8,128)}) %all-reduce.9.cloned.1.call-update) | async-done | bytes 81936 | tf_op jit(solution)/shard_map/psum | solution.py:20
  564.1 1.2 fusion.8
  565.3 60.2 %psum.46 = f32[64,64]{0,1:T(8,128)S(1)} all-reduce(f32[64,64]{0,1:T(8,128)S(1)} %fusion.8), channel_id=1, replica_groups=mesh['outer'=16,'shard'=16] {'shard'}, use_global_device_ids=true, to_apply=%region_6.9 | all-reduce | flops 4096 | bytes 32768 | tf_op jit(solution)/shard_map/psum | solution.py:22
  625.7 5.8 cholesky.55
  631.5 0.6 compare_reduce_fusion
  632.2 0.7 fusion.18
  632.9 4.9 custom-call.7
  637.8 1.3 convolution_bitcast_fusion
  639.1 3.4 fusion.35
  642.5 259.6 %all-reduce.11.cloned.1.call-done = f32[1024,64]{1,0:T(8,128)} async-done(((f32[1024,64]{1,0:T(8,128)}), f32[1024,64]{1,0:T(8,128)}) %all-reduce.11.cloned.1.call-update) | async-done | bytes 262160 | tf_op jit(solution)/shard_map/psum | solution.py:28
  902.1 4.9 multiply_subtract_fusion
  (18 shorter events, 0.5 us)
Async XLA Ops:
  7.2 2.4 copy-start
  7.2 112.0 %all-reduce.5.cloned.1.call-start = ((), (), s32[]{:S(2)}) async-start(), calls=%async_computation | async-start | bytes 196608 | tf_op jit(solution)/shard_map/psum | solution.py:20
  11.5 445.6 %all-reduce.7.cloned.1.call-start = ((), (), s32[]{:S(2)}) async-start(), calls=%async_computation.1 | async-start | bytes 1048576 | tf_op jit(solution)/shard_map/psum | solution.py:28
  197.5 366.6 %all-reduce.9.cloned.1.call-start = ((), (), s32[]{:S(2)}) async-start(), calls=%async_computation.2 | async-start | bytes 196608 | tf_op jit(solution)/shard_map/psum | solution.py:20
  460.1 442.0 %all-reduce.11.cloned.1.call-start = ((), (), s32[]{:S(2)}) async-start(), calls=%async_computation.3 | async-start | bytes 1048576 | tf_op jit(solution)/shard_map/psum | solution.py:28
  637.7 264.3 %copy-start.1 = (f32[320,1024]{1,0:T(8,128)S(1)}, f32[320,1024]{1,0:T(8,128)}, u32[]{:S(2)}) copy-start(f32[320,1024]{1,0:T(8,128)} %param.8) | copy-start | bytes 3932164
Sparse Core Ops, SparseCore 0:
  11.6 107.5 all-reduce.4
  197.6 259.4 all-reduce.6
  460.2 103.8 all-reduce.8
  642.6 259.4 all-reduce.10
where the time goes:
time: 915 us; the launch traced here: 914 us
  waiting for transfers between devices  731 us (80%)
  blocking collectives  120 us (13%)
  other arithmetic  26.5 us (3%)
  matrix products  21.6 us (2%)
  between operations  13.9 us (2%)
    psum x2, waiting for transfers between devices, body(): right = lax.psum(right_part, ('outer', 'shard')) / replicas  519 us
    psum x2, waiting for transfers between devices, body(): left = lax.psum(left_part, 'outer') / replicas  212 us
    psum x2, blocking collectives, body(): gram = lax.psum(gram_part, 'shard')  120 us
  transfers between devices with their start and end apart: 4, of which 4 were waited for; matrix products, arithmetic and copies ran while one was open for 0% of the time, Pallas kernels for 0%

commit v1 on v0

v1 whole, which is shorter than its diff:
```python
import jax
import jax.numpy as jnp
from jax import lax
from jax.sharding import Mesh, PartitionSpec as P

ITERS = 2
REPLICAS = 16
RANK = 64
NZ, NC, NX, NY = 8, 2, 4, 4
HALF = 160
KV = 1024
SLICE = KV // NZ

momentum_decay = 0.9
outer_rate = 0.7

HI = lax.Precision.HIGHEST
SWAP = [(0, 1), (1, 0)]


def gathered(chunk, axes, n):
    return lax.all_to_all(jnp.broadcast_to(chunk[None], (n,) + chunk.shape), axes, 0, 0, tiled=True)


def reduced_right(piece, left, z, c):
    wt = lax.dot_general(left, piece, (((0,), (0,)), ((), ())), precision=HI)
    gram = lax.dot_general(left, left, (((0,), (0,)), ((), ())), precision=HI)
    rows = lax.dynamic_slice_in_dim(gram, z * 8, 8, 0).reshape(2, 4, RANK)
    rows = jnp.pad(rows, ((0, 0), (0, 4), (0, 128 - RANK)))
    pack = jnp.concatenate([wt.reshape(2, 32, 128), rows], axis=1)
    mine = lax.dynamic_index_in_dim(pack, c, 0, keepdims=False)
    other = lax.dynamic_index_in_dim(pack, 1 - c, 0, keepdims=False)
    chunk = mine + lax.ppermute(other, "c", SWAP)
    chunk = gathered(chunk, ("x", "y"), NX * NY).sum(0)
    full = gathered(chunk, ("z", "c"), NZ * NC).reshape(NZ, NC, 40, 128)
    wt = full[:, :, :32].transpose(1, 2, 0, 3).reshape(RANK, KV)
    gram = full[:, :, 32:36, :RANK].reshape(RANK, RANK)
    return wt, gram


def inverse_factor(gram):
    factor = jnp.linalg.cholesky(gram)
    return lax.linalg.triangular_solve(
        factor, jnp.eye(RANK, dtype=jnp.float32), left_side=True, lower=True
    )


def body(base, local, error, momentum, query):
    z, c = lax.axis_index("z"), lax.axis_index("c")
    field = base - local[0].astype(jnp.float32) + error[0]
    halves = field.reshape(2, HALF, KV)
    mine = lax.dynamic_index_in_dim(halves, c, 0, keepdims=False)
    other = lax.dynamic_index_in_dim(halves, 1 - c, 0, keepdims=False)
    pair = mine + lax.ppermute(other, "c", SWAP)
    left_part = jnp.dot(pair, query, precision=HI)
    left_pack = jnp.concatenate([left_part[:80], left_part[80:]], axis=1)
    send = jnp.concatenate(
        [
            pair.reshape(HALF, NZ, SLICE).transpose(1, 0, 2),
            jnp.broadcast_to(left_pack[None], (NZ, 80, 128)),
        ],
        axis=1,
    )
    got = lax.all_to_all(send, "z", 0, 0, tiled=True).sum(0) / REPLICAS
    piece = got[:HALF]
    left = jnp.concatenate([got[HALF:, :RANK], got[HALF:, RANK:]], axis=0)
    rows = lax.all_gather(piece, "z")
    wt, gram = reduced_right(piece, left, z, c)
    for step in range(1, ITERS):
        inv = inverse_factor(gram)
        rt = jnp.dot(inv, wt, precision=HI)
        left = jnp.einsum("zdk,qzk->dq", rows, rt.reshape(RANK, NZ, SLICE), precision=HI)
        wt, gram = reduced_right(piece, left, z, c)
    inv = inverse_factor(gram)
    theirs = lax.ppermute(left, "c", SWAP)
    left = jnp.where(c == 0, jnp.concatenate([left, theirs], 0), jnp.concatenate([theirs, left], 0))
    basis = lax.dot_general(left, inv, (((1,), (1,)), ((), ())), precision=HI)
    rt = jnp.dot(inv, wt, precision=HI)
    approx = jnp.dot(basis, rt, precision=HI)
    new_error = (field - approx)[None]
    new_momentum = momentum_decay * momentum + approx
    new_base = base - outer_rate * (approx + momentum_decay * new_momentum)
    return (new_base, new_error, new_momentum)


def solution(mesh):
    mesh = Mesh(mesh.devices.reshape(NZ, NC, NX, NY), ("z", "c", "x", "y"))
    outer, shard = ("z", "c"), ("x", "y")
    in_specs = (
        P(shard, None),
        P(outer, shard, None),
        P(outer, shard, None),
        P(shard, None),
        P(),
    )
    out_specs = (P(shard, None), P(outer, shard, None), P(shard, None))
    return jax.shard_map(body, mesh=mesh, in_specs=in_specs, out_specs=out_specs, check_vma=False)
```

time: 915 us -> 166 us (0.18)
  waiting for transfers between devices: 731 us -> 43.9 us
  blocking collectives: 120 us -> 51.6 us
  starting transfers between devices: 0.16 us -> 29.5 us
  between operations: 13.9 us -> 0.94 us
  matrix products: 21.6 us -> 9.05 us
    psum x4 -> x0, waiting for transfers between devices: 731 us -> none  [the longest x2 519 us: body(): right = lax.psum(right_part, ('outer', 'shard')) / replicas]
    psum x2 -> x0, blocking collectives: 120 us -> none  [body(): gram = lax.psum(gram_part, 'shard')]
    all_to_all x0 -> x3, waiting for transfers between devices: none -> 40.5 us  [the longest x1 27.8 us: body(): got = lax.all_to_all(send, 'z', 0, 0, tiled=True).sum(0) / REPLICAS]
    all_gather x0 -> x1, blocking collectives: none -> 25.9 us  [body(): rows = lax.all_gather(piece, 'z')]
    all_to_all x0 -> x2, blocking collectives: none -> 25.7 us  [gathered(): lax.all_to_all(jnp.broadcast_to(chunk[None], (n,) + chunk.shape), axes, 0...]
    all_to_all x0 -> x3, starting transfers between devices: none -> 19.2 us  [the longest x2 12.7 us: gathered(): lax.all_to_all(jnp.broadcast_to(chunk[None], (n,) + chunk.shape), axes, 0...]
    dot_general x7 -> x10, matrix products: 19.1 us -> 8.54 us  [the longest x1 4.77 us: body(): approx = jnp.dot(basis, rt, precision=HI)]
    ppermute x0 -> x4, starting transfers between devices: none -> 10.3 us  [the longest x2 6.64 us: reduced_right(): chunk = mine + lax.ppermute(other, 'c', SWAP)]
  transfers between devices with their start and end apart: 4 -> 7, of which waited for: 4 -> 5; matrix products, arithmetic and copies ran while one was open for 0% -> 8% of each run, Pallas kernels for 0% -> 0%
where the time goes in v1:
time: 166 us; the launch traced here: 165 us
  blocking collectives  51.6 us (31%)
  waiting for transfers between devices  43.9 us (26%)
  starting transfers between devices  29.5 us (18%)
  other arithmetic  26.7 us (16%)
  matrix products  9.05 us (5%)
  local copies, waits for them, and re-layouts  3.67 us (2%)
    all_to_all x1, waiting for transfers between devices, body(): got = lax.all_to_all(send, 'z', 0, 0, tiled=True).sum(0) / REPLICAS  27.8 us
    all_gather x1, blocking collectives, body(): rows = lax.all_gather(piece, 'z')  25.9 us
    all_to_all x2, blocking collectives, gathered(): lax.all_to_all(jnp.broadcast_to(chunk[None], (n,) + chunk.shape), axes, 0...  25.7 us
    another operation x6, other arithmetic, inverse_factor(): factor = jnp.linalg.cholesky(gram)  13 us
    all_to_all x2, starting transfers between devices, gathered(): lax.all_to_all(jnp.broadcast_to(chunk[None], (n,) + chunk.shape), axes, 0...  12.7 us
    all_to_all x2, waiting for transfers between devices, gathered(): lax.all_to_all(jnp.broadcast_to(chunk[None], (n,) + chunk.shape), axes, 0...  12.7 us
    another operation x4, other arithmetic, inverse_factor(): lax.linalg.triangular_solve(factor, jnp.eye(RANK, dtype=jnp.float32), lef...  11.1 us
    ppermute x2, starting transfers between devices, reduced_right(): chunk = mine + lax.ppermute(other, 'c', SWAP)  6.64 us
  transfers between devices with their start and end apart: 7, of which 5 were waited for; matrix products, arithmetic and copies ran while one was open for 8% of the time, Pallas kernels for 0%

profile of v1, /device:TPU:1, one launch (start us, length us, event | category | flops | bytes accessed | tf_op | source)
XLA Modules:
  0.0 165.3 jit_solution(9764448321600937311)
XLA Ops:
  0.7 2.2 %fusion = f32[320,1024]{1,0:T(8,128)S(1)} fusion(f32[320,1024]{1,0:T(8,128)} %param.8, f32[1,320,1024]{2,1,0:T(8,128)} %param.10, bf16[1,320,1024]{2,1,0:T(8,128)(2,1)} %param.9), kind=kLoop, calls=%fused_computation.1 | loop fusion | flops 983040 | bytes 4587520 | tf_op jit(solution)/shard_map/add | solution.py:50
  2.9 3.3 %collective-permute-start = (f32[160,1024]{1,0:T(8,128)S(1)}, f32[160,1024]{1,0:T(8,128)S(1)}, u32[]{:S(2)}, u32[]{:S(2)}) collective-permute-start(f32[160,1024]{1,0:T(8,128)S(1)} %dynamic-slice_bitcast_fusion), channel_id=1, source_target_pairs={{0,16},{16,0},{1,17},{17,1},{2,18},{18,2},{3,19},{19,3},{4,20},{20... | collective-permute-start | bytes 1966088 | tf_op jit(solution)/shard_map/ppermute | solution.py:54
  6.3 1.7 %collective-permute-done = f32[160,1024]{1,0:T(8,128)S(1)} collective-permute-done((f32[160,1024]{1,0:T(8,128)S(1)}, f32[160,1024]{1,0:T(8,128)S(1)}, u32[]{:S(2)}, u32[]{:S(2)}) %collective-permute-start) | collective-permute-done | bytes 655392 | tf_op jit(solution)/shard_map/ppermute | solution.py:54
  8.2 0.8 fusion.7
  9.3 1.1 copy.41
  10.4 6.4 %all-to-all-start = ((f32[8,240,128]{2,1,0:T(8,128)}), f32[8,240,128]{2,1,0:T(8,128)S(1)}, u32[]{:S(2)}, u32[]{:S(2)}) async-start(f32[8,240,128]{2,1,0:T(8,128)} %copy.41), calls=%async_computation | async-start | bytes 1966080 | tf_op jit(solution)/shard_map/all_to_all | solution.py:64
  16.8 27.8 %all-to-all-done = f32[8,240,128]{2,1,0:T(8,128)S(1)} async-done(((f32[8,240,128]{2,1,0:T(8,128)}), f32[8,240,128]{2,1,0:T(8,128)S(1)}, u32[]{:S(2)}, u32[]{:S(2)}) %all-to-all-start) | async-done | bytes 983072 | tf_op jit(solution)/shard_map/all_to_all | solution.py:64
  46.1 0.8 collective-permute-done.1
  47.0 14.5 %all_to_all.25 = f32[16,40,128]{2,1,0:T(8,128)S(1)} all-to-all(f32[16,40,128]{2,1,0:T(8,128)S(1)} %broadcast_in_dim.14), channel_id=1, replica_groups=mesh['z'=8,'c'=2,'x'=4,'y'=4] {'x','y'}, dimensions={0} | all-to-all | bytes 655360 | tf_op jit(solution)/shard_map/all_to_all | solution.py:22
  61.6 0.7 broadcast_in_dim.15
  62.3 5.5 %all-to-all-start.2 = ((f32[16,40,128]{2,1,0:T(8,128)}), f32[16,40,128]{2,1,0:T(8,128)S(1)}, u32[]{:S(2)}, u32[]{:S(2)}) async-start(f32[16,40,128]{2,1,0:T(8,128)} %broadcast_in_dim.15), calls=%async_computation.2 | async-start | bytes 655360 | tf_op jit(solution)/shard_map/all_to_all | solution.py:22
  67.8 25.9 %all-gather = f32[1280,128]{1,0:T(8,128)S(1)} all-gather(f32[160,128]{1,0:T(8,128)S(1)} %slice.44), channel_id=2, replica_groups=mesh['z'=8,'c'=2,'x'=4,'y'=4] {'z'}, dimensions={0}, use_global_device_ids=true | all-gather | bytes 737280 | tf_op jit(solution)/shard_map/all_gather | solution.py:67
  94.0 5.8 %cholesky.44 = f32[64,64]{1,0:T(8,128)S(1)} custom-call(f32[64,64]{1,0:T(8,128)S(1)} %fusion.26), custom_call_target="Cholesky" | custom-call | tf_op jit(solution)/shard_map/jit(cholesky)/cholesky | solution.py:42
  101.2 4.9 %custom-call.6 = f32[1,64,64]{1,2,0:T(8,128)S(1)} custom-call(f32[1,64,64]{2,1,0:T(8,128)S(1)} %fusion.21), custom_call_target="InvertDiagBlocksLowerTriangular" | custom-call | tf_op jit(solution)/shard_map/triangular_solve/custom-call.0 | solution.py:43
  106.7 0.8 convolution_bitcast_fusion
  108.0 6.1 %collective-permute-start.3 = (f32[40,128]{1,0:T(8,128)S(1)}, f32[40,128]{1,0:T(8,128)S(1)}, u32[]{:S(2)}, u32[]{:S(2)}) collective-permute-start(f32[40,128]{1,0:T(8,128)S(1)} %dynamic-slice_bitcast_fusion.1), channel_id=1, source_target_pairs={{0,16},{16,0},{1,17},{17,1},{2,18},{18,2},{3,19},{19,3},{4,20},{20... | collective-permute-start | bytes 61448 | tf_op jit(solution)/shard_map/ppermute | solution.py:33
  114.0 0.8 collective-permute-done.3
  114.9 11.2 %all_to_all.26 = f32[16,40,128]{2,1,0:T(8,128)S(1)} all-to-all(f32[16,40,128]{2,1,0:T(8,128)S(1)} %broadcast_in_dim.16), channel_id=1, replica_groups=mesh['z'=8,'c'=2,'x'=4,'y'=4] {'x','y'}, dimensions={0} | all-to-all | bytes 655360 | tf_op jit(solution)/shard_map/all_to_all | solution.py:22
  126.1 0.7 broadcast_in_dim.17
  126.9 7.3 %all-to-all-start.4 = ((f32[16,40,128]{2,1,0:T(8,128)}), f32[16,40,128]{2,1,0:T(8,128)S(1)}, u32[]{:S(2)}, u32[]{:S(2)}) async-start(f32[16,40,128]{2,1,0:T(8,128)} %broadcast_in_dim.17), calls=%async_computation.4 | async-start | bytes 655360 | tf_op jit(solution)/shard_map/all_to_all | solution.py:22
  134.5 12.7 %all-to-all-done.4 = f32[16,40,128]{2,1,0:T(8,128)S(1)} async-done(((f32[16,40,128]{2,1,0:T(8,128)}), f32[16,40,128]{2,1,0:T(8,128)S(1)}, u32[]{:S(2)}, u32[]{:S(2)}) %all-to-all-start.4) | async-done | bytes 327712 | tf_op jit(solution)/shard_map/all_to_all | solution.py:22
  147.5 5.8 %cholesky.55 = f32[64,64]{1,0:T(8,128)S(1)} custom-call(f32[64,64]{1,0:T(8,128)S(1)} %fusion.24), custom_call_target="Cholesky" | custom-call | tf_op jit(solution)/shard_map/jit(cholesky)/cholesky | solution.py:42
  154.7 4.9 %custom-call.7 = f32[1,64,64]{1,2,0:T(8,128)S(1)} custom-call(f32[1,64,64]{2,1,0:T(8,128)S(1)} %fusion.22), custom_call_target="InvertDiagBlocksLowerTriangular" | custom-call | tf_op jit(solution)/shard_map/triangular_solve/custom-call.0 | solution.py:43
  160.6 4.8 %multiply_subtract_fusion = (f32[320,1024]{1,0:T(8,128)}, f32[320,1024]{1,0:T(8,128)}, f32[1,320,1024]{2,1,0:T(8,128)}) fusion(f32[320,1024]{1,0:T(8,128)S(1)} %copy-done.1, f32[320,1024]{1,0:T(8,128)} %param.11, f32[320,1024]{1,0:T(8,128)S(1)} %fusion, f32[320,64]{0,1:T(8,128)S(1)} %fusion.9, f32[64,1024]{1,0:T(8,128)S(1)} %fusion.1), kind=kOutput, calls=%fused_computation.3 | convolution fusion | flops 253952000 | bytes 8208384 | tf_op jit(solution)/shard_map/dot_general | solution.py:79
  (57 shorter events, 7.7 us)
Async XLA Ops:
  0.6 7.6 %copy-start = (f32[1024,64]{0,1:T(8,128)S(1)}, f32[1024,64]{0,1:T(8,128)}, u32[]{:S(2)}) copy-start(f32[1024,64]{0,1:T(8,128)} %param.12) | copy-start | bytes 786436
  2.9 5.1 %collective-permute-start = (f32[160,1024]{1,0:T(8,128)S(1)}, f32[160,1024]{1,0:T(8,128)S(1)}, u32[]{:S(2)}, u32[]{:S(2)}) collective-permute-start(f32[160,1024]{1,0:T(8,128)S(1)} %dynamic-slice_bitcast_fusion), channel_id=1, source_target_pairs={{0,16},{16,0},{1,17},{17,1},{2,18},{18,2},{3,19},{19,3},{4,20},{20... | collective-permute-start | bytes 1966088 | tf_op jit(solution)/shard_map/ppermute | solution.py:54
  10.4 34.2 %all-to-all-start = ((f32[8,240,128]{2,1,0:T(8,128)}), f32[8,240,128]{2,1,0:T(8,128)S(1)}, u32[]{:S(2)}, u32[]{:S(2)}) async-start(f32[8,240,128]{2,1,0:T(8,128)} %copy.41), calls=%async_computation | async-start | bytes 1966080 | tf_op jit(solution)/shard_map/all_to_all | solution.py:64
  45.5 1.4 collective-permute-start.1
  62.3 31.4 %all-to-all-start.2 = ((f32[16,40,128]{2,1,0:T(8,128)}), f32[16,40,128]{2,1,0:T(8,128)S(1)}, u32[]{:S(2)}, u32[]{:S(2)}) async-start(f32[16,40,128]{2,1,0:T(8,128)} %broadcast_in_dim.15), calls=%async_computation.2 | async-start | bytes 655360 | tf_op jit(solution)/shard_map/all_to_all | solution.py:22
  108.0 6.9 %collective-permute-start.3 = (f32[40,128]{1,0:T(8,128)S(1)}, f32[40,128]{1,0:T(8,128)S(1)}, u32[]{:S(2)}, u32[]{:S(2)}) collective-permute-start(f32[40,128]{1,0:T(8,128)S(1)} %dynamic-slice_bitcast_fusion.1), channel_id=1, source_target_pairs={{0,16},{16,0},{1,17},{17,1},{2,18},{18,2},{3,19},{19,3},{4,20},{20... | collective-permute-start | bytes 61448 | tf_op jit(solution)/shard_map/ppermute | solution.py:33
  126.9 33.7 %copy-start.1 = (f32[320,1024]{1,0:T(8,128)S(1)}, f32[320,1024]{1,0:T(8,128)}, u32[]{:S(2)}) copy-start(f32[320,1024]{1,0:T(8,128)} %param.8) | copy-start | bytes 3932164
  126.9 20.3 %all-to-all-start.4 = ((f32[16,40,128]{2,1,0:T(8,128)}), f32[16,40,128]{2,1,0:T(8,128)S(1)}, u32[]{:S(2)}, u32[]{:S(2)}) async-start(f32[16,40,128]{2,1,0:T(8,128)} %broadcast_in_dim.17), calls=%async_computation.4 | async-start | bytes 655360 | tf_op jit(solution)/shard_map/all_to_all | solution.py:22
  134.1 26.1 %collective-permute-start.2 = (f32[160,64]{0,1:T(8,128)S(1)}, f32[160,64]{0,1:T(8,128)S(1)}, u32[]{:S(2)}, u32[]{:S(2)}) collective-permute-start(f32[160,64]{0,1:T(8,128)S(1)} %convolution_bitcast_fusion), channel_id=1, source_target_pairs={{0,16},{16,0},{1,17},{17,1},{2,18},{18,2},{3,19},{19,3},{4,20},{20... | collective-permute-start | bytes 122888 | tf_op jit(solution)/shard_map/ppermute | solution.py:75

commit v2 on v0

v2 whole, which is shorter than its diff:
```python
import functools
import jax
import jax.numpy as jnp
from jax import lax
from jax.experimental import pallas as pl
from jax.experimental.pallas import tpu as pltpu
from jax.sharding import Mesh, PartitionSpec as P

ITERS = 2
REPLICAS = 16
RANK = 64
NZ, NC, NX, NY = 8, 2, 4, 4
ROWS = 320
HALF = 160
KV = 1024
SLICE = KV // NZ
PACK = 40

momentum_decay = 0.9
outer_rate = 0.7

HI = lax.Precision.HIGHEST
SWAP = [(0, 1), (1, 0)]
F32 = jnp.float32
VMEM = pl.BlockSpec(memory_space=pltpu.VMEM)
SMEM = pl.BlockSpec(memory_space=pltpu.SMEM)
ANY = pl.BlockSpec(memory_space=pl.ANY)
PARAMS = pltpu.CompilerParams(vmem_limit_bytes=32 * 2**20)


def shape(*dims):
    return jax.ShapeDtypeStruct(dims, F32)


def dot(a, b, ca, cb):
    return lax.dot_general(a, b, (((ca,), (cb,)), ((), ())), precision=HI, preferred_element_type=F32)


def spread(x):
    return jnp.broadcast_to(x, (8, 128))


def inverse_factor(gram):
    n = RANK // 8
    eye = (
        lax.broadcasted_iota(jnp.int32, (RANK, RANK), 0)
        == lax.broadcasted_iota(jnp.int32, (RANK, RANK), 1)
    ).astype(F32)
    full = jnp.concatenate([gram, eye], axis=1)
    a = [full[8 * i : 8 * i + 8] for i in range(n)]
    sub = lax.broadcasted_iota(jnp.int32, (8, 128), 0)
    for b in range(n):
        p = a[b]
        at = 8 * b
        e = [spread(p[:, at + j : at + j + 1]) for j in range(8)]
        cols = [[spread(a[i][:, at + j : at + j + 1]) for j in range(8)] for i in range(b + 1, n)]
        for k in range(8):
            s = lax.rsqrt(spread(e[k][k : k + 1]))
            f = jnp.where(sub > k, e[k] * (s * s), 0.0)
            u = [None] * 8
            for j in range(k + 1, 8):
                row = spread(e[j][k : k + 1])
                u[j] = row * s
                e[j] = e[j] - f * row
            prow = spread(p[k : k + 1])
            p = jnp.where(sub == k, prow * s, p - f * prow)
            for ci in cols:
                ci[k] = ci[k] * s
                for j in range(k + 1, 8):
                    ci[j] = ci[j] - ci[k] * u[j]
        for i in range(b + 1, n):
            for k in range(8):
                a[i] = a[i] - cols[i - b - 1][k] * spread(p[k : k + 1])
        a[b] = p
    return jnp.concatenate(a, axis=0)[:, RANK:]


def unpack(full):
    wt = jnp.concatenate(
        [jnp.concatenate([full[z, c, :32] for c in range(NC)], axis=0) for z in range(NZ)], axis=1
    )
    gram = jnp.concatenate(
        [full[z, c, 32:36, :RANK] for z in range(NZ) for c in range(NC)], axis=0
    )
    return wt, gram


def put_message(left, piece, z, c, gram_ref, pack_ref, keep_ref, send_ref):
    wt = dot(left, piece, 0, 0)
    gram_ref[...] = jnp.zeros((RANK, 128), F32)
    gram_ref[:, :RANK] = dot(left, left, 0, 0)
    rows = gram_ref[pl.ds(pl.multiple_of(z * 8, 8), 8), :]
    pack_ref[0, :32] = wt[:32]
    pack_ref[1, :32] = wt[32:]
    pack_ref[0, 32:] = rows
    pack_ref[1, 32:] = jnp.concatenate([rows[4:], rows[:4]], axis=0)
    keep_ref[...] = pack_ref[c]
    send_ref[...] = pack_ref[1 - c]


def first_send(mine_ref, theirs_ref, query_ref, out_ref):
    pair = mine_ref[...] + theirs_ref[...]
    left = dot(pair, query_ref[...], 1, 0)
    packed = jnp.concatenate([left[: HALF // 2], left[HALF // 2 :]], axis=1)
    for z in range(NZ):
        out_ref[z, :HALF] = pair[:, z * SLICE : (z + 1) * SLICE]
        out_ref[z, HALF:] = packed


def first_left(at_ref, got_ref, piece_ref, keep_ref, send_ref, gram_ref, pack_ref):
    total = got_ref[0]
    for z in range(1, NZ):
        total = total + got_ref[z]
    total = total * (1.0 / REPLICAS)
    piece = total[:HALF]
    piece_ref[...] = piece
    left = jnp.concatenate([total[HALF:, :RANK], total[HALF:, RANK:]], axis=0)
    put_message(left, piece, at_ref[0], at_ref[1], gram_ref, pack_ref, keep_ref, send_ref)


def sum_spread(*refs):
    *ins, out_ref = refs
    parts = []
    for ref in ins:
        parts += [ref[...]] if len(ref.shape) == 2 else [ref[i] for i in range(ref.shape[0])]
    total = functools.reduce(lambda a, b: a + b, parts)
    for i in range(out_ref.shape[0]):
        out_ref[i] = total


def next_left(at_ref, full_ref, rows_ref, piece_ref, left_ref, keep_ref, send_ref, gram_ref, pack_ref):
    wt, gram = unpack(full_ref)
    rt = dot(inverse_factor(gram), wt, 1, 0)
    rows = jnp.concatenate([rows_ref[z] for z in range(NZ)], axis=1)
    left = dot(rows, rt, 1, 1)
    left_ref[...] = left
    put_message(left, piece_ref[...], at_ref[0], at_ref[1], gram_ref, pack_ref, keep_ref, send_ref)


def finish(at_ref, full_ref, mine_ref, theirs_ref, field_in, base_in, mom_in, base_out, err_out, mom_out,
           left_ref, field, base, mom, nbase, nerr, nmom, in_sem, out_sem):
    loads = [
        pltpu.make_async_copy(src, dst, in_sem.at[i])
        for i, (src, dst) in enumerate([(field_in, field), (base_in, base), (mom_in, mom)])
    ]
    for load in loads:
        load.start()
    c = at_ref[1]
    left_ref[c] = mine_ref[...]
    left_ref[1 - c] = theirs_ref[...]
    wt, gram = unpack(full_ref)
    inv = inverse_factor(gram)
    rt = dot(inv, wt, 1, 0)
    stores = []
    for load in loads:
        load.wait()
    part = HALF // 2
    for i in range(ROWS // part):
        here = pl.ds(i * part, part)
        basis = dot(left_ref[i // 2, pl.ds((i % 2) * part, part)], inv, 1, 1)
        approx = dot(basis, rt, 1, 0)
        nerr[here] = field[here] - approx
        momentum = momentum_decay * mom[here] + approx
        nmom[here] = momentum
        nbase[here] = base[here] - outer_rate * (approx + momentum_decay * momentum)
        for j, (src, dst) in enumerate([(nbase, base_out), (nerr, err_out), (nmom, mom_out)]):
            store = pltpu.make_async_copy(src.at[here], dst.at[here], out_sem.at[j, i])
            store.start()
            stores.append(store)
    for store in stores:
        store.wait()


def gathered(operand, axes):
    return lax.all_to_all(operand, axes, 0, 0, tiled=True)


def summed_right(keep, send):
    xy, zc = NX * NY, NZ * NC
    theirs = lax.ppermute(send, "c", SWAP)
    chunks = pl.pallas_call(
        sum_spread, out_shape=shape(xy, PACK, 128), in_specs=[VMEM] * 2, out_specs=VMEM
    )(keep, theirs)
    got = gathered(chunks, ("x", "y"))
    chunks = pl.pallas_call(
        sum_spread, out_shape=shape(zc, PACK, 128), in_specs=[VMEM], out_specs=VMEM
    )(got)
    return gathered(chunks, ("z", "c")).reshape(NZ, NC, PACK, 128)


def body(base, local, error, momentum, query):
    z, c = lax.axis_index("z"), lax.axis_index("c")
    at = jnp.stack([z, c]).astype(jnp.int32)
    field = base - local[0].astype(F32) + error[0]
    halves = field.reshape(2, HALF, KV)
    mine = lax.dynamic_index_in_dim(halves, c, 0, keepdims=False)
    other = lax.dynamic_index_in_dim(halves, 1 - c, 0, keepdims=False)
    theirs = lax.ppermute(other, "c", SWAP)
    send = pl.pallas_call(
        first_send,
        out_shape=shape(NZ, HALF + HALF // 2, 128),
        in_specs=[VMEM] * 3,
        out_specs=VMEM,
        compiler_params=PARAMS,
    )(mine, theirs, query)
    got = lax.all_to_all(send, "z", 0, 0, tiled=True)
    message = [shape(PACK, 128), shape(PACK, 128)]
    scratch = [pltpu.VMEM((RANK, 128), F32), pltpu.VMEM((2, PACK, 128), F32)]
    piece, keep, send = pl.pallas_call(
        first_left,
        out_shape=[shape(HALF, SLICE)] + message,
        in_specs=[SMEM, VMEM],
        out_specs=[VMEM] * 3,
        scratch_shapes=scratch,
        compiler_params=PARAMS,
    )(at, got)
    rows = gathered(jnp.broadcast_to(piece[None], (NZ, HALF, SLICE)), "z")
    full = summed_right(keep, send)
    for step in range(1, ITERS):
        left, keep, send = pl.pallas_call(
            next_left,
            out_shape=[shape(HALF, RANK)] + message,
            in_specs=[SMEM] + [VMEM] * 3,
            out_specs=[VMEM] * 3,
            scratch_shapes=scratch,
            compiler_params=PARAMS,
        )(at, full, rows, piece)
        theirs = lax.ppermute(left, "c", SWAP)
        full = summed_right(keep, send)
    big = pltpu.VMEM((ROWS, KV), F32)
    new_base, new_error, new_momentum = pl.pallas_call(
        finish,
        out_shape=[shape(ROWS, KV)] * 3,
        in_specs=[SMEM] + [VMEM] * 3 + [ANY] * 3,
        out_specs=[ANY] * 3,
        scratch_shapes=[pltpu.VMEM((2, HALF, RANK), F32)]
        + [big] * 6
        + [pltpu.SemaphoreType.DMA((3,)), pltpu.SemaphoreType.DMA((3, 4))],
        compiler_params=PARAMS,
    )(at, full, left, theirs, field, base, momentum)
    return new_base, new_error[None], new_momentum


def solution(mesh):
    mesh = Mesh(mesh.devices.reshape(NZ, NC, NX, NY), ("z", "c", "x", "y"))
    outer, shard = ("z", "c"), ("x", "y")
    in_specs = (
        P(shard, None),
        P(outer, shard, None),
        P(outer, shard, None),
        P(shard, None),
        P(),
    )
    out_specs = (P(shard, None), P(outer, shard, None), P(shard, None))
    return jax.shard_map(body, mesh=mesh, in_specs=in_specs, out_specs=out_specs, check_vma=False)
```

time: 915 us -> 157 us (0.17)
  waiting for transfers between devices: 731 us -> 43.9 us
  blocking collectives: 120 us -> 69.3 us
  other arithmetic: 26.5 us -> 2.26 us
  matrix products: 21.6 us -> 0 us
  Pallas kernels: 0 us -> 19.7 us
  starting transfers between devices: 0.16 us -> 15.8 us
  between operations: 13.9 us -> 0.7 us
    psum x4 -> x0, waiting for transfers between devices: 731 us -> none  [the longest x2 519 us: body(): right = lax.psum(right_part, ('outer', 'shard')) / replicas]
    psum x2 -> x0, blocking collectives: 120 us -> none  [body(): gram = lax.psum(gram_part, 'shard')]
    all_to_all x0 -> x4, blocking collectives: none -> 69.3 us  [gathered(): return lax.all_to_all(operand, axes, 0, 0, tiled=True)]
    all_to_all x0 -> x2, waiting for transfers between devices: none -> 39.5 us  [the longest x1 27.7 us: body(): got = lax.all_to_all(send, 'z', 0, 0, tiled=True)]
    another operation x10 -> x1, other arithmetic: 24.1 us -> 0.07 us  [body(): at = jnp.stack([z, c]).astype(jnp.int32)]
    pallas_call x0 -> x8, Pallas kernels: none -> 19.7 us  [the longest x1 6.43 us: body(): pl.pallas_call(finish, out_shape=[shape(ROWS, KV)] * 3, in_specs=[SMEM] +...]
    dot_general x7 -> x0, matrix products: 19.1 us -> none  [the longest x2 6.88 us: body(): jnp.einsum('dk,dq->kq', field, basis, precision=lax.Precision.HIGHEST)]
    all_to_all x0 -> x2, starting transfers between devices: none -> 11.3 us  [the longest x1 6.45 us: body(): got = lax.all_to_all(send, 'z', 0, 0, tiled=True)]
  transfers between devices with their start and end apart: 4 -> 6, of which waited for: 4 -> 6; matrix products, arithmetic and copies ran while one was open for 0% -> 0% of each run, Pallas kernels for 0% -> 0%
where the time goes in v2:
time: 157 us
  blocking collectives  69.3 us (44%)
  waiting for transfers between devices  43.9 us (28%)
  Pallas kernels  19.7 us (13%)
  starting transfers between devices  15.8 us (10%)
  local copies, waits for them, and re-layouts  4.95 us (3%)
  other arithmetic  2.26 us (1%)
    all_to_all x4, blocking collectives, gathered(): return lax.all_to_all(operand, axes, 0, 0, tiled=True)  69.3 us
    all_to_all x1, waiting for transfers between devices, body(): got = lax.all_to_all(send, 'z', 0, 0, tiled=True)  27.7 us
    all_to_all x1, waiting for transfers between devices, gathered(): return lax.all_to_all(operand, axes, 0, 0, tiled=True)  11.8 us
    all_to_all x1, starting transfers between devices, body(): got = lax.all_to_all(send, 'z', 0, 0, tiled=True)  6.45 us
    pallas_call x1, Pallas kernels, body(): pl.pallas_call(finish, out_shape=[shape(ROWS, KV)] * 3, in_specs=[SMEM] +...  6.43 us
    all_to_all x1, starting transfers between devices, gathered(): return lax.all_to_all(operand, axes, 0, 0, tiled=True)  4.83 us
    pallas_call x1, Pallas kernels, body(): pl.pallas_call(next_left, out_shape=[shape(HALF, RANK)] + message, in_spe...  4.14 us
    unnamed x15, local copies, waits for them, and re-layouts  3.94 us
  transfers between devices with their start and end apart: 6, of which 6 were waited for; matrix products, arithmetic and copies ran while one was open for 0% of the time, Pallas kernels for 0%

profile of v2, /device:TPU:1, one launch (start us, length us, event | category | flops | bytes accessed | tf_op | source)
XLA Modules:
  0.0 156.6 jit_solution(6696503997559394594)
XLA Ops:
  0.6 2.2 %fusion.field_in = f32[320,1024]{1,0:T(8,128)S(1)} fusion(f32[320,1024]{1,0:T(8,128)} %base_in.1, f32[1,320,1024]{2,1,0:T(8,128)} %param.7, bf16[1,320,1024]{2,1,0:T(8,128)(2,1)} %param.6), kind=kLoop, calls=%fused_computation.1 | loop fusion | flops 983040 | bytes 4587520 | tf_op jit(solution)/shard_map/add | solution.py:194
  2.8 1.0 dynamic-slice_bitcast_fusion
  3.8 3.2 %collective-permute-start = (f32[160,1024]{1,0:T(8,128)}, f32[160,1024]{1,0:T(8,128)S(1)}, u32[]{:S(2)}, u32[]{:S(2)}) collective-permute-start(f32[160,1024]{1,0:T(8,128)} %get-tuple-element.21), channel_id=1, source_target_pairs={{0,16},{16,0},{1,17},{17,1},{2,18},{18,2},{3,19},{19,3},{4,20},{20... | collective-permute-start | bytes 1966088 | tf_op jit(solution)/shard_map/ppermute | solution.py:198
  7.2 1.7 %collective-permute-done.theirs_ref = f32[160,1024]{1,0:T(8,128)S(1)} collective-permute-done((f32[160,1024]{1,0:T(8,128)}, f32[160,1024]{1,0:T(8,128)S(1)}, u32[]{:S(2)}, u32[]{:S(2)}) %collective-permute-start) | collective-permute-done | bytes 655392 | tf_op jit(solution)/shard_map/ppermute | solution.py:198
  9.0 1.8 %shard_map.76 = f32[8,240,128]{2,1,0:T(8,128)} custom-call(f32[160,1024]{1,0:T(8,128)S(1)} %get-tuple-element.22.mine_ref, f32[160,1024]{1,0:T(8,128)S(1)} %collective-permute-done.theirs_ref, f32[1024,64]{1,0:T(8,128)S(1)} %copy.8.query_ref), custom_call_target="tpu_custom_call" | custom-call | tf_op jit(solution)/shard_map/pallas_call | solution.py:199
  10.7 6.4 %all-to-all-start = ((f32[8,240,128]{2,1,0:T(8,128)}), f32[8,240,128]{2,1,0:T(8,128)S(1)}, u32[]{:S(2)}, u32[]{:S(2)}) async-start(f32[8,240,128]{2,1,0:T(8,128)} %shard_map.76), calls=%async_computation | async-start | bytes 1966080 | tf_op jit(solution)/shard_map/all_to_all | solution.py:206
  17.3 27.7 %all-to-all-done.got_ref = f32[8,240,128]{2,1,0:T(8,128)S(1)} async-done(((f32[8,240,128]{2,1,0:T(8,128)}), f32[8,240,128]{2,1,0:T(8,128)S(1)}, u32[]{:S(2)}, u32[]{:S(2)}) %all-to-all-start) | async-done | bytes 983072 | tf_op jit(solution)/shard_map/all_to_all | solution.py:206
  45.0 1.0 shard_map.77
  47.1 0.8 collective-permute-done.1.refs_1_
  48.5 1.5 shard_map.78
  50.0 14.8 %all_to_all.30.refs_0_ = f32[16,40,128]{2,1,0:T(8,128)} all-to-all(f32[16,40,128]{2,1,0:T(8,128)} %shard_map.78), channel_id=1, replica_groups=mesh['z'=8,'c'=2,'x'=4,'y'=4] {'x','y'}, dimensions={0} | all-to-all | bytes 655360 | tf_op jit(solution)/shard_map/all_to_all | solution.py:175
  64.8 1.7 %shard_map.79 = f32[16,40,128]{2,1,0:T(8,128)} custom-call(f32[16,40,128]{2,1,0:T(8,128)} %all_to_all.30.refs_0_), custom_call_target="tpu_custom_call" | custom-call | tf_op jit(solution)/shard_map/pallas_call | solution.py:185
  66.6 18.5 %all_to_all.31 = f32[16,40,128]{2,1,0:T(8,128)S(1)} all-to-all(f32[16,40,128]{2,1,0:T(8,128)} %shard_map.79), channel_id=1, replica_groups=mesh['z'=8,'c'=2,'x'=4,'y'=4] {'z','c'}, dimensions={0} | all-to-all | bytes 655360 | tf_op jit(solution)/shard_map/all_to_all | solution.py:175
  85.1 23.2 %all_to_all.32.rows_ref = f32[8,160,128]{2,1,0:T(8,128)S(1)} all-to-all(f32[8,160,128]{2,1,0:T(8,128)S(1)} %broadcast_in_dim.4), channel_id=1, replica_groups=mesh['z'=8,'c'=2,'x'=4,'y'=4] {'z'}, dimensions={0} | all-to-all | bytes 1310720 | tf_op jit(solution)/shard_map/all_to_all | solution.py:175
  108.3 4.1 %shard_map.80 = (f32[160,64]{1,0:T(8,128)S(1)}, f32[40,128]{1,0:T(8,128)S(1)}, f32[40,128]{1,0:T(8,128)S(1)}) custom-call(s32[2]{0:T(128)S(1)} %pad_add_fusion.at_ref, f32[8,2,40,128]{3,2,1,0:T(8,128)S(1)} %bitcast.17, f32[8,160,128]{2,1,0:T(8,128)S(1)} %all_to_all.32.rows_ref, f32[160,128]{1,0:T(8,128)S(1)} %get-tuple-element.14.piece_ref), custom_call_target="tpu_custom_call" | custom-call | tf_op jit(solution)/shard_map/pallas_call | solution.py:220
  113.5 0.8 collective-permute-done.2.refs_1_
  115.0 1.5 shard_map.81
  116.5 12.8 %all_to_all.33.refs_0_ = f32[16,40,128]{2,1,0:T(8,128)} all-to-all(f32[16,40,128]{2,1,0:T(8,128)} %shard_map.81), channel_id=1, replica_groups=mesh['z'=8,'c'=2,'x'=4,'y'=4] {'x','y'}, dimensions={0} | all-to-all | bytes 655360 | tf_op jit(solution)/shard_map/all_to_all | solution.py:175
  129.3 1.7 %shard_map.82 = f32[16,40,128]{2,1,0:T(8,128)} custom-call(f32[16,40,128]{2,1,0:T(8,128)} %all_to_all.33.refs_0_), custom_call_target="tpu_custom_call" | custom-call | tf_op jit(solution)/shard_map/pallas_call | solution.py:185
  131.0 4.8 %all-to-all-start.5 = ((f32[16,40,128]{2,1,0:T(8,128)}), f32[16,40,128]{2,1,0:T(8,128)S(1)}, u32[]{:S(2)}, u32[]{:S(2)}) async-start(f32[16,40,128]{2,1,0:T(8,128)} %shard_map.82), calls=%async_computation.5 | async-start | bytes 655360 | tf_op jit(solution)/shard_map/all_to_all | solution.py:175
  136.1 1.0 collective-permute-done.3.theirs_ref
  137.1 11.8 %all-to-all-done.5 = f32[16,40,128]{2,1,0:T(8,128)S(1)} async-done(((f32[16,40,128]{2,1,0:T(8,128)}), f32[16,40,128]{2,1,0:T(8,128)S(1)}, u32[]{:S(2)}, u32[]{:S(2)}) %all-to-all-start.5) | async-done | bytes 327712 | tf_op jit(solution)/shard_map/all_to_all | solution.py:175
  148.9 1.3 copy-done.1
  150.2 6.4 %shard_map.83 = (f32[320,1024]{1,0:T(8,128)}, f32[320,1024]{1,0:T(8,128)}, f32[320,1024]{1,0:T(8,128)}) custom-call(s32[2]{0:T(128)S(1)} %pad_add_fusion.at_ref, f32[8,2,40,128]{3,2,1,0:T(8,128)S(1)} %bitcast.16, f32[160,64]{1,0:T(8,128)S(1)} %get-tuple-element.17.mine_ref, f32[160,64]{1,0:T(8,128)S(1)} %collective-permute-done.3.theirs_ref, ...), custom_call_target="tpu_custom_call" | custom-call | tf_op jit(solution)/shard_map/pallas_call | solution.py:231
  (19 shorter events, 4.0 us)
Async XLA Ops:
  2.8 4.2 %copy-start.4 = (f32[1024,64]{0,1:T(8,128)S(1)}, f32[1024,64]{0,1:T(8,128)}, u32[]{:S(2)}) copy-start(f32[1024,64]{0,1:T(8,128)} %param.9) | copy-start | bytes 786436
  3.8 5.2 %collective-permute-start = (f32[160,1024]{1,0:T(8,128)}, f32[160,1024]{1,0:T(8,128)S(1)}, u32[]{:S(2)}, u32[]{:S(2)}) collective-permute-start(f32[160,1024]{1,0:T(8,128)} %get-tuple-element.21), channel_id=1, source_target_pairs={{0,16},{16,0},{1,17},{17,1},{2,18},{18,2},{3,19},{19,3},{4,20},{20... | collective-permute-start | bytes 1966088 | tf_op jit(solution)/shard_map/ppermute | solution.py:198
  10.7 34.2 %all-to-all-start = ((f32[8,240,128]{2,1,0:T(8,128)}), f32[8,240,128]{2,1,0:T(8,128)S(1)}, u32[]{:S(2)}, u32[]{:S(2)}) async-start(f32[8,240,128]{2,1,0:T(8,128)} %shard_map.76), calls=%async_computation | async-start | bytes 1966080 | tf_op jit(solution)/shard_map/all_to_all | solution.py:206
  45.9 0.6 copy-start.3
  46.6 1.3 collective-permute-start.1
  47.9 0.6 copy-start.5
  112.4 0.6 copy-start.2
  113.0 35.8 %copy-start = (f32[320,1024]{1,0:T(8,128)S(1)}, f32[320,1024]{1,0:T(8,128)}, u32[]{:S(2)}) copy-start(f32[320,1024]{1,0:T(8,128)} %base_in.1) | copy-start | bytes 3932164
  113.0 1.3 collective-permute-start.2
  114.4 0.6 copy-start.6
  131.0 17.9 %all-to-all-start.5 = ((f32[16,40,128]{2,1,0:T(8,128)}), f32[16,40,128]{2,1,0:T(8,128)S(1)}, u32[]{:S(2)}, u32[]{:S(2)}) async-start(f32[16,40,128]{2,1,0:T(8,128)} %shard_map.82), calls=%async_computation.5 | async-start | bytes 655360 | tf_op jit(solution)/shard_map/all_to_all | solution.py:175
  135.8 1.3 collective-permute-start.3
  148.9 1.3 copy-start.1

commit v3 on v2

v3 whole, which is shorter than its diff:
```python
import functools
import jax
import jax.numpy as jnp
from jax import lax
from jax.experimental import pallas as pl
from jax.experimental.pallas import tpu as pltpu
from jax.sharding import Mesh, PartitionSpec as P

ITERS = 2
REPLICAS = 16
RANK = 64
NZ, NC, NX, NY = 8, 2, 4, 4
XY, ZC = NX * NY, NZ * NC
ROWS = 320
HALF = ROWS // 2
KV = 1024
SLICE = KV // NZ
PART = RANK // NC
LEFT = ROWS * PART // 128
GRAM = PART * RANK // 128
PACK = PART + GRAM

momentum_decay = 0.9
outer_rate = 0.7

HI = lax.Precision.HIGHEST
SWAP = [(0, 1), (1, 0)]
F32 = jnp.float32
VMEM = pl.BlockSpec(memory_space=pltpu.VMEM)
SMEM = pl.BlockSpec(memory_space=pltpu.SMEM)
ANY = pl.BlockSpec(memory_space=pl.ANY)


def shape(*dims):
    return jax.ShapeDtypeStruct(dims, F32)


def call(kernel, outs, ins, scratch=(), mib=8, flops=10**6):
    return pl.pallas_call(
        kernel,
        out_shape=outs,
        in_specs=ins,
        out_specs=jax.tree.map(lambda _: VMEM, outs),
        scratch_shapes=list(scratch),
        compiler_params=pltpu.CompilerParams(vmem_limit_bytes=mib * 2**20),
        cost_estimate=pl.CostEstimate(flops=flops, bytes_accessed=2**20, transcendentals=0),
    )


def dot(a, b, ca, cb):
    return lax.dot_general(a, b, (((ca,), (cb,)), ((), ())), precision=HI, preferred_element_type=F32)


def add_up(ref):
    return functools.reduce(lambda a, b: a + b, [ref[i] for i in range(ref.shape[0])])


def spread(x):
    return jnp.broadcast_to(x, (8, 128))


def inverse_factor(gram):
    n = RANK // 8
    eye = (
        lax.broadcasted_iota(jnp.int32, (RANK, RANK), 0)
        == lax.broadcasted_iota(jnp.int32, (RANK, RANK), 1)
    ).astype(F32)
    full = jnp.concatenate([gram, eye], axis=1)
    a = [full[8 * i : 8 * i + 8] for i in range(n)]
    sub = lax.broadcasted_iota(jnp.int32, (8, 128), 0)
    for b in range(n):
        p = a[b]
        at = 8 * b
        e = [spread(p[:, at + j : at + j + 1]) for j in range(8)]
        cols = [[spread(a[i][:, at + j : at + j + 1]) for j in range(8)] for i in range(b + 1, n)]
        for k in range(8):
            s = lax.rsqrt(spread(e[k][k : k + 1]))
            f = jnp.where(sub > k, e[k] * (s * s), 0.0)
            u = [None] * 8
            for j in range(k + 1, 8):
                row = spread(e[j][k : k + 1])
                u[j] = row * s
                e[j] = e[j] - f * row
            prow = spread(p[k : k + 1])
            p = jnp.where(sub == k, prow * s, p - f * prow)
            for ci in cols:
                ci[k] = ci[k] * s
                for j in range(k + 1, 8):
                    ci[j] = ci[j] - ci[k] * u[j]
        for i in range(b + 1, n):
            for k in range(8):
                a[i] = a[i] - cols[i - b - 1][k] * spread(p[k : k + 1])
        a[b] = p
    return jnp.concatenate(a, axis=0)[:, RANK:]


def in_order(c, mine, theirs):
    first = c == 0
    return jnp.where(first, mine, theirs), jnp.where(first, theirs, mine)


def gram_of(c, mine, theirs):
    halves = in_order(c, mine, theirs)
    return jnp.concatenate([p for h in halves for p in (h[:, :RANK], h[:, RANK:])], axis=0)


def put_message(c, left_ref, piece, out_ref):
    own = left_ref[pl.ds(pl.multiple_of(c * PART, PART), PART)]
    wt = dot(own, piece, 1, 0)
    gram = dot(own, left_ref[...], 1, 1)
    gram = jnp.concatenate([gram[:GRAM], gram[GRAM:]], axis=1)
    for i in range(XY):
        out_ref[i, :PART] = wt
        out_ref[i, PART:] = gram


def first_send(at_ref, field_ref, theirs_ref, query_ref, out_ref):
    mine = field_ref[pl.ds(pl.multiple_of(at_ref[0] * HALF, HALF), HALF)]
    pair = mine + theirs_ref[...]
    left = dot(pair, query_ref[...], 1, 0)
    packed = jnp.concatenate([left[: HALF // 2], left[HALF // 2 :]], axis=1)
    for z in range(NZ):
        out_ref[z, :HALF] = pair[:, z * SLICE : (z + 1) * SLICE]
        out_ref[z, HALF:] = packed


def mean_over_z(got_ref, out_ref):
    out_ref[...] = add_up(got_ref) * (1.0 / REPLICAS)


def first_message(at_ref, mine_ref, theirs_ref, out_ref, piece_ref, left_ref):
    c = at_ref[0]
    halves = in_order(c, mine_ref[...], theirs_ref[...])
    piece = jnp.concatenate([h[:HALF] for h in halves], axis=0)
    left = jnp.concatenate([p for h in halves for p in (h[HALF:, :RANK], h[HALF:, RANK:])], axis=0)
    piece_ref[...] = piece
    left_ref[...] = left.T
    put_message(c, left_ref, piece, out_ref)


def left_parts(got_ref, piece_ref, out_ref, gram_ref):
    total = add_up(got_ref)
    gram_ref[...] = total[PART:]
    left = dot(piece_ref[...], total[:PART], 1, 1)
    packed = jnp.concatenate([left[i * LEFT : (i + 1) * LEFT] for i in range(128 // PART)], axis=1)
    for z in range(NZ):
        out_ref[z] = packed


def factor(at_ref, mine_ref, theirs_ref, out_ref):
    out_ref[...] = inverse_factor(gram_of(at_ref[0], mine_ref[...], theirs_ref[...]))


def total_of(got_ref, out_ref):
    out_ref[...] = add_up(got_ref)


def next_message(at_ref, mine_ref, theirs_ref, inv_ref, piece_ref, out_ref, left_ref):
    c = at_ref[0]
    first, second = in_order(c, mine_ref[...], theirs_ref[...])
    left = jnp.concatenate(
        [
            jnp.concatenate([h[:, i * PART : (i + 1) * PART] for h in (first, second)], axis=1)
            for i in range(128 // PART)
        ],
        axis=0,
    )
    left_ref[...] = dot(inv_ref[...], left, 1, 1)
    put_message(c, left_ref, piece_ref[...], out_ref)


def right_parts(got_ref, out_ref, gram_ref):
    total = add_up(got_ref)
    gram_ref[...] = total[PART:]
    for i in range(ZC):
        out_ref[i] = total[:PART]


def coefficients(at_ref, mine_ref, theirs_ref, left_ref, out_ref):
    inv = inverse_factor(gram_of(at_ref[0], mine_ref[...], theirs_ref[...]))
    basis = dot(inv, left_ref[...], 1, 0)
    out_ref[...] = dot(basis, inv, 0, 0)


def finish(full_ref, coef_ref, field_in, base_in, mom_in, base_out, err_out, mom_out,
           field, base, mom, nbase, nerr, nmom, in_sem, out_sem):
    loads = [
        pltpu.make_async_copy(src, dst, in_sem.at[i])
        for i, (src, dst) in enumerate([(field_in, field), (base_in, base), (mom_in, mom)])
    ]
    for load in loads:
        load.start()
    wt = jnp.concatenate(
        [jnp.concatenate([full_ref[z * NC + c] for c in range(NC)], axis=0) for z in range(NZ)], axis=1
    )
    for load in loads:
        load.wait()
    stores = []
    part = HALF // 2
    for i in range(ROWS // part):
        here = pl.ds(i * part, part)
        approx = dot(coef_ref[here], wt, 1, 0)
        nerr[here] = field[here] - approx
        momentum = momentum_decay * mom[here] + approx
        nmom[here] = momentum
        nbase[here] = base[here] - outer_rate * (approx + momentum_decay * momentum)
        for j, (src, dst) in enumerate([(nbase, base_out), (nerr, err_out), (nmom, mom_out)]):
            store = pltpu.make_async_copy(src.at[here], dst.at[here], out_sem.at[j, i])
            store.start()
            stores.append(store)
    for store in stores:
        store.wait()


def exchange(operand, axes):
    return lax.all_to_all(operand, axes, 0, 0, tiled=True)


def swap(x):
    return lax.ppermute(x, "c", SWAP)


def body(base, local, error, momentum, query):
    c = lax.axis_index("c")
    at = c.astype(jnp.int32)[None]
    there = (1 - c) * HALF
    rows = lambda x: lax.dynamic_slice_in_dim(x, there, HALF, 0)
    theirs = swap(rows(base) - rows(local[0]).astype(F32) + rows(error[0]))
    field = base - local[0].astype(F32) + error[0]
    send = call(first_send, shape(NZ, HALF + HALF // 2, 128), [SMEM] + [VMEM] * 3)(
        at, field, theirs, query
    )
    mean = call(mean_over_z, shape(HALF + HALF // 2, 128), [VMEM])(exchange(send, "z"))
    send, piece, left = call(
        first_message, [shape(XY, PACK, 128), shape(ROWS, SLICE), shape(RANK, ROWS)], [SMEM] + [VMEM] * 2
    )(at, mean, swap(mean))
    for step in range(1, ITERS):
        send, gram = call(left_parts, [shape(NZ, LEFT, 128), shape(GRAM, 128)], [VMEM] * 2)(
            exchange(send, ("x", "y")), piece
        )
        got = exchange(send, "z")
        inv = call(factor, shape(RANK, RANK), [SMEM] + [VMEM] * 2, flops=10**9)(at, gram, swap(gram))
        part = call(total_of, shape(LEFT, 128), [VMEM])(got)
        send, left = call(
            next_message, [shape(XY, PACK, 128), shape(RANK, ROWS)], [SMEM] + [VMEM] * 4
        )(at, part, swap(part), inv, piece)
    send, gram = call(right_parts, [shape(ZC, PART, 128), shape(GRAM, 128)], [VMEM])(
        exchange(send, ("x", "y"))
    )
    full = exchange(send, ("z", "c"))
    coef = call(coefficients, shape(ROWS, RANK), [SMEM] + [VMEM] * 3, flops=10**9)(
        at, gram, swap(gram), left
    )
    big = pltpu.VMEM((ROWS, KV), F32)
    new_base, new_error, new_momentum = pl.pallas_call(
        finish,
        out_shape=[shape(ROWS, KV)] * 3,
        in_specs=[VMEM] * 2 + [ANY] * 3,
        out_specs=[ANY] * 3,
        scratch_shapes=[big] * 6
        + [pltpu.SemaphoreType.DMA((3,)), pltpu.SemaphoreType.DMA((3, 4))],
        compiler_params=pltpu.CompilerParams(vmem_limit_bytes=16 * 2**20),
    )(full, coef, field, base, momentum)
    return new_base, new_error[None], new_momentum


def solution(mesh):
    mesh = Mesh(mesh.devices.reshape(NZ, NC, NX, NY), ("z", "c", "x", "y"))
    outer, shard = ("z", "c"), ("x", "y")
    in_specs = (
        P(shard, None),
        P(outer, shard, None),
        P(outer, shard, None),
        P(shard, None),
        P(),
    )
    out_specs = (P(shard, None), P(outer, shard, None), P(shard, None))
    return jax.shard_map(body, mesh=mesh, in_specs=in_specs, out_specs=out_specs, check_vma=False)
```

time: 157 us -> 119 us (0.76)
  waiting for transfers between devices: 43.9 us -> 19.3 us
  blocking collectives: 69.3 us -> 60.9 us
  Pallas kernels: 19.7 us -> 13.2 us
  local copies, waits for them, and re-layouts: 4.95 us -> 1.52 us
  starting transfers between devices: 15.8 us -> 18.7 us
  other arithmetic: 2.26 us -> 4.26 us
    all_to_all x2, waiting for transfers between devices: 39.5 us -> 17.4 us  [exchange(): return lax.all_to_all(operand, axes, 0, 0, tiled=True)]
    all_to_all x4 -> x3, blocking collectives: 69.3 us -> 60.9 us  [exchange(): return lax.all_to_all(operand, axes, 0, 0, tiled=True)]
    pallas_call x8 -> x10, Pallas kernels: 19.7 us -> 13.2 us  [the longest x1 2.75 us: body(): pl.pallas_call(finish, out_shape=[shape(ROWS, KV)] * 3, in_specs=[VMEM] *...]
    ppermute x4 -> x5, starting transfers between devices: 4.52 us -> 10.2 us  [swap(): return lax.ppermute(x, 'c', SWAP)]
    all_to_all x2, starting transfers between devices: 11.3 us -> 8.42 us  [exchange(): return lax.all_to_all(operand, axes, 0, 0, tiled=True)]
    ppermute x4 -> x5, waiting for transfers between devices: 4.39 us -> 1.9 us  [swap(): return lax.ppermute(x, 'c', SWAP)]
    add x0 -> x1, other arithmetic: none -> 2.47 us  [body(): theirs = swap(rows(base) - rows(local[0]).astype(F32) + rows(error[0]))]
    unnamed x15 -> x7, local copies, waits for them, and re-layouts: 3.94 us -> 1.52 us
  transfers between devices with their start and end apart: 6 -> 7, of which waited for: 6 -> 5; matrix products, arithmetic and copies ran while one was open for 0% -> 2% of each run, Pallas kernels for 0% -> 4%
where the time goes in v3:
time: 119 us; the launch traced here: 118 us
  blocking collectives  60.9 us (51%)
  waiting for transfers between devices  19.3 us (16%)
  starting transfers between devices  18.7 us (16%)
  Pallas kernels  13.2 us (11%)
  other arithmetic  4.26 us (4%)
  local copies, waits for them, and re-layouts  1.52 us (1%)
    all_to_all x3, blocking collectives, exchange(): return lax.all_to_all(operand, axes, 0, 0, tiled=True)  60.9 us
    all_to_all x2, waiting for transfers between devices, exchange(): return lax.all_to_all(operand, axes, 0, 0, tiled=True)  17.4 us
    ppermute x5, starting transfers between devices, swap(): return lax.ppermute(x, 'c', SWAP)  10.2 us
    all_to_all x2, starting transfers between devices, exchange(): return lax.all_to_all(operand, axes, 0, 0, tiled=True)  8.42 us
    pallas_call x1, Pallas kernels, body(): pl.pallas_call(finish, out_shape=[shape(ROWS, KV)] * 3, in_specs=[VMEM] *...  2.75 us
    pallas_call x1, Pallas kernels, body(): call(coefficients, shape(ROWS, RANK), [SMEM] + [VMEM] * 3, flops=10 ** 9)  2.74 us
    add x1, other arithmetic, body(): theirs = swap(rows(base) - rows(local[0]).astype(F32) + rows(error[0]))  2.47 us
  transfers between devices with their start and end apart: 7, of which 5 were waited for; matrix products, arithmetic and copies ran while one was open for 2% of the time, Pallas kernels for 4%

profile of v3, /device:TPU:1, one launch (start us, length us, event | category | flops | bytes accessed | tf_op | source)
XLA Modules:
  0.0 118.5 jit_solution(17818893806796450112)
XLA Ops:
  0.7 2.5 %fusion.1 = f32[160,1024]{1,0:T(8,128)} fusion(f32[1,320,1024]{2,1,0:T(8,128)} %param.7, s32[]{:T(128)S(6)} %select_n.2, f32[320,1024]{1,0:T(8,128)} %base_in.1, bf16[1,320,1024]{2,1,0:T(8,128)(2,1)} %param.6), kind=kLoop, calls=%fused_computation.3 | loop fusion | flops 491520 | bytes 2293764 | tf_op jit(solution)/shard_map/add | solution.py:228
  3.1 3.2 %collective-permute-start = (f32[160,1024]{1,0:T(8,128)}, f32[160,1024]{1,0:T(8,128)}, u32[]{:S(2)}, u32[]{:S(2)}) collective-permute-start(f32[160,1024]{1,0:T(8,128)} %fusion.1), channel_id=1, source_target_pairs={{0,16},{16,0},{1,17},{17,1},{2,18},{18,2},{3,19},{19,3},{4,20},{20... | collective-permute-start | bytes 1966088 | tf_op jit(solution)/shard_map/ppermute | solution.py:220
  6.6 1.8 %fusion.field_ref.field_in = f32[320,1024]{1,0:T(8,128)S(1)} fusion(f32[320,1024]{1,0:T(8,128)S(1)} %copy-done, f32[1,320,1024]{2,1,0:T(8,128)} %param.7, bf16[1,320,1024]{2,1,0:T(8,128)(2,1)} %param.6), kind=kLoop, calls=%fused_computation.1 | loop fusion | flops 983040 | bytes 4587520 | tf_op jit(solution)/shard_map/add | solution.py:229
  8.4 1.9 %shard_map.76 = f32[8,240,128]{2,1,0:T(8,128)S(1)} custom-call(s32[1]{0:T(128)} %bitcast.at_ref, f32[320,1024]{1,0:T(8,128)S(1)} %fusion.field_ref.field_in, f32[160,1024]{1,0:T(8,128)} %collective-permute-done.theirs_ref, f32[1024,64]{1,0:T(8,128)S(1)} %copy.8.query_ref), custom_call_target="tpu_custom_call" | custom-call | flops 1000000 | bytes 1048576 | tf_op jit(solution)/shard_map/pallas_call | solution.py:230
  10.3 32.7 %all_to_all.25.got_ref = f32[8,240,128]{2,1,0:T(8,128)S(1)} all-to-all(f32[8,240,128]{2,1,0:T(8,128)S(1)} %shard_map.76), channel_id=1, replica_groups=mesh['z'=8,'c'=2,'x'=4,'y'=4] {'z'}, dimensions={0} | all-to-all | bytes 1966080 | tf_op jit(solution)/shard_map/all_to_all | solution.py:216
  43.1 1.9 %collective-permute-start.1 = (f32[240,128]{1,0:T(8,128)S(1)}, f32[240,128]{1,0:T(8,128)S(1)}, u32[]{:S(2)}, u32[]{:S(2)}) collective-permute-start(f32[240,128]{1,0:T(8,128)S(1)} %shard_map.77.mine_ref), channel_id=1, source_target_pairs={{0,16},{16,0},{1,17},{17,1},{2,18},{18,2},{3,19},{19,3},{4,20},{20... | collective-permute-start | bytes 368648 | tf_op jit(solution)/shard_map/ppermute | solution.py:220
  45.0 1.0 collective-permute-done.1.theirs_ref
  46.0 0.9 shard_map.78
  46.9 15.8 %all_to_all.26.got_ref = f32[16,48,128]{2,1,0:T(8,128)S(1)} all-to-all(f32[16,48,128]{2,1,0:T(8,128)S(1)} %get-tuple-element.14), channel_id=1, replica_groups=mesh['z'=8,'c'=2,'x'=4,'y'=4] {'x','y'}, dimensions={0} | all-to-all | bytes 786432 | tf_op jit(solution)/shard_map/all_to_all | solution.py:216
  62.6 1.1 shard_map.79
  63.7 3.4 %all-to-all-start.2 = ((f32[8,80,128]{2,1,0:T(8,128)}), f32[8,80,128]{2,1,0:T(8,128)S(1)}, u32[]{:S(2)}, u32[]{:S(2)}) async-start(f32[8,80,128]{2,1,0:T(8,128)} %get-tuple-element.16), calls=%async_computation.2 | async-start | bytes 655360 | tf_op jit(solution)/shard_map/all_to_all | solution.py:216
  67.2 1.6 %collective-permute-start.3 = (f32[16,128]{1,0:T(8,128)S(1)}, f32[16,128]{1,0:T(8,128)S(1)}, u32[]{:S(2)}, u32[]{:S(2)}) collective-permute-start(f32[16,128]{1,0:T(8,128)S(1)} %get-tuple-element.17.mine_ref), channel_id=1, source_target_pairs={{0,16},{16,0},{1,17},{17,1},{2,18},{18,2},{3,19},{19,3},{4,20},{20... | collective-permute-start | bytes 24584 | tf_op jit(solution)/shard_map/ppermute | solution.py:220
  68.8 9.4 %all-to-all-done.2.got_ref = f32[8,80,128]{2,1,0:T(8,128)S(1)} async-done(((f32[8,80,128]{2,1,0:T(8,128)}), f32[8,80,128]{2,1,0:T(8,128)S(1)}, u32[]{:S(2)}, u32[]{:S(2)}) %all-to-all-start.2) | async-done | bytes 327712 | tf_op jit(solution)/shard_map/all_to_all | solution.py:216
  78.2 3.2 %collective-permute-start.2 = (f32[80,128]{1,0:T(8,128)S(1)}, f32[80,128]{1,0:T(8,128)S(1)}, u32[]{:S(2)}, u32[]{:S(2)}) collective-permute-start(f32[80,128]{1,0:T(8,128)S(1)} %shard_map.80.mine_ref), channel_id=1, source_target_pairs={{0,16},{16,0},{1,17},{17,1},{2,18},{18,2},{3,19},{19,3},{4,20},{20... | collective-permute-start | bytes 122888 | tf_op jit(solution)/shard_map/ppermute | solution.py:220
  81.4 2.1 %shard_map.81.inv_ref = f32[64,64]{1,0:T(8,128)S(1)} custom-call(s32[1]{0:T(128)} %bitcast.at_ref, f32[16,128]{1,0:T(8,128)S(1)} %get-tuple-element.17.mine_ref, f32[16,128]{1,0:T(8,128)S(1)} %collective-permute-done.3.theirs_ref), custom_call_target="tpu_custom_call" | custom-call | flops 1000000000 | bytes 1048576 | tf_op jit(solution)/shard_map/pallas_call | solution.py:242
  83.6 0.9 shard_map.82
  84.5 12.4 %all_to_all.27.got_ref = f32[16,48,128]{2,1,0:T(8,128)S(1)} all-to-all(f32[16,48,128]{2,1,0:T(8,128)S(1)} %get-tuple-element.18), channel_id=1, replica_groups=mesh['z'=8,'c'=2,'x'=4,'y'=4] {'x','y'}, dimensions={0} | all-to-all | bytes 786432 | tf_op jit(solution)/shard_map/all_to_all | solution.py:216
  96.8 0.7 shard_map.83
  97.6 5.0 %all-to-all-start.4 = ((f32[16,32,128]{2,1,0:T(8,128)}), f32[16,32,128]{2,1,0:T(8,128)S(1)}, u32[]{:S(2)}, u32[]{:S(2)}) async-start(f32[16,32,128]{2,1,0:T(8,128)} %get-tuple-element.19), calls=%async_computation.4 | async-start | bytes 524288 | tf_op jit(solution)/shard_map/all_to_all | solution.py:216
  102.9 0.9 collective-permute-done.4.theirs_ref
  103.7 2.7 %shard_map.84.coef_ref = f32[320,64]{1,0:T(8,128)S(1)} custom-call(s32[1]{0:T(128)} %bitcast.at_ref, f32[16,128]{1,0:T(8,128)S(1)} %get-tuple-element.20.mine_ref, f32[16,128]{1,0:T(8,128)S(1)} %collective-permute-done.4.theirs_ref, f32[64,320]{1,0:T(8,128)S(1)} %get-tuple-element.21.left_ref), custom_call_target="tpu_custom_call" | custom-call | flops 1000000000 | bytes 1048576 | tf_op jit(solution)/shard_map/pallas_call | solution.py:251
  106.5 7.9 %all-to-all-done.4.full_ref = f32[16,32,128]{2,1,0:T(8,128)S(1)} async-done(((f32[16,32,128]{2,1,0:T(8,128)}), f32[16,32,128]{2,1,0:T(8,128)S(1)}, u32[]{:S(2)}, u32[]{:S(2)}) %all-to-all-start.4) | async-done | bytes 262176 | tf_op jit(solution)/shard_map/all_to_all | solution.py:216
  114.4 1.3 %copy-done.1 = f32[320,1024]{1,0:T(8,128)S(1)} copy-done((f32[320,1024]{1,0:T(8,128)S(1)}, f32[320,1024]{1,0:T(8,128)}, u32[]{:S(2)}) %copy-start.1) | copy-done | bytes 1310744
  115.7 2.7 %shard_map.85 = (f32[320,1024]{1,0:T(8,128)}, f32[320,1024]{1,0:T(8,128)}, f32[320,1024]{1,0:T(8,128)}) custom-call(f32[16,32,128]{2,1,0:T(8,128)S(1)} %all-to-all-done.4.full_ref, f32[320,64]{1,0:T(8,128)S(1)} %shard_map.84.coef_ref, f32[320,1024]{1,0:T(8,128)S(1)} %fusion.field_ref.field_in, f32[320,1024]{1,0:T(8,128)S(1)} %copy-done, ...), custom_call_target="tpu_custom_call" | custom-call | tf_op jit(solution)/shard_map/pallas_call | solution.py:255
  (12 shorter events, 0.6 us)
Async XLA Ops:
  0.6 5.7 %copy-start.2 = (f32[1024,64]{0,1:T(8,128)S(1)}, f32[1024,64]{0,1:T(8,128)}, u32[]{:S(2)}) copy-start(f32[1024,64]{0,1:T(8,128)} %param.9) | copy-start | bytes 786436
  0.6 5.9 %copy-start = (f32[320,1024]{1,0:T(8,128)S(1)}, f32[320,1024]{1,0:T(8,128)}, u32[]{:S(2)}) copy-start(f32[320,1024]{1,0:T(8,128)} %base_in.1) | copy-start | bytes 3932164
  3.1 5.3 %collective-permute-start = (f32[160,1024]{1,0:T(8,128)}, f32[160,1024]{1,0:T(8,128)}, u32[]{:S(2)}, u32[]{:S(2)}) collective-permute-start(f32[160,1024]{1,0:T(8,128)} %fusion.1), channel_id=1, source_target_pairs={{0,16},{16,0},{1,17},{17,1},{2,18},{18,2},{3,19},{19,3},{4,20},{20... | collective-permute-start | bytes 1966088 | tf_op jit(solution)/shard_map/ppermute | solution.py:220
  43.1 2.9 %collective-permute-start.1 = (f32[240,128]{1,0:T(8,128)S(1)}, f32[240,128]{1,0:T(8,128)S(1)}, u32[]{:S(2)}, u32[]{:S(2)}) collective-permute-start(f32[240,128]{1,0:T(8,128)S(1)} %shard_map.77.mine_ref), channel_id=1, source_target_pairs={{0,16},{16,0},{1,17},{17,1},{2,18},{18,2},{3,19},{19,3},{4,20},{20... | collective-permute-start | bytes 368648 | tf_op jit(solution)/shard_map/ppermute | solution.py:220
  63.7 14.5 %all-to-all-start.2 = ((f32[8,80,128]{2,1,0:T(8,128)}), f32[8,80,128]{2,1,0:T(8,128)S(1)}, u32[]{:S(2)}, u32[]{:S(2)}) async-start(f32[8,80,128]{2,1,0:T(8,128)} %get-tuple-element.16), calls=%async_computation.2 | async-start | bytes 655360 | tf_op jit(solution)/shard_map/all_to_all | solution.py:216
  67.2 14.3 %collective-permute-start.3 = (f32[16,128]{1,0:T(8,128)S(1)}, f32[16,128]{1,0:T(8,128)S(1)}, u32[]{:S(2)}, u32[]{:S(2)}) collective-permute-start(f32[16,128]{1,0:T(8,128)S(1)} %get-tuple-element.17.mine_ref), channel_id=1, source_target_pairs={{0,16},{16,0},{1,17},{17,1},{2,18},{18,2},{3,19},{19,3},{4,20},{20... | collective-permute-start | bytes 24584 | tf_op jit(solution)/shard_map/ppermute | solution.py:220
  78.2 5.3 %collective-permute-start.2 = (f32[80,128]{1,0:T(8,128)S(1)}, f32[80,128]{1,0:T(8,128)S(1)}, u32[]{:S(2)}, u32[]{:S(2)}) collective-permute-start(f32[80,128]{1,0:T(8,128)S(1)} %shard_map.80.mine_ref), channel_id=1, source_target_pairs={{0,16},{16,0},{1,17},{17,1},{2,18},{18,2},{3,19},{19,3},{4,20},{20... | collective-permute-start | bytes 122888 | tf_op jit(solution)/shard_map/ppermute | solution.py:220
  97.6 16.9 %all-to-all-start.4 = ((f32[16,32,128]{2,1,0:T(8,128)}), f32[16,32,128]{2,1,0:T(8,128)S(1)}, u32[]{:S(2)}, u32[]{:S(2)}) async-start(f32[16,32,128]{2,1,0:T(8,128)} %get-tuple-element.19), calls=%async_computation.4 | async-start | bytes 524288 | tf_op jit(solution)/shard_map/all_to_all | solution.py:216
  102.6 1.2 collective-permute-start.4
  114.4 1.3 %copy-start.1 = (f32[320,1024]{1,0:T(8,128)S(1)}, f32[320,1024]{1,0:T(8,128)}, u32[]{:S(2)}) copy-start(f32[320,1024]{1,0:T(8,128)} %mom_in.1) | copy-start | bytes 3932164

commit v4 on v3

--- a/solution.py
+++ b/solution.py
@@ -28,7 +28,7 @@
 F32 = jnp.float32
 VMEM = pl.BlockSpec(memory_space=pltpu.VMEM)
 SMEM = pl.BlockSpec(memory_space=pltpu.SMEM)
-ANY = pl.BlockSpec(memory_space=pl.ANY)
+HBM = pl.BlockSpec(memory_space=pltpu.HBM)
 
 
 def shape(*dims):
@@ -114,10 +114,34 @@
         out_ref[i, PART:] = gram
 
 
-def first_send(at_ref, field_ref, theirs_ref, query_ref, out_ref):
-    mine = field_ref[pl.ds(pl.multiple_of(at_ref[0] * HALF, HALF), HALF)]
-    pair = mine + theirs_ref[...]
-    left = dot(pair, query_ref[...], 1, 0)
+def half_field(there, base_in, local_in, error_in, base, local, error, sem, out_ref):
+    part = HALF // 2
+    loads = []
+    for i in range(2):
+        here = pl.ds(i * part, part)
+        rows = pl.ds(pl.multiple_of(there + i * part, part), part)
+        for j, (src, dst) in enumerate([(base_in, base), (local_in.at[0], local), (error_in.at[0], error)]):
+            load = pltpu.make_async_copy(src.at[rows], dst.at[here], sem.at[i, j])
+            load.start()
+            loads.append(load)
+    for i in range(2):
+        here = pl.ds(i * part, part)
+        for load in loads[3 * i : 3 * i + 3]:
+            load.wait()
+        out_ref[here] = base[here] - local[here].astype(F32) + error[here]
+
+
+def other_half(at_ref, base_in, local_in, error_in, out_ref, base, local, error, sem):
+    half_field((1 - at_ref[0]) * HALF, base_in, local_in, error_in, base, local, error, sem, out_ref)
+
+
+def own_half(at_ref, base_in, local_in, error_in, out_ref, base, local, error, sem):
+    half_field(at_ref[0] * HALF, base_in, local_in, error_in, base, local, error, sem, out_ref)
+
+
+def first_send(mine_ref, theirs_ref, query_ref, out_ref):
+    pair = mine_ref[...] + theirs_ref[...]
+    left = dot(pair, query_ref[...], 1, 1)
     packed = jnp.concatenate([left[: HALF // 2], left[HALF // 2 :]], axis=1)
     for z in range(NZ):
         out_ref[z, :HALF] = pair[:, z * SLICE : (z + 1) * SLICE]
@@ -151,7 +175,7 @@
     out_ref[...] = inverse_factor(gram_of(at_ref[0], mine_ref[...], theirs_ref[...]))
 
 
-def total_of(got_ref, out_ref):
+def total_of(got_ref, inv_ref, out_ref):
     out_ref[...] = add_up(got_ref)
 
 
@@ -176,25 +200,28 @@
         out_ref[i] = total[:PART]
 
 
-def coefficients(at_ref, mine_ref, theirs_ref, left_ref, out_ref):
-    inv = inverse_factor(gram_of(at_ref[0], mine_ref[...], theirs_ref[...]))
-    basis = dot(inv, left_ref[...], 1, 0)
-    out_ref[...] = dot(basis, inv, 0, 0)
-
-
-def finish(full_ref, coef_ref, field_in, base_in, mom_in, base_out, err_out, mom_out,
-           field, base, mom, nbase, nerr, nmom, in_sem, out_sem):
+def coefficients(at_ref, mine_ref, theirs_ref, left_ref, own_ref, other_ref, base_in, mom_in,
+                 coef_ref, field_ref, base_ref, mom_ref, sem):
     loads = [
-        pltpu.make_async_copy(src, dst, in_sem.at[i])
-        for i, (src, dst) in enumerate([(field_in, field), (base_in, base), (mom_in, mom)])
+        pltpu.make_async_copy(src, dst, sem.at[i])
+        for i, (src, dst) in enumerate([(base_in, base_ref), (mom_in, mom_ref)])
     ]
     for load in loads:
         load.start()
+    c = at_ref[0]
+    inv = inverse_factor(gram_of(c, mine_ref[...], theirs_ref[...]))
+    basis = dot(inv, left_ref[...], 1, 0)
+    coef_ref[...] = dot(basis, inv, 0, 0)
+    field_ref[pl.ds(pl.multiple_of(c * HALF, HALF), HALF)] = own_ref[...]
+    field_ref[pl.ds(pl.multiple_of((1 - c) * HALF, HALF), HALF)] = other_ref[...]
+    for load in loads:
+        load.wait()
+
+
+def finish(full_ref, coef_ref, field, base, mom, base_out, err_out, mom_out, nbase, nerr, nmom, out_sem):
     wt = jnp.concatenate(
         [jnp.concatenate([full_ref[z * NC + c] for c in range(NC)], axis=0) for z in range(NZ)], axis=1
     )
-    for load in loads:
-        load.wait()
     stores = []
     part = HALF // 2
     for i in range(ROWS // part):
@@ -223,13 +250,15 @@
 def body(base, local, error, momentum, query):
     c = lax.axis_index("c")
     at = c.astype(jnp.int32)[None]
-    there = (1 - c) * HALF
-    rows = lambda x: lax.dynamic_slice_in_dim(x, there, HALF, 0)
-    theirs = swap(rows(base) - rows(local[0]).astype(F32) + rows(error[0]))
-    field = base - local[0].astype(F32) + error[0]
-    send = call(first_send, shape(NZ, HALF + HALF // 2, 128), [SMEM] + [VMEM] * 3)(
-        at, field, theirs, query
-    )
+    buffers = [pltpu.VMEM((HALF, KV), t) for t in (F32, jnp.bfloat16, F32)]
+    buffers.append(pltpu.SemaphoreType.DMA((2, 3)))
+    half = lambda kernel: call(kernel, shape(HALF, KV), [SMEM] + [HBM] * 3, buffers, mib=60)(
+        at, base, local, error
+    )
+    other = half(other_half)
+    theirs = swap(other)
+    own = half(own_half)
+    send = call(first_send, shape(NZ, HALF + HALF // 2, 128), [VMEM] * 3)(own, theirs, query.T)
     mean = call(mean_over_z, shape(HALF + HALF // 2, 128), [VMEM])(exchange(send, "z"))
     send, piece, left = call(
         first_message, [shape(XY, PACK, 128), shape(ROWS, SLICE), shape(RANK, ROWS)], [SMEM] + [VMEM] * 2
@@ -240,7 +269,7 @@
         )
         got = exchange(send, "z")
         inv = call(factor, shape(RANK, RANK), [SMEM] + [VMEM] * 2, flops=10**9)(at, gram, swap(gram))
-        part = call(total_of, shape(LEFT, 128), [VMEM])(got)
+        part = call(total_of, shape(LEFT, 128), [VMEM, HBM])(got, inv)
         send, left = call(
             next_message, [shape(XY, PACK, 128), shape(RANK, ROWS)], [SMEM] + [VMEM] * 4
         )(at, part, swap(part), inv, piece)
@@ -248,19 +277,23 @@
         exchange(send, ("x", "y"))
     )
     full = exchange(send, ("z", "c"))
-    coef = call(coefficients, shape(ROWS, RANK), [SMEM] + [VMEM] * 3, flops=10**9)(
-        at, gram, swap(gram), left
-    )
-    big = pltpu.VMEM((ROWS, KV), F32)
+    whole = shape(ROWS, KV)
+    coef, field, old_base, old_momentum = call(
+        coefficients,
+        [shape(ROWS, RANK)] + [whole] * 3,
+        [SMEM] + [VMEM] * 5 + [HBM] * 2,
+        [pltpu.SemaphoreType.DMA((2,))],
+        mib=16,
+        flops=10**9,
+    )(at, gram, swap(gram), left, own, other, base, momentum)
     new_base, new_error, new_momentum = pl.pallas_call(
         finish,
-        out_shape=[shape(ROWS, KV)] * 3,
-        in_specs=[VMEM] * 2 + [ANY] * 3,
-        out_specs=[ANY] * 3,
-        scratch_shapes=[big] * 6
-        + [pltpu.SemaphoreType.DMA((3,)), pltpu.SemaphoreType.DMA((3, 4))],
+        out_shape=[whole] * 3,
+        in_specs=[VMEM] * 5,
+        out_specs=[HBM] * 3,
+        scratch_shapes=[pltpu.VMEM((ROWS, KV), F32)] * 3 + [pltpu.SemaphoreType.DMA((3, 4))],
         compiler_params=pltpu.CompilerParams(vmem_limit_bytes=16 * 2**20),
-    )(full, coef, field, base, momentum)
+    )(full, coef, field, old_base, old_momentum)
     return new_base, new_error[None], new_momentum
 
 

time: 119 us -> 120 us (level)
  local copies, waits for them, and re-layouts: 1.52 us -> 9.52 us
  waiting for transfers between devices: 19.3 us -> 13.2 us
  other arithmetic: 4.26 us -> 0 us
  Pallas kernels: 13.2 us -> 16.6 us
  blocking collectives: 60.9 us -> 62.4 us
  starting transfers between devices: 18.7 us -> 17.3 us
    unnamed x7 -> x24, local copies, waits for them, and re-layouts: 1.52 us -> 9.52 us
    all_to_all x2, waiting for transfers between devices: 17.4 us -> 9.67 us  [exchange(): return lax.all_to_all(operand, axes, 0, 0, tiled=True)]
    add x2 -> x0, other arithmetic: 4.26 us -> none  [the longest x1 2.47 us: body(): theirs = swap(rows(base) - rows(local[0]).astype(F32) + rows(error[0]))]
    pallas_call x4 -> x6, Pallas kernels: 7.4 us -> 10.8 us  [the longest x2 4.65 us: body(): call(kernel, shape(HALF, KV), [SMEM] + [HBM] * 3, buffers, mib=60)]
    ppermute x5, waiting for transfers between devices: 1.9 us -> 3.54 us  [swap(): return lax.ppermute(x, 'c', SWAP)]
    all_to_all x3, blocking collectives: 60.9 us -> 62.4 us  [exchange(): return lax.all_to_all(operand, axes, 0, 0, tiled=True)]
    ppermute x5, starting transfers between devices: 10.2 us -> 9 us  [swap(): return lax.ppermute(x, 'c', SWAP)]
  transfers between devices with their start and end apart: 7 -> 7, of which waited for: 5 -> 6; matrix products, arithmetic and copies ran while one was open for 2% -> 0% of each run, Pallas kernels for 4% -> 6%
where the time goes in v4:
time: 120 us
  blocking collectives  62.4 us (52%)
  starting transfers between devices  17.3 us (14%)
  Pallas kernels  16.6 us (14%)
  waiting for transfers between devices  13.2 us (11%)
  local copies, waits for them, and re-layouts  9.52 us (8%)
    all_to_all x3, blocking collectives, exchange(): return lax.all_to_all(operand, axes, 0, 0, tiled=True)  62.4 us
    all_to_all x2, waiting for transfers between devices, exchange(): return lax.all_to_all(operand, axes, 0, 0, tiled=True)  9.67 us
    unnamed x24, local copies, waits for them, and re-layouts  9.52 us
    ppermute x5, starting transfers between devices, swap(): return lax.ppermute(x, 'c', SWAP)  9 us
    all_to_all x2, starting transfers between devices, exchange(): return lax.all_to_all(operand, axes, 0, 0, tiled=True)  8.27 us
    pallas_call x2, Pallas kernels, body(): call(kernel, shape(HALF, KV), [SMEM] + [HBM] * 3, buffers, mib=60)  4.65 us
    ppermute x5, waiting for transfers between devices, swap(): return lax.ppermute(x, 'c', SWAP)  3.54 us
    pallas_call x1, Pallas kernels, body(): call(coefficients, [shape(ROWS, RANK)] + [whole] * 3, [SMEM] + [VMEM] * 5...  2.96 us
  transfers between devices with their start and end apart: 7, of which 6 were waited for; matrix products, arithmetic and copies ran while one was open for 0% of the time, Pallas kernels for 6%

profile of v4, /device:TPU:1, one launch (start us, length us, event | category | flops | bytes accessed | tf_op | source)
XLA Modules:
  0.0 119.7 jit_solution(8233029984307561679)
XLA Ops:
  0.6 2.3 %shard_map.77.other_ref = f32[160,1024]{1,0:T(8,128)} custom-call(s32[1]{0:T(128)} %bitcast.at_ref, f32[320,1024]{1,0:T(8,128)} %base_in.5, bf16[1,320,1024]{2,1,0:T(8,128)(2,1)} %local_in.3, f32[1,320,1024]{2,1,0:T(8,128)} %error_in.3), custom_call_target="tpu_custom_call" | custom-call | flops 1000000 | bytes 1048576 | tf_op jit(solution)/shard_map/pallas_call | solution.py:255
  3.0 3.3 %collective-permute-start = (f32[160,1024]{1,0:T(8,128)}, f32[160,1024]{1,0:T(8,128)S(1)}, u32[]{:S(2)}, u32[]{:S(2)}) collective-permute-start(f32[160,1024]{1,0:T(8,128)} %shard_map.77.other_ref), channel_id=1, source_target_pairs={{0,16},{16,0},{1,17},{17,1},{2,18},{18,2},{3,19},{19,3},{4,20},{20... | collective-permute-start | bytes 1966088 | tf_op jit(solution)/shard_map/ppermute | solution.py:247
  6.3 2.3 %shard_map.76.mine_ref.own_ref = f32[160,1024]{1,0:T(8,128)} custom-call(s32[1]{0:T(128)} %bitcast.at_ref, f32[320,1024]{1,0:T(8,128)} %base_in.5, bf16[1,320,1024]{2,1,0:T(8,128)(2,1)} %local_in.3, f32[1,320,1024]{2,1,0:T(8,128)} %error_in.3), custom_call_target="tpu_custom_call" | custom-call | flops 1000000 | bytes 1048576 | tf_op jit(solution)/shard_map/pallas_call | solution.py:255
  8.7 1.1 copy-done.1
  10.5 34.1 %all_to_all.25.got_ref = f32[8,240,128]{2,1,0:T(8,128)S(1)} all-to-all(f32[8,240,128]{2,1,0:T(8,128)S(1)} %shard_map.78), channel_id=1, replica_groups=mesh['z'=8,'c'=2,'x'=4,'y'=4] {'z'}, dimensions={0} | all-to-all | bytes 1966080 | tf_op jit(solution)/shard_map/all_to_all | solution.py:243
  47.0 15.8 %all_to_all.26.got_ref = f32[16,48,128]{2,1,0:T(8,128)S(1)} all-to-all(f32[16,48,128]{2,1,0:T(8,128)S(1)} %get-tuple-element.18), channel_id=1, replica_groups=mesh['z'=8,'c'=2,'x'=4,'y'=4] {'x','y'}, dimensions={0} | all-to-all | bytes 786432 | tf_op jit(solution)/shard_map/all_to_all | solution.py:243
  62.8 1.1 shard_map.81
  63.9 3.4 %all-to-all-start.2 = ((f32[8,80,128]{2,1,0:T(8,128)}), f32[8,80,128]{2,1,0:T(8,128)S(1)}, u32[]{:S(2)}, u32[]{:S(2)}) async-start(f32[8,80,128]{2,1,0:T(8,128)} %get-tuple-element.20), calls=%async_computation.2 | async-start | bytes 655360 | tf_op jit(solution)/shard_map/all_to_all | solution.py:243
  67.4 1.6 %collective-permute-start.2 = (f32[16,128]{1,0:T(8,128)S(1)}, f32[16,128]{1,0:T(8,128)S(1)}, u32[]{:S(2)}, u32[]{:S(2)}) collective-permute-start(f32[16,128]{1,0:T(8,128)S(1)} %get-tuple-element.21.mine_ref), channel_id=1, source_target_pairs={{0,16},{16,0},{1,17},{17,1},{2,18},{18,2},{3,19},{19,3},{4,20},{20... | collective-permute-start | bytes 24584 | tf_op jit(solution)/shard_map/ppermute | solution.py:247
  69.8 2.1 %shard_map.82.inv_ref = f32[64,64]{1,0:T(8,128)S(1)} custom-call(s32[1]{0:T(128)} %bitcast.at_ref, f32[16,128]{1,0:T(8,128)S(1)} %get-tuple-element.21.mine_ref, f32[16,128]{1,0:T(8,128)S(1)} %collective-permute-done.2.theirs_ref), custom_call_target="tpu_custom_call" | custom-call | flops 1000000000 | bytes 1048576 | tf_op jit(solution)/shard_map/pallas_call | solution.py:271
  72.0 6.5 %all-to-all-done.2.got_ref = f32[8,80,128]{2,1,0:T(8,128)S(1)} async-done(((f32[8,80,128]{2,1,0:T(8,128)}), f32[8,80,128]{2,1,0:T(8,128)S(1)}, u32[]{:S(2)}, u32[]{:S(2)}) %all-to-all-start.2) | async-done | bytes 327712 | tf_op jit(solution)/shard_map/all_to_all | solution.py:243
  78.4 3.2 %collective-permute-start.3 = (f32[80,128]{1,0:T(8,128)S(1)}, f32[80,128]{1,0:T(8,128)S(1)}, u32[]{:S(2)}, u32[]{:S(2)}) collective-permute-start(f32[80,128]{1,0:T(8,128)S(1)} %shard_map.83.mine_ref), channel_id=1, source_target_pairs={{0,16},{16,0},{1,17},{17,1},{2,18},{18,2},{3,19},{19,3},{4,20},{20... | collective-permute-start | bytes 122888 | tf_op jit(solution)/shard_map/ppermute | solution.py:247
  83.4 12.5 %all_to_all.27.got_ref = f32[16,48,128]{2,1,0:T(8,128)S(1)} all-to-all(f32[16,48,128]{2,1,0:T(8,128)S(1)} %get-tuple-element.22), channel_id=1, replica_groups=mesh['z'=8,'c'=2,'x'=4,'y'=4] {'x','y'}, dimensions={0} | all-to-all | bytes 786432 | tf_op jit(solution)/shard_map/all_to_all | solution.py:243
  96.6 4.8 %all-to-all-start.4 = ((f32[16,32,128]{2,1,0:T(8,128)}), f32[16,32,128]{2,1,0:T(8,128)S(1)}, u32[]{:S(2)}, u32[]{:S(2)}) async-start(f32[16,32,128]{2,1,0:T(8,128)} %get-tuple-element.23), calls=%async_computation.4 | async-start | bytes 524288 | tf_op jit(solution)/shard_map/all_to_all | solution.py:243
  102.6 1.3 %copy-done.4 = f32[320,1024]{1,0:T(8,128)S(1)} copy-done((f32[320,1024]{1,0:T(8,128)S(1)}, f32[320,1024]{1,0:T(8,128)}, u32[]{:S(2)}) %copy-start.4) | copy-done | bytes 1310744
  104.0 3.0 %shard_map.86 = (f32[320,64]{1,0:T(8,128)S(1)}, f32[320,1024]{1,0:T(8,128)S(1)}, f32[320,1024]{1,0:T(8,128)S(1)}, f32[320,1024]{1,0:T(8,128)S(1)}) custom-call(s32[1]{0:T(128)} %bitcast.at_ref, f32[16,128]{1,0:T(8,128)S(1)} %get-tuple-element.24.mine_ref, f32[16,128]{1,0:T(8,128)S(1)} %collective-permute-done.4.theirs_ref, ...), custom_call_target="tpu_custom_call" | custom-call | flops 1000000000 | bytes 1048576 | tf_op jit(solution)/shard_map/pallas_call | solution.py:281
  106.9 1.0 copy-done.5
  108.0 1.1 copy-done.7
  109.0 1.1 copy-done.9
  110.1 3.2 %all-to-all-done.4.full_ref = f32[16,32,128]{2,1,0:T(8,128)S(1)} async-done(((f32[16,32,128]{2,1,0:T(8,128)}), f32[16,32,128]{2,1,0:T(8,128)S(1)}, u32[]{:S(2)}, u32[]{:S(2)}) %all-to-all-start.4) | async-done | bytes 262176 | tf_op jit(solution)/shard_map/all_to_all | solution.py:243
  113.3 1.3 %copy-done.6 = f32[320,1024]{1,0:T(8,128)S(1)} copy-done((f32[320,1024]{1,0:T(8,128)S(1)}, f32[320,1024]{1,0:T(8,128)}, u32[]{:S(2)}) %copy-start.6) | copy-done | bytes 1310744
  114.6 1.3 %copy-done.8 = f32[320,1024]{1,0:T(8,128)S(1)} copy-done((f32[320,1024]{1,0:T(8,128)S(1)}, f32[320,1024]{1,0:T(8,128)}, u32[]{:S(2)}) %copy-start.8) | copy-done | bytes 1310744
  115.9 1.3 %copy-done.10 = f32[320,1024]{1,0:T(8,128)S(1)} copy-done((f32[320,1024]{1,0:T(8,128)S(1)}, f32[320,1024]{1,0:T(8,128)}, u32[]{:S(2)}) %copy-start.10) | copy-done | bytes 1310744
  117.3 2.5 %shard_map.87 = (f32[320,1024]{1,0:T(8,128)}, f32[320,1024]{1,0:T(8,128)}, f32[320,1024]{1,0:T(8,128)}) custom-call(f32[16,32,128]{2,1,0:T(8,128)S(1)} %all-to-all-done.4.full_ref, f32[320,64]{1,0:T(8,128)S(1)} %get-tuple-element.26.coef_ref, f32[320,1024]{1,0:T(8,128)S(1)} %copy-done.6, f32[320,1024]{1,0:T(8,128)S(1)} %copy-done.8, f32[320,1024]{1,0:T(8,128)S(1)} %copy-done.10), custom_call_target="tpu_custom_call" | custom-call | tf_op jit(solution)/shard_map/pallas_call | solution.py:289
  (29 shorter events, 7.7 us)
Async XLA Ops:
  3.0 5.7 %copy-start.11 = (f32[1024,64]{0,1:T(8,128)S(1)}, f32[1024,64]{0,1:T(8,128)}, u32[]{:S(2)}) copy-start(f32[1024,64]{0,1:T(8,128)} %param.9) | copy-start | bytes 786436
  3.0 5.7 %collective-permute-start = (f32[160,1024]{1,0:T(8,128)}, f32[160,1024]{1,0:T(8,128)S(1)}, u32[]{:S(2)}, u32[]{:S(2)}) collective-permute-start(f32[160,1024]{1,0:T(8,128)} %shard_map.77.other_ref), channel_id=1, source_target_pairs={{0,16},{16,0},{1,17},{17,1},{2,18},{18,2},{3,19},{19,3},{4,20},{20... | collective-permute-start | bytes 1966088 | tf_op jit(solution)/shard_map/ppermute | solution.py:247
  8.7 1.1 copy-start.1
  44.6 1.5 %collective-permute-start.1 = (f32[240,128]{1,0:T(8,128)S(1)}, f32[240,128]{1,0:T(8,128)S(1)}, u32[]{:S(2)}, u32[]{:S(2)}) collective-permute-start(f32[240,128]{1,0:T(8,128)S(1)} %shard_map.79.mine_ref), channel_id=1, source_target_pairs={{0,16},{16,0},{1,17},{17,1},{2,18},{18,2},{3,19},{19,3},{4,20},{20... | collective-permute-start | bytes 368648 | tf_op jit(solution)/shard_map/ppermute | solution.py:247
  63.9 14.5 %all-to-all-start.2 = ((f32[8,80,128]{2,1,0:T(8,128)}), f32[8,80,128]{2,1,0:T(8,128)S(1)}, u32[]{:S(2)}, u32[]{:S(2)}) async-start(f32[8,80,128]{2,1,0:T(8,128)} %get-tuple-element.20), calls=%async_computation.2 | async-start | bytes 655360 | tf_op jit(solution)/shard_map/all_to_all | solution.py:243
  67.4 2.4 %collective-permute-start.2 = (f32[16,128]{1,0:T(8,128)S(1)}, f32[16,128]{1,0:T(8,128)S(1)}, u32[]{:S(2)}, u32[]{:S(2)}) collective-permute-start(f32[16,128]{1,0:T(8,128)S(1)} %get-tuple-element.21.mine_ref), channel_id=1, source_target_pairs={{0,16},{16,0},{1,17},{17,1},{2,18},{18,2},{3,19},{19,3},{4,20},{20... | collective-permute-start | bytes 24584 | tf_op jit(solution)/shard_map/ppermute | solution.py:247
  69.8 32.8 %copy-start.3 = (f32[160,1024]{1,0:T(8,128)S(1)}, f32[160,1024]{1,0:T(8,128)}, u32[]{:S(2)}) copy-start(f32[160,1024]{1,0:T(8,128)} %shard_map.77.other_ref) | copy-start | bytes 1966084
  72.0 30.7 %copy-start = (f32[320,1024]{1,0:T(8,128)S(1)}, f32[320,1024]{1,0:T(8,128)}, u32[]{:S(2)}) copy-start(f32[320,1024]{1,0:T(8,128)} %base_in.5) | copy-start | bytes 3932164
  72.0 30.7 %copy-start.2 = (f32[160,1024]{1,0:T(8,128)S(1)}, f32[160,1024]{1,0:T(8,128)}, u32[]{:S(2)}) copy-start(f32[160,1024]{1,0:T(8,128)} %shard_map.76.mine_ref.own_ref) | copy-start | bytes 1966084
  78.4 4.1 %collective-permute-start.3 = (f32[80,128]{1,0:T(8,128)S(1)}, f32[80,128]{1,0:T(8,128)S(1)}, u32[]{:S(2)}, u32[]{:S(2)}) collective-permute-start(f32[80,128]{1,0:T(8,128)S(1)} %shard_map.83.mine_ref), channel_id=1, source_target_pairs={{0,16},{16,0},{1,17},{17,1},{2,18},{18,2},{3,19},{19,3},{4,20},{20... | collective-permute-start | bytes 122888 | tf_op jit(solution)/shard_map/ppermute | solution.py:247
  96.6 16.7 %all-to-all-start.4 = ((f32[16,32,128]{2,1,0:T(8,128)}), f32[16,32,128]{2,1,0:T(8,128)S(1)}, u32[]{:S(2)}, u32[]{:S(2)}) async-start(f32[16,32,128]{2,1,0:T(8,128)} %get-tuple-element.23), calls=%async_computation.4 | async-start | bytes 524288 | tf_op jit(solution)/shard_map/all_to_all | solution.py:243
  101.5 1.2 collective-permute-start.4
  102.6 1.3 %copy-start.4 = (f32[320,1024]{1,0:T(8,128)S(1)}, f32[320,1024]{1,0:T(8,128)}, u32[]{:S(2)}) copy-start(f32[320,1024]{1,0:T(8,128)} %mom_in.1) | copy-start | bytes 3932164
  106.9 1.1 copy-start.5
  108.0 1.1 copy-start.7
  109.0 1.1 copy-start.9
  113.3 1.3 %copy-start.6 = (f32[320,1024]{1,0:T(8,128)S(1)}, f32[320,1024]{1,0:T(8,128)}, u32[]{:S(2)}) copy-start(f32[320,1024]{1,0:T(8,128)} %copy-done.5) | copy-start | bytes 3932164
  114.6 1.3 %copy-start.8 = (f32[320,1024]{1,0:T(8,128)S(1)}, f32[320,1024]{1,0:T(8,128)}, u32[]{:S(2)}) copy-start(f32[320,1024]{1,0:T(8,128)} %copy-done.7) | copy-start | bytes 3932164
  115.9 1.3 %copy-start.10 = (f32[320,1024]{1,0:T(8,128)S(1)}, f32[320,1024]{1,0:T(8,128)}, u32[]{:S(2)}) copy-start(f32[320,1024]{1,0:T(8,128)} %copy-done.9) | copy-start | bytes 3932164

commit v5 on v4

--- a/solution.py
+++ b/solution.py
@@ -243,6 +243,14 @@
     return lax.all_to_all(operand, axes, 0, 0, tiled=True)
 
 
+def in_hbm(x):
+    return pltpu.with_memory_space_constraint(x, pltpu.HBM)
+
+
+def in_vmem(x):
+    return pltpu.with_memory_space_constraint(x, pltpu.VMEM)
+
+
 def swap(x):
     return lax.ppermute(x, "c", SWAP)
 
@@ -252,8 +260,8 @@
     at = c.astype(jnp.int32)[None]
     buffers = [pltpu.VMEM((HALF, KV), t) for t in (F32, jnp.bfloat16, F32)]
     buffers.append(pltpu.SemaphoreType.DMA((2, 3)))
-    half = lambda kernel: call(kernel, shape(HALF, KV), [SMEM] + [HBM] * 3, buffers, mib=60)(
-        at, base, local, error
+    half = lambda kernel: call(kernel, shape(HALF, KV), [SMEM] + [HBM] * 3, buffers)(
+        at, in_hbm(base), in_hbm(local), in_hbm(error)
     )
     other = half(other_half)
     theirs = swap(other)
@@ -285,7 +293,7 @@
         [pltpu.SemaphoreType.DMA((2,))],
         mib=16,
         flops=10**9,
-    )(at, gram, swap(gram), left, own, other, base, momentum)
+    )(at, gram, swap(gram), left, own, other, in_hbm(base), in_hbm(momentum))
     new_base, new_error, new_momentum = pl.pallas_call(
         finish,
         out_shape=[whole] * 3,
@@ -293,7 +301,7 @@
         out_specs=[HBM] * 3,
         scratch_shapes=[pltpu.VMEM((ROWS, KV), F32)] * 3 + [pltpu.SemaphoreType.DMA((3, 4))],
         compiler_params=pltpu.CompilerParams(vmem_limit_bytes=16 * 2**20),
-    )(full, coef, field, old_base, old_momentum)
+    )(full, coef, in_vmem(field), in_vmem(old_base), in_vmem(old_momentum))
     return new_base, new_error[None], new_momentum
 
 

time: 120 us -> 116 us (0.967)
  local copies, waits for them, and re-layouts: 9.52 us -> 4.74 us
  waiting for transfers between devices: 13.2 us -> 15.3 us
  blocking collectives: 62.4 us -> 61 us
  starting transfers between devices: 17.3 us -> 18.6 us
    unnamed x24 -> x10, local copies, waits for them, and re-layouts: 9.52 us -> 4.74 us
    all_to_all x2, waiting for transfers between devices: 9.67 us -> 11.5 us  [exchange(): return lax.all_to_all(operand, axes, 0, 0, tiled=True)]
    pallas_call x2, Pallas kernels: 4.65 us -> 2.98 us  [body(): call(kernel, shape(HALF, KV), [SMEM] + [HBM] * 3, buffers)]
    ppermute x5, starting transfers between devices: 9 us -> 10.3 us  [swap(): return lax.ppermute(x, 'c', SWAP)]
    all_to_all x3, blocking collectives: 62.4 us -> 61 us  [exchange(): return lax.all_to_all(operand, axes, 0, 0, tiled=True)]
  transfers between devices with their start and end apart: 7 -> 7, of which waited for: 6 -> 7; matrix products, arithmetic and copies ran while one was open for 0% -> 0% of each run, Pallas kernels for 6% -> 6%
where the time goes in v5:
time: 116 us
  blocking collectives  61 us (53%)
  starting transfers between devices  18.6 us (16%)
  Pallas kernels  15.5 us (13%)
  waiting for transfers between devices  15.3 us (13%)
  local copies, waits for them, and re-layouts  4.74 us (4%)
    all_to_all x3, blocking collectives, exchange(): return lax.all_to_all(operand, axes, 0, 0, tiled=True)  61 us
    all_to_all x2, waiting for transfers between devices, exchange(): return lax.all_to_all(operand, axes, 0, 0, tiled=True)  11.5 us
    ppermute x5, starting transfers between devices, swap(): return lax.ppermute(x, 'c', SWAP)  10.3 us
    all_to_all x2, starting transfers between devices, exchange(): return lax.all_to_all(operand, axes, 0, 0, tiled=True)  8.27 us
    unnamed x10, local copies, waits for them, and re-layouts  4.74 us
    ppermute x5, waiting for transfers between devices, swap(): return lax.ppermute(x, 'c', SWAP)  3.77 us
    pallas_call x1, Pallas kernels, body(): call(coefficients, [shape(ROWS, RANK)] + [whole] * 3, [SMEM] + [VMEM] * 5...  3.48 us
    pallas_call x2, Pallas kernels, body(): call(kernel, shape(HALF, KV), [SMEM] + [HBM] * 3, buffers)  2.98 us
  transfers between devices with their start and end apart: 7, of which 7 were waited for; matrix products, arithmetic and copies ran while one was open for 0% of the time, Pallas kernels for 6%

profile of v5, /device:TPU:1, one launch (start us, length us, event | category | flops | bytes accessed | tf_op | source)
XLA Modules:
  0.0 115.9 jit_solution(8414068492019229763)
XLA Ops:
  0.6 1.5 %shard_map.77.other_ref = f32[160,1024]{1,0:T(8,128)S(1)} custom-call(s32[1]{0:T(128)} %bitcast.at_ref, f32[320,1024]{1,0:T(8,128)} %base_in.5, bf16[1,320,1024]{2,1,0:T(8,128)(2,1)} %local_in.3, f32[1,320,1024]{2,1,0:T(8,128)} %error_in.3), custom_call_target="tpu_custom_call" | custom-call | flops 1000000 | bytes 1048576 | tf_op jit(solution)/shard_map/pallas_call | solution.py:263
  2.1 3.3 %collective-permute-start = (f32[160,1024]{1,0:T(8,128)S(1)}, f32[160,1024]{1,0:T(8,128)S(1)}, u32[]{:S(2)}, u32[]{:S(2)}) collective-permute-start(f32[160,1024]{1,0:T(8,128)S(1)} %shard_map.77.other_ref), channel_id=1, source_target_pairs={{0,16},{16,0},{1,17},{17,1},{2,18},{18,2},{3,19},{19,3},{4,20},{20... | collective-permute-start | bytes 1966088 | tf_op jit(solution)/shard_map/ppermute | solution.py:255
  5.5 1.5 %shard_map.76.mine_ref.own_ref = f32[160,1024]{1,0:T(8,128)S(1)} custom-call(s32[1]{0:T(128)} %bitcast.at_ref, f32[320,1024]{1,0:T(8,128)} %base_in.5, bf16[1,320,1024]{2,1,0:T(8,128)(2,1)} %local_in.3, f32[1,320,1024]{2,1,0:T(8,128)} %error_in.3), custom_call_target="tpu_custom_call" | custom-call | flops 1000000 | bytes 1048576 | tf_op jit(solution)/shard_map/pallas_call | solution.py:263
  8.0 32.7 %all_to_all.25.got_ref = f32[8,240,128]{2,1,0:T(8,128)S(1)} all-to-all(f32[8,240,128]{2,1,0:T(8,128)S(1)} %shard_map.78), channel_id=1, replica_groups=mesh['z'=8,'c'=2,'x'=4,'y'=4] {'z'}, dimensions={0} | all-to-all | bytes 1966080 | tf_op jit(solution)/shard_map/all_to_all | solution.py:243
  40.8 1.9 %collective-permute-start.1 = (f32[240,128]{1,0:T(8,128)S(1)}, f32[240,128]{1,0:T(8,128)S(1)}, u32[]{:S(2)}, u32[]{:S(2)}) collective-permute-start(f32[240,128]{1,0:T(8,128)S(1)} %shard_map.79.mine_ref), channel_id=1, source_target_pairs={{0,16},{16,0},{1,17},{17,1},{2,18},{18,2},{3,19},{19,3},{4,20},{20... | collective-permute-start | bytes 368648 | tf_op jit(solution)/shard_map/ppermute | solution.py:255
  42.7 1.0 collective-permute-done.1.theirs_ref
  43.6 0.9 shard_map.80
  44.5 15.8 %all_to_all.26.got_ref = f32[16,48,128]{2,1,0:T(8,128)S(1)} all-to-all(f32[16,48,128]{2,1,0:T(8,128)S(1)} %get-tuple-element.18), channel_id=1, replica_groups=mesh['z'=8,'c'=2,'x'=4,'y'=4] {'x','y'}, dimensions={0} | all-to-all | bytes 786432 | tf_op jit(solution)/shard_map/all_to_all | solution.py:243
  60.3 1.1 shard_map.81
  61.4 3.4 %all-to-all-start.2 = ((f32[8,80,128]{2,1,0:T(8,128)}), f32[8,80,128]{2,1,0:T(8,128)S(1)}, u32[]{:S(2)}, u32[]{:S(2)}) async-start(f32[8,80,128]{2,1,0:T(8,128)} %get-tuple-element.20), calls=%async_computation.2 | async-start | bytes 655360 | tf_op jit(solution)/shard_map/all_to_all | solution.py:243
  64.8 1.6 %collective-permute-start.2 = (f32[16,128]{1,0:T(8,128)S(1)}, f32[16,128]{1,0:T(8,128)S(1)}, u32[]{:S(2)}, u32[]{:S(2)}) collective-permute-start(f32[16,128]{1,0:T(8,128)S(1)} %get-tuple-element.21.mine_ref), channel_id=1, source_target_pairs={{0,16},{16,0},{1,17},{17,1},{2,18},{18,2},{3,19},{19,3},{4,20},{20... | collective-permute-start | bytes 24584 | tf_op jit(solution)/shard_map/ppermute | solution.py:255
  67.3 2.1 %shard_map.82.inv_ref = f32[64,64]{1,0:T(8,128)S(1)} custom-call(s32[1]{0:T(128)} %bitcast.at_ref, f32[16,128]{1,0:T(8,128)S(1)} %get-tuple-element.21.mine_ref, f32[16,128]{1,0:T(8,128)S(1)} %collective-permute-done.2.theirs_ref), custom_call_target="tpu_custom_call" | custom-call | flops 1000000000 | bytes 1048576 | tf_op jit(solution)/shard_map/pallas_call | solution.py:279
  69.4 6.5 %all-to-all-done.2.got_ref = f32[8,80,128]{2,1,0:T(8,128)S(1)} async-done(((f32[8,80,128]{2,1,0:T(8,128)}), f32[8,80,128]{2,1,0:T(8,128)S(1)}, u32[]{:S(2)}, u32[]{:S(2)}) %all-to-all-start.2) | async-done | bytes 327712 | tf_op jit(solution)/shard_map/all_to_all | solution.py:243
  75.9 3.2 %collective-permute-start.3 = (f32[80,128]{1,0:T(8,128)S(1)}, f32[80,128]{1,0:T(8,128)S(1)}, u32[]{:S(2)}, u32[]{:S(2)}) collective-permute-start(f32[80,128]{1,0:T(8,128)S(1)} %shard_map.83.mine_ref), channel_id=1, source_target_pairs={{0,16},{16,0},{1,17},{17,1},{2,18},{18,2},{3,19},{19,3},{4,20},{20... | collective-permute-start | bytes 122888 | tf_op jit(solution)/shard_map/ppermute | solution.py:255
  79.1 0.9 collective-permute-done.3.theirs_ref
  80.8 12.5 %all_to_all.27.got_ref = f32[16,48,128]{2,1,0:T(8,128)S(1)} all-to-all(f32[16,48,128]{2,1,0:T(8,128)S(1)} %get-tuple-element.22), channel_id=1, replica_groups=mesh['z'=8,'c'=2,'x'=4,'y'=4] {'x','y'}, dimensions={0} | all-to-all | bytes 786432 | tf_op jit(solution)/shard_map/all_to_all | solution.py:243
  94.1 4.8 %all-to-all-start.4 = ((f32[16,32,128]{2,1,0:T(8,128)}), f32[16,32,128]{2,1,0:T(8,128)S(1)}, u32[]{:S(2)}, u32[]{:S(2)}) async-start(f32[16,32,128]{2,1,0:T(8,128)} %get-tuple-element.23), calls=%async_computation.4 | async-start | bytes 524288 | tf_op jit(solution)/shard_map/all_to_all | solution.py:243
  100.1 3.5 %shard_map.86 = (f32[320,64]{1,0:T(8,128)S(1)}, f32[320,1024]{1,0:T(8,128)S(1)}, f32[320,1024]{1,0:T(8,128)S(1)}, f32[320,1024]{1,0:T(8,128)S(1)}) custom-call(s32[1]{0:T(128)} %bitcast.at_ref, f32[16,128]{1,0:T(8,128)S(1)} %get-tuple-element.24.mine_ref, f32[16,128]{1,0:T(8,128)S(1)} %collective-permute-done.4.theirs_ref, ...), custom_call_target="tpu_custom_call" | custom-call | flops 1000000000 | bytes 1048576 | tf_op jit(solution)/shard_map/pallas_call | solution.py:289
  103.6 1.0 copy-done
  104.6 1.1 copy-done.2
  105.7 5.1 %all-to-all-done.4.full_ref = f32[16,32,128]{2,1,0:T(8,128)S(1)} async-done(((f32[16,32,128]{2,1,0:T(8,128)}), f32[16,32,128]{2,1,0:T(8,128)S(1)}, u32[]{:S(2)}, u32[]{:S(2)}) %all-to-all-start.4) | async-done | bytes 262176 | tf_op jit(solution)/shard_map/all_to_all | solution.py:243
  110.8 1.3 %copy-done.1 = f32[320,1024]{1,0:T(8,128)S(1)} copy-done((f32[320,1024]{1,0:T(8,128)S(1)}, f32[320,1024]{1,0:T(8,128)}, u32[]{:S(2)}) %copy-start.1) | copy-done | bytes 1310744
  112.1 1.3 %copy-done.3 = f32[320,1024]{1,0:T(8,128)S(1)} copy-done((f32[320,1024]{1,0:T(8,128)S(1)}, f32[320,1024]{1,0:T(8,128)}, u32[]{:S(2)}) %copy-start.3) | copy-done | bytes 1310744
  113.4 2.4 %shard_map.87 = (f32[320,1024]{1,0:T(8,128)}, f32[320,1024]{1,0:T(8,128)}, f32[320,1024]{1,0:T(8,128)}) custom-call(f32[16,32,128]{2,1,0:T(8,128)S(1)} %all-to-all-done.4.full_ref, f32[320,64]{1,0:T(8,128)S(1)} %get-tuple-element.26.coef_ref, f32[320,1024]{1,0:T(8,128)S(1)} %get-tuple-element.27.field, f32[320,1024]{1,0:T(8,128)S(1)} %copy-done.1, ...), custom_call_target="tpu_custom_call" | custom-call | tf_op jit(solution)/shard_map/pallas_call | solution.py:297
  (15 shorter events, 4.7 us)
Async XLA Ops:
  2.1 5.1 %copy-start.4 = (f32[1024,64]{0,1:T(8,128)S(1)}, f32[1024,64]{0,1:T(8,128)}, u32[]{:S(2)}) copy-start(f32[1024,64]{0,1:T(8,128)} %param.9) | copy-start | bytes 786436
  2.1 5.1 %collective-permute-start = (f32[160,1024]{1,0:T(8,128)S(1)}, f32[160,1024]{1,0:T(8,128)S(1)}, u32[]{:S(2)}, u32[]{:S(2)}) collective-permute-start(f32[160,1024]{1,0:T(8,128)S(1)} %shard_map.77.other_ref), channel_id=1, source_target_pairs={{0,16},{16,0},{1,17},{17,1},{2,18},{18,2},{3,19},{19,3},{4,20},{20... | collective-permute-start | bytes 1966088 | tf_op jit(solution)/shard_map/ppermute | solution.py:255
  40.8 2.9 %collective-permute-start.1 = (f32[240,128]{1,0:T(8,128)S(1)}, f32[240,128]{1,0:T(8,128)S(1)}, u32[]{:S(2)}, u32[]{:S(2)}) collective-permute-start(f32[240,128]{1,0:T(8,128)S(1)} %shard_map.79.mine_ref), channel_id=1, source_target_pairs={{0,16},{16,0},{1,17},{17,1},{2,18},{18,2},{3,19},{19,3},{4,20},{20... | collective-permute-start | bytes 368648 | tf_op jit(solution)/shard_map/ppermute | solution.py:255
  61.4 14.5 %all-to-all-start.2 = ((f32[8,80,128]{2,1,0:T(8,128)}), f32[8,80,128]{2,1,0:T(8,128)S(1)}, u32[]{:S(2)}, u32[]{:S(2)}) async-start(f32[8,80,128]{2,1,0:T(8,128)} %get-tuple-element.20), calls=%async_computation.2 | async-start | bytes 655360 | tf_op jit(solution)/shard_map/all_to_all | solution.py:243
  64.8 2.4 %collective-permute-start.2 = (f32[16,128]{1,0:T(8,128)S(1)}, f32[16,128]{1,0:T(8,128)S(1)}, u32[]{:S(2)}, u32[]{:S(2)}) collective-permute-start(f32[16,128]{1,0:T(8,128)S(1)} %get-tuple-element.21.mine_ref), channel_id=1, source_target_pairs={{0,16},{16,0},{1,17},{17,1},{2,18},{18,2},{3,19},{19,3},{4,20},{20... | collective-permute-start | bytes 24584 | tf_op jit(solution)/shard_map/ppermute | solution.py:255
  75.9 4.1 %collective-permute-start.3 = (f32[80,128]{1,0:T(8,128)S(1)}, f32[80,128]{1,0:T(8,128)S(1)}, u32[]{:S(2)}, u32[]{:S(2)}) collective-permute-start(f32[80,128]{1,0:T(8,128)S(1)} %shard_map.83.mine_ref), channel_id=1, source_target_pairs={{0,16},{16,0},{1,17},{17,1},{2,18},{18,2},{3,19},{19,3},{4,20},{20... | collective-permute-start | bytes 122888 | tf_op jit(solution)/shard_map/ppermute | solution.py:255
  94.1 16.7 %all-to-all-start.4 = ((f32[16,32,128]{2,1,0:T(8,128)}), f32[16,32,128]{2,1,0:T(8,128)S(1)}, u32[]{:S(2)}, u32[]{:S(2)}) async-start(f32[16,32,128]{2,1,0:T(8,128)} %get-tuple-element.23), calls=%async_computation.4 | async-start | bytes 524288 | tf_op jit(solution)/shard_map/all_to_all | solution.py:243
  98.9 1.2 %collective-permute-start.4 = (f32[16,128]{1,0:T(8,128)S(1)}, f32[16,128]{1,0:T(8,128)S(1)}, u32[]{:S(2)}, u32[]{:S(2)}) collective-permute-start(f32[16,128]{1,0:T(8,128)S(1)} %get-tuple-element.24.mine_ref), channel_id=1, source_target_pairs={{0,16},{16,0},{1,17},{17,1},{2,18},{18,2},{3,19},{19,3},{4,20},{20... | collective-permute-start | bytes 24584 | tf_op jit(solution)/shard_map/ppermute | solution.py:255
  103.6 1.1 copy-start
  104.6 1.1 copy-start.2
  110.8 1.3 %copy-start.1 = (f32[320,1024]{1,0:T(8,128)S(1)}, f32[320,1024]{1,0:T(8,128)}, u32[]{:S(2)}) copy-start(f32[320,1024]{1,0:T(8,128)} %copy-done) | copy-start | bytes 3932164
  112.1 1.3 %copy-start.3 = (f32[320,1024]{1,0:T(8,128)S(1)}, f32[320,1024]{1,0:T(8,128)}, u32[]{:S(2)}) copy-start(f32[320,1024]{1,0:T(8,128)} %copy-done.2) | copy-start | bytes 3932164

commit v6 on v5

--- a/solution.py
+++ b/solution.py
@@ -200,43 +200,59 @@
         out_ref[i] = total[:PART]
 
 
-def coefficients(at_ref, mine_ref, theirs_ref, left_ref, own_ref, other_ref, base_in, mom_in,
-                 coef_ref, field_ref, base_ref, mom_ref, sem):
+def coefficients(at_ref, mine_ref, theirs_ref, left_ref, base_in, mom_in, coef_ref, base_ref, base, mom, sem):
     loads = [
         pltpu.make_async_copy(src, dst, sem.at[i])
-        for i, (src, dst) in enumerate([(base_in, base_ref), (mom_in, mom_ref)])
+        for i, (src, dst) in enumerate([(base_in, base), (mom_in, mom)])
     ]
     for load in loads:
         load.start()
-    c = at_ref[0]
-    inv = inverse_factor(gram_of(c, mine_ref[...], theirs_ref[...]))
+    inv = inverse_factor(gram_of(at_ref[0], mine_ref[...], theirs_ref[...]))
     basis = dot(inv, left_ref[...], 1, 0)
     coef_ref[...] = dot(basis, inv, 0, 0)
-    field_ref[pl.ds(pl.multiple_of(c * HALF, HALF), HALF)] = own_ref[...]
-    field_ref[pl.ds(pl.multiple_of((1 - c) * HALF, HALF), HALF)] = other_ref[...]
     for load in loads:
         load.wait()
-
-
-def finish(full_ref, coef_ref, field, base, mom, base_out, err_out, mom_out, nbase, nerr, nmom, out_sem):
+    base_ref[...] = base[...] - (outer_rate * momentum_decay * momentum_decay) * mom[...]
+
+
+def finish(at_ref, full_ref, coef_ref, own, other, base, mom_in, base_out, err_out, mom_out,
+           mom, nbase, nerr, nmom, in_sem, out_sem):
+    c = at_ref[0]
+    part = HALF // 2
+    count = ROWS // part
+    at = [i * part if i < count // 2 else (i - count // 2) * part for i in range(count)]
+    here = [pl.ds(i * part, part) for i in range(count)]
+    rows = [
+        pl.ds(pl.multiple_of((c if i < count // 2 else 1 - c) * HALF + at[i], part), part)
+        for i in range(count)
+    ]
+    loads = [
+        pltpu.make_async_copy(mom_in.at[rows[i]], mom.at[here[i]], in_sem.at[i]) for i in range(count)
+    ]
+    for load in loads:
+        load.start()
     wt = jnp.concatenate(
-        [jnp.concatenate([full_ref[z * NC + c] for c in range(NC)], axis=0) for z in range(NZ)], axis=1
+        [jnp.concatenate([full_ref[z * NC + k] for k in range(NC)], axis=0) for z in range(NZ)], axis=1
     )
     stores = []
-    part = HALF // 2
-    for i in range(ROWS // part):
-        here = pl.ds(i * part, part)
-        approx = dot(coef_ref[here], wt, 1, 0)
-        nerr[here] = field[here] - approx
-        momentum = momentum_decay * mom[here] + approx
-        nmom[here] = momentum
-        nbase[here] = base[here] - outer_rate * (approx + momentum_decay * momentum)
-        for j, (src, dst) in enumerate([(nbase, base_out), (nerr, err_out), (nmom, mom_out)]):
-            store = pltpu.make_async_copy(src.at[here], dst.at[here], out_sem.at[j, i])
-            store.start()
-            stores.append(store)
-    for store in stores:
-        store.wait()
+
+    def store(j, i, src, dst):
+        copy = pltpu.make_async_copy(src.at[here[i]], dst.at[rows[i]], out_sem.at[j, i])
+        copy.start()
+        stores.append(copy)
+
+    for i in range(count):
+        field = own if i < count // 2 else other
+        approx = dot(coef_ref[rows[i]], wt, 1, 0)
+        nerr[here[i]] = field[pl.ds(at[i], part)] - approx
+        store(0, i, nerr, err_out)
+        nbase[here[i]] = base[rows[i]] - (outer_rate * (1.0 + momentum_decay)) * approx
+        store(1, i, nbase, base_out)
+        loads[i].wait()
+        nmom[here[i]] = momentum_decay * mom[here[i]] + approx
+        store(2, i, nmom, mom_out)
+    for copy in stores:
+        copy.wait()
 
 
 def exchange(operand, axes):
@@ -286,22 +302,22 @@
     )
     full = exchange(send, ("z", "c"))
     whole = shape(ROWS, KV)
-    coef, field, old_base, old_momentum = call(
+    big = pltpu.VMEM((ROWS, KV), F32)
+    coef, partial_base = call(
         coefficients,
-        [shape(ROWS, RANK)] + [whole] * 3,
-        [SMEM] + [VMEM] * 5 + [HBM] * 2,
-        [pltpu.SemaphoreType.DMA((2,))],
-        mib=16,
+        [shape(ROWS, RANK), whole],
+        [SMEM] + [VMEM] * 3 + [HBM] * 2,
+        [big] * 2 + [pltpu.SemaphoreType.DMA((2,))],
         flops=10**9,
-    )(at, gram, swap(gram), left, own, other, in_hbm(base), in_hbm(momentum))
+    )(at, gram, swap(gram), left, in_hbm(base), in_hbm(momentum))
     new_base, new_error, new_momentum = pl.pallas_call(
         finish,
         out_shape=[whole] * 3,
-        in_specs=[VMEM] * 5,
+        in_specs=[SMEM] + [VMEM] * 5 + [HBM],
         out_specs=[HBM] * 3,
-        scratch_shapes=[pltpu.VMEM((ROWS, KV), F32)] * 3 + [pltpu.SemaphoreType.DMA((3, 4))],
+        scratch_shapes=[big] * 4 + [pltpu.SemaphoreType.DMA((4,)), pltpu.SemaphoreType.DMA((3, 4))],
         compiler_params=pltpu.CompilerParams(vmem_limit_bytes=16 * 2**20),
-    )(full, coef, in_vmem(field), in_vmem(old_base), in_vmem(old_momentum))
+    )(at, full, coef, in_vmem(own), in_vmem(other), in_vmem(partial_base), in_hbm(momentum))
     return new_base, new_error[None], new_momentum
 
 

time: 116 us -> 115 us (level)
  local copies, waits for them, and re-layouts: 4.74 us -> 0.01 us
  waiting for transfers between devices: 15.3 us -> 16.9 us
  Pallas kernels: 15.5 us -> 16.9 us
    unnamed x10 -> x2, local copies, waits for them, and re-layouts: 4.74 us -> 0.01 us
    all_to_all x2, waiting for transfers between devices: 11.5 us -> 13.2 us  [exchange(): return lax.all_to_all(operand, axes, 0, 0, tiled=True)]
    pallas_call x2, Pallas kernels: 5.93 us -> 7.4 us  [the longest x1 3.97 us: body(): call(coefficients, [shape(ROWS, RANK), whole], [SMEM] + [VMEM] * 3 + [HBM...]
  transfers between devices with their start and end apart: 7 -> 7, of which waited for: 7 -> 7; matrix products, arithmetic and copies ran while one was open for 0% -> 0% of each run, Pallas kernels for 6% -> 7%
where the time goes in v6:
time: 115 us; the launch traced here: 114 us
  blocking collectives  61 us (53%)
  starting transfers between devices  18.6 us (16%)
  Pallas kernels  16.9 us (15%)
  waiting for transfers between devices  16.9 us (15%)
    all_to_all x3, blocking collectives, exchange(): return lax.all_to_all(operand, axes, 0, 0, tiled=True)  61 us
    all_to_all x2, waiting for transfers between devices, exchange(): return lax.all_to_all(operand, axes, 0, 0, tiled=True)  13.2 us
    ppermute x5, starting transfers between devices, swap(): return lax.ppermute(x, 'c', SWAP)  10.3 us
    all_to_all x2, starting transfers between devices, exchange(): return lax.all_to_all(operand, axes, 0, 0, tiled=True)  8.27 us
    pallas_call x1, Pallas kernels, body(): call(coefficients, [shape(ROWS, RANK), whole], [SMEM] + [VMEM] * 3 + [HBM...  3.97 us
    ppermute x5, waiting for transfers between devices, swap(): return lax.ppermute(x, 'c', SWAP)  3.77 us
    pallas_call x1, Pallas kernels, body(): pl.pallas_call(finish, out_shape=[whole] * 3, in_specs=[SMEM] + [VMEM] *...  3.43 us
    pallas_call x2, Pallas kernels, body(): call(kernel, shape(HALF, KV), [SMEM] + [HBM] * 3, buffers)  2.98 us
  transfers between devices with their start and end apart: 7, of which 7 were waited for; matrix products, arithmetic and copies ran while one was open for 0% of the time, Pallas kernels for 7%

profile of v6, /device:TPU:1, one launch (start us, length us, event | category | flops | bytes accessed | tf_op | source)
XLA Modules:
  0.0 114.2 jit_solution(14460495962433680119)
XLA Ops:
  0.6 1.5 %shard_map.77.other = f32[160,1024]{1,0:T(8,128)S(1)} custom-call(s32[1]{0:T(128)} %bitcast.at_ref, f32[320,1024]{1,0:T(8,128)} %base_in.5, bf16[1,320,1024]{2,1,0:T(8,128)(2,1)} %local_in.3, f32[1,320,1024]{2,1,0:T(8,128)} %error_in.3), custom_call_target="tpu_custom_call" | custom-call | flops 1000000 | bytes 1048576 | tf_op jit(solution)/shard_map/pallas_call | solution.py:279
  2.1 3.3 %collective-permute-start = (f32[160,1024]{1,0:T(8,128)S(1)}, f32[160,1024]{1,0:T(8,128)S(1)}, u32[]{:S(2)}, u32[]{:S(2)}) collective-permute-start(f32[160,1024]{1,0:T(8,128)S(1)} %shard_map.77.other), channel_id=1, source_target_pairs={{0,16},{16,0},{1,17},{17,1},{2,18},{18,2},{3,19},{19,3},{4,20},{20... | collective-permute-start | bytes 1966088 | tf_op jit(solution)/shard_map/ppermute | solution.py:271
  5.5 1.5 %shard_map.76.mine_ref.own = f32[160,1024]{1,0:T(8,128)S(1)} custom-call(s32[1]{0:T(128)} %bitcast.at_ref, f32[320,1024]{1,0:T(8,128)} %base_in.5, bf16[1,320,1024]{2,1,0:T(8,128)(2,1)} %local_in.3, f32[1,320,1024]{2,1,0:T(8,128)} %error_in.3), custom_call_target="tpu_custom_call" | custom-call | flops 1000000 | bytes 1048576 | tf_op jit(solution)/shard_map/pallas_call | solution.py:279
  7.2 0.8 shard_map.78
  8.0 32.7 %all_to_all.25.got_ref = f32[8,240,128]{2,1,0:T(8,128)S(1)} all-to-all(f32[8,240,128]{2,1,0:T(8,128)S(1)} %shard_map.78), channel_id=1, replica_groups=mesh['z'=8,'c'=2,'x'=4,'y'=4] {'z'}, dimensions={0} | all-to-all | bytes 1966080 | tf_op jit(solution)/shard_map/all_to_all | solution.py:259
  40.8 1.9 %collective-permute-start.1 = (f32[240,128]{1,0:T(8,128)S(1)}, f32[240,128]{1,0:T(8,128)S(1)}, u32[]{:S(2)}, u32[]{:S(2)}) collective-permute-start(f32[240,128]{1,0:T(8,128)S(1)} %shard_map.79.mine_ref), channel_id=1, source_target_pairs={{0,16},{16,0},{1,17},{17,1},{2,18},{18,2},{3,19},{19,3},{4,20},{20... | collective-permute-start | bytes 368648 | tf_op jit(solution)/shard_map/ppermute | solution.py:271
  42.7 1.0 collective-permute-done.1.theirs_ref
  43.6 0.9 shard_map.80
  44.5 15.8 %all_to_all.26.got_ref = f32[16,48,128]{2,1,0:T(8,128)S(1)} all-to-all(f32[16,48,128]{2,1,0:T(8,128)S(1)} %get-tuple-element.16), channel_id=1, replica_groups=mesh['z'=8,'c'=2,'x'=4,'y'=4] {'x','y'}, dimensions={0} | all-to-all | bytes 786432 | tf_op jit(solution)/shard_map/all_to_all | solution.py:259
  60.3 1.1 shard_map.81
  61.4 3.4 %all-to-all-start.2 = ((f32[8,80,128]{2,1,0:T(8,128)}), f32[8,80,128]{2,1,0:T(8,128)S(1)}, u32[]{:S(2)}, u32[]{:S(2)}) async-start(f32[8,80,128]{2,1,0:T(8,128)} %get-tuple-element.18), calls=%async_computation.2 | async-start | bytes 655360 | tf_op jit(solution)/shard_map/all_to_all | solution.py:259
  64.8 1.6 %collective-permute-start.2 = (f32[16,128]{1,0:T(8,128)S(1)}, f32[16,128]{1,0:T(8,128)S(1)}, u32[]{:S(2)}, u32[]{:S(2)}) collective-permute-start(f32[16,128]{1,0:T(8,128)S(1)} %get-tuple-element.19.mine_ref), channel_id=1, source_target_pairs={{0,16},{16,0},{1,17},{17,1},{2,18},{18,2},{3,19},{19,3},{4,20},{20... | collective-permute-start | bytes 24584 | tf_op jit(solution)/shard_map/ppermute | solution.py:271
  66.4 0.8 collective-permute-done.2.theirs_ref
  67.3 2.1 %shard_map.82.inv_ref = f32[64,64]{1,0:T(8,128)S(1)} custom-call(s32[1]{0:T(128)} %bitcast.at_ref, f32[16,128]{1,0:T(8,128)S(1)} %get-tuple-element.19.mine_ref, f32[16,128]{1,0:T(8,128)S(1)} %collective-permute-done.2.theirs_ref), custom_call_target="tpu_custom_call" | custom-call | flops 1000000000 | bytes 1048576 | tf_op jit(solution)/shard_map/pallas_call | solution.py:295
  69.4 6.5 %all-to-all-done.2.got_ref = f32[8,80,128]{2,1,0:T(8,128)S(1)} async-done(((f32[8,80,128]{2,1,0:T(8,128)}), f32[8,80,128]{2,1,0:T(8,128)S(1)}, u32[]{:S(2)}, u32[]{:S(2)}) %all-to-all-start.2) | async-done | bytes 327712 | tf_op jit(solution)/shard_map/all_to_all | solution.py:259
  75.9 3.2 %collective-permute-start.3 = (f32[80,128]{1,0:T(8,128)S(1)}, f32[80,128]{1,0:T(8,128)S(1)}, u32[]{:S(2)}, u32[]{:S(2)}) collective-permute-start(f32[80,128]{1,0:T(8,128)S(1)} %shard_map.83.mine_ref), channel_id=1, source_target_pairs={{0,16},{16,0},{1,17},{17,1},{2,18},{18,2},{3,19},{19,3},{4,20},{20... | collective-permute-start | bytes 122888 | tf_op jit(solution)/shard_map/ppermute | solution.py:271
  79.1 0.9 collective-permute-done.3.theirs_ref
  80.0 0.9 shard_map.84
  80.8 12.5 %all_to_all.27.got_ref = f32[16,48,128]{2,1,0:T(8,128)S(1)} all-to-all(f32[16,48,128]{2,1,0:T(8,128)S(1)} %get-tuple-element.20), channel_id=1, replica_groups=mesh['z'=8,'c'=2,'x'=4,'y'=4] {'x','y'}, dimensions={0} | all-to-all | bytes 786432 | tf_op jit(solution)/shard_map/all_to_all | solution.py:259
  94.1 4.8 %all-to-all-start.4 = ((f32[16,32,128]{2,1,0:T(8,128)}), f32[16,32,128]{2,1,0:T(8,128)S(1)}, u32[]{:S(2)}, u32[]{:S(2)}) async-start(f32[16,32,128]{2,1,0:T(8,128)} %get-tuple-element.21), calls=%async_computation.4 | async-start | bytes 524288 | tf_op jit(solution)/shard_map/all_to_all | solution.py:259
  99.2 0.9 collective-permute-done.4.theirs_ref
  100.1 4.0 %shard_map.86 = (f32[320,64]{1,0:T(8,128)S(1)}, f32[320,1024]{1,0:T(8,128)S(1)}) custom-call(s32[1]{0:T(128)} %bitcast.at_ref, f32[16,128]{1,0:T(8,128)S(1)} %get-tuple-element.22.mine_ref, f32[16,128]{1,0:T(8,128)S(1)} %collective-permute-done.4.theirs_ref, f32[64,320]{1,0:T(8,128)S(1)} %get-tuple-element.23.left_ref, f32[320,1024]{1,0:T(8,128)} %base_in.5, ...), custom_call_target="tpu_custom_call" | custom-call | flops 1000000000 | bytes 1048576 | tf_op jit(solution)/shard_map/pallas_call | solution.py:306
  104.1 6.7 %all-to-all-done.4.full_ref = f32[16,32,128]{2,1,0:T(8,128)S(1)} async-done(((f32[16,32,128]{2,1,0:T(8,128)}), f32[16,32,128]{2,1,0:T(8,128)S(1)}, u32[]{:S(2)}, u32[]{:S(2)}) %all-to-all-start.4) | async-done | bytes 262176 | tf_op jit(solution)/shard_map/all_to_all | solution.py:259
  110.8 3.4 %shard_map.87 = (f32[320,1024]{1,0:T(8,128)}, f32[320,1024]{1,0:T(8,128)}, f32[320,1024]{1,0:T(8,128)}) custom-call(s32[1]{0:T(128)} %bitcast.at_ref, f32[16,32,128]{2,1,0:T(8,128)S(1)} %all-to-all-done.4.full_ref, f32[320,64]{1,0:T(8,128)S(1)} %get-tuple-element.24.coef_ref, f32[160,1024]{1,0:T(8,128)S(1)} %shard_map.76.mine_ref.own, ...), custom_call_target="tpu_custom_call" | custom-call | tf_op jit(solution)/shard_map/pallas_call | solution.py:313
  (7 shorter events, 1.4 us)
Async XLA Ops:
  2.1 5.1 %copy-start = (f32[1024,64]{0,1:T(8,128)S(1)}, f32[1024,64]{0,1:T(8,128)}, u32[]{:S(2)}) copy-start(f32[1024,64]{0,1:T(8,128)} %param.9) | copy-start | bytes 786436
  2.1 5.1 %collective-permute-start = (f32[160,1024]{1,0:T(8,128)S(1)}, f32[160,1024]{1,0:T(8,128)S(1)}, u32[]{:S(2)}, u32[]{:S(2)}) collective-permute-start(f32[160,1024]{1,0:T(8,128)S(1)} %shard_map.77.other), channel_id=1, source_target_pairs={{0,16},{16,0},{1,17},{17,1},{2,18},{18,2},{3,19},{19,3},{4,20},{20... | collective-permute-start | bytes 1966088 | tf_op jit(solution)/shard_map/ppermute | solution.py:271
  40.8 2.9 %collective-permute-start.1 = (f32[240,128]{1,0:T(8,128)S(1)}, f32[240,128]{1,0:T(8,128)S(1)}, u32[]{:S(2)}, u32[]{:S(2)}) collective-permute-start(f32[240,128]{1,0:T(8,128)S(1)} %shard_map.79.mine_ref), channel_id=1, source_target_pairs={{0,16},{16,0},{1,17},{17,1},{2,18},{18,2},{3,19},{19,3},{4,20},{20... | collective-permute-start | bytes 368648 | tf_op jit(solution)/shard_map/ppermute | solution.py:271
  61.4 14.5 %all-to-all-start.2 = ((f32[8,80,128]{2,1,0:T(8,128)}), f32[8,80,128]{2,1,0:T(8,128)S(1)}, u32[]{:S(2)}, u32[]{:S(2)}) async-start(f32[8,80,128]{2,1,0:T(8,128)} %get-tuple-element.18), calls=%async_computation.2 | async-start | bytes 655360 | tf_op jit(solution)/shard_map/all_to_all | solution.py:259
  64.8 2.4 %collective-permute-start.2 = (f32[16,128]{1,0:T(8,128)S(1)}, f32[16,128]{1,0:T(8,128)S(1)}, u32[]{:S(2)}, u32[]{:S(2)}) collective-permute-start(f32[16,128]{1,0:T(8,128)S(1)} %get-tuple-element.19.mine_ref), channel_id=1, source_target_pairs={{0,16},{16,0},{1,17},{17,1},{2,18},{18,2},{3,19},{19,3},{4,20},{20... | collective-permute-start | bytes 24584 | tf_op jit(solution)/shard_map/ppermute | solution.py:271
  75.9 4.1 %collective-permute-start.3 = (f32[80,128]{1,0:T(8,128)S(1)}, f32[80,128]{1,0:T(8,128)S(1)}, u32[]{:S(2)}, u32[]{:S(2)}) collective-permute-start(f32[80,128]{1,0:T(8,128)S(1)} %shard_map.83.mine_ref), channel_id=1, source_target_pairs={{0,16},{16,0},{1,17},{17,1},{2,18},{18,2},{3,19},{19,3},{4,20},{20... | collective-permute-start | bytes 122888 | tf_op jit(solution)/shard_map/ppermute | solution.py:271
  94.1 16.7 %all-to-all-start.4 = ((f32[16,32,128]{2,1,0:T(8,128)}), f32[16,32,128]{2,1,0:T(8,128)S(1)}, u32[]{:S(2)}, u32[]{:S(2)}) async-start(f32[16,32,128]{2,1,0:T(8,128)} %get-tuple-element.21), calls=%async_computation.4 | async-start | bytes 524288 | tf_op jit(solution)/shard_map/all_to_all | solution.py:259
  98.9 1.2 %collective-permute-start.4 = (f32[16,128]{1,0:T(8,128)S(1)}, f32[16,128]{1,0:T(8,128)S(1)}, u32[]{:S(2)}, u32[]{:S(2)}) collective-permute-start(f32[16,128]{1,0:T(8,128)S(1)} %get-tuple-element.22.mine_ref), channel_id=1, source_target_pairs={{0,16},{16,0},{1,17},{17,1},{2,18},{18,2},{3,19},{19,3},{4,20},{20... | collective-permute-start | bytes 24584 | tf_op jit(solution)/shard_map/ppermute | solution.py:271

commit v7 on v6

--- a/solution.py
+++ b/solution.py
@@ -10,6 +10,8 @@
 REPLICAS = 16
 RANK = 64
 NZ, NC, NX, NY = 8, 2, 4, 4
+NH = NZ // 2
+Z = ("h", "l")
 XY, ZC = NX * NY, NZ * NC
 ROWS = 320
 HALF = ROWS // 2
@@ -25,6 +27,11 @@
 
 HI = lax.Precision.HIGHEST
 SWAP = [(0, 1), (1, 0)]
+PAIRS = (
+    [(i, i ^ 1) for i in range(NZ)],
+    [(i, (i + 1 if i % 2 else i - 1) % NZ) for i in range(NZ)],
+)
+PAIRED = HALF // 2
 F32 = jnp.float32
 VMEM = pl.BlockSpec(memory_space=pltpu.VMEM)
 SMEM = pl.BlockSpec(memory_space=pltpu.SMEM)
@@ -139,13 +146,32 @@
     half_field(at_ref[0] * HALF, base_in, local_in, error_in, base, local, error, sem, out_ref)
 
 
-def first_send(mine_ref, theirs_ref, query_ref, out_ref):
-    pair = mine_ref[...] + theirs_ref[...]
-    left = dot(pair, query_ref[...], 1, 1)
-    packed = jnp.concatenate([left[: HALF // 2], left[HALF // 2 :]], axis=1)
-    for z in range(NZ):
-        out_ref[z, :HALF] = pair[:, z * SLICE : (z + 1) * SLICE]
-        out_ref[z, HALF:] = packed
+def first_send(low_ref, mine_ref, theirs_ref, query_ref, keep_ref, left_ref, first_ref, second_ref, pair_ref):
+    pair_ref[...] = mine_ref[...] + theirs_ref[...]
+    low = low_ref[0]
+    for h in range(NH):
+        slices = [pl.ds(pl.multiple_of((2 * h + l) * SLICE, SLICE), SLICE) for l in (low, 1 - low)]
+        keep_ref[h] = pair_ref[:, slices[0]]
+        for i, ref in enumerate((first_ref, second_ref)):
+            ref[pl.ds(h * PAIRED, PAIRED)] = pair_ref[pl.ds(i * PAIRED, PAIRED), slices[1]]
+    left = dot(pair_ref[...], query_ref[...], 1, 1)
+    n = PAIRED // 2
+    for i, ref in enumerate((first_ref, second_ref)):
+        at = i * PAIRED
+        packed = jnp.concatenate([left[at : at + n], left[at + n : at + 2 * n]], axis=1)
+        ref[NH * PAIRED :] = packed
+        left_ref[i * n : (i + 1) * n] = packed
+
+
+def fold(keep_ref, left_ref, first_ref, second_ref, out_ref):
+    n = PAIRED // 2
+    for i, ref in enumerate((first_ref, second_ref)):
+        rows = slice(i * PAIRED, (i + 1) * PAIRED)
+        for h in range(NH):
+            out_ref[h, rows] = keep_ref[h, rows] + ref[h * PAIRED : (h + 1) * PAIRED]
+        packed = left_ref[i * n : (i + 1) * n] + ref[NH * PAIRED :]
+        for h in range(NH):
+            out_ref[h, HALF + i * n : HALF + (i + 1) * n] = packed
 
 
 def mean_over_z(got_ref, out_ref):
@@ -156,7 +182,16 @@
     c = at_ref[0]
     halves = in_order(c, mine_ref[...], theirs_ref[...])
     piece = jnp.concatenate([h[:HALF] for h in halves], axis=0)
-    left = jnp.concatenate([p for h in halves for p in (h[HALF:, :RANK], h[HALF:, RANK:])], axis=0)
+    n = PAIRED // 2
+    left = jnp.concatenate(
+        [
+            h[at : at + n, lanes]
+            for h in halves
+            for at in (HALF, HALF + n)
+            for lanes in (slice(0, RANK), slice(RANK, 2 * RANK))
+        ],
+        axis=0,
+    )
     piece_ref[...] = piece
     left_ref[...] = left.T
     put_message(c, left_ref, piece, out_ref)
@@ -274,6 +309,7 @@
 def body(base, local, error, momentum, query):
     c = lax.axis_index("c")
     at = c.astype(jnp.int32)[None]
+    low = lax.axis_index("l").astype(jnp.int32)[None]
     buffers = [pltpu.VMEM((HALF, KV), t) for t in (F32, jnp.bfloat16, F32)]
     buffers.append(pltpu.SemaphoreType.DMA((2, 3)))
     half = lambda kernel: call(kernel, shape(HALF, KV), [SMEM] + [HBM] * 3, buffers)(
@@ -282,8 +318,17 @@
     other = half(other_half)
     theirs = swap(other)
     own = half(own_half)
-    send = call(first_send, shape(NZ, HALF + HALF // 2, 128), [VMEM] * 3)(own, theirs, query.T)
-    mean = call(mean_over_z, shape(HALF + HALF // 2, 128), [VMEM])(exchange(send, "z"))
+    message = shape(NH * PAIRED + PAIRED // 2, 128)
+    keep, left, first, second = call(
+        first_send,
+        [shape(NH, HALF, SLICE), shape(HALF // 2, 128), message, message],
+        [SMEM] + [VMEM] * 3,
+        [pltpu.VMEM((HALF, KV), F32)],
+    )(low, own, theirs, query.T)
+    first = lax.ppermute(first, Z, PAIRS[0])
+    second = lax.ppermute(second, Z, PAIRS[1])
+    send = call(fold, shape(NH, HALF + HALF // 2, 128), [VMEM] * 4)(keep, left, first, second)
+    mean = call(mean_over_z, shape(HALF + HALF // 2, 128), [VMEM])(exchange(send, "h"))
     send, piece, left = call(
         first_message, [shape(XY, PACK, 128), shape(ROWS, SLICE), shape(RANK, ROWS)], [SMEM] + [VMEM] * 2
     )(at, mean, swap(mean))
@@ -291,7 +336,7 @@
         send, gram = call(left_parts, [shape(NZ, LEFT, 128), shape(GRAM, 128)], [VMEM] * 2)(
             exchange(send, ("x", "y")), piece
         )
-        got = exchange(send, "z")
+        got = exchange(send, Z)
         inv = call(factor, shape(RANK, RANK), [SMEM] + [VMEM] * 2, flops=10**9)(at, gram, swap(gram))
         part = call(total_of, shape(LEFT, 128), [VMEM, HBM])(got, inv)
         send, left = call(
@@ -300,7 +345,7 @@
     send, gram = call(right_parts, [shape(ZC, PART, 128), shape(GRAM, 128)], [VMEM])(
         exchange(send, ("x", "y"))
     )
-    full = exchange(send, ("z", "c"))
+    full = exchange(send, Z + ("c",))
     whole = shape(ROWS, KV)
     big = pltpu.VMEM((ROWS, KV), F32)
     coef, partial_base = call(
@@ -322,8 +367,8 @@
 
 
 def solution(mesh):
-    mesh = Mesh(mesh.devices.reshape(NZ, NC, NX, NY), ("z", "c", "x", "y"))
-    outer, shard = ("z", "c"), ("x", "y")
+    mesh = Mesh(mesh.devices.reshape(NH, 2, NC, NX, NY), ("h", "l", "c", "x", "y"))
+    outer, shard = ("h", "l", "c"), ("x", "y")
     in_specs = (
         P(shard, None),
         P(outer, shard, None),

time: 115 us -> 110 us (0.957)
  blocking collectives: 61 us -> 46.6 us
  starting transfers between devices: 18.6 us -> 24.1 us
  waiting for transfers between devices: 16.9 us -> 21.3 us
    all_to_all x3, blocking collectives: 61 us -> 46.6 us  [exchange(): return lax.all_to_all(operand, axes, 0, 0, tiled=True)]
    ppermute x0 -> x2, starting transfers between devices: none -> 4.64 us  [the longest x1 4.55 us: body(): second = lax.ppermute(second, Z, PAIRS[1])]
    ppermute x0 -> x2, waiting for transfers between devices: none -> 4.39 us  [the longest x1 3.1 us: body(): second = lax.ppermute(second, Z, PAIRS[1])]
  transfers between devices with their start and end apart: 7 -> 9, of which waited for: 7 -> 9; matrix products, arithmetic and copies ran while one was open for 0% -> 0% of each run, Pallas kernels for 7% -> 7%
where the time goes in v7:
time: 110 us
  blocking collectives  46.6 us (42%)
  starting transfers between devices  24.1 us (22%)
  waiting for transfers between devices  21.3 us (19%)
  Pallas kernels  17 us (15%)
    all_to_all x3, blocking collectives, exchange(): return lax.all_to_all(operand, axes, 0, 0, tiled=True)  46.6 us
    all_to_all x2, waiting for transfers between devices, exchange(): return lax.all_to_all(operand, axes, 0, 0, tiled=True)  13.2 us
    ppermute x5, starting transfers between devices, swap(): return lax.ppermute(x, 'c', SWAP)  11.2 us
    all_to_all x2, starting transfers between devices, exchange(): return lax.all_to_all(operand, axes, 0, 0, tiled=True)  8.28 us
    ppermute x1, starting transfers between devices, body(): second = lax.ppermute(second, Z, PAIRS[1])  4.55 us
    pallas_call x1, Pallas kernels, body(): call(coefficients, [shape(ROWS, RANK), whole], [SMEM] + [VMEM] * 3 + [HBM...  3.97 us
    ppermute x5, waiting for transfers between devices, swap(): return lax.ppermute(x, 'c', SWAP)  3.72 us
    pallas_call x1, Pallas kernels, body(): pl.pallas_call(finish, out_shape=[whole] * 3, in_specs=[SMEM] + [VMEM] *...  3.42 us
  transfers between devices with their start and end apart: 9, of which 9 were waited for; matrix products, arithmetic and copies ran while one was open for 0% of the time, Pallas kernels for 7%

profile of v7, /device:TPU:1, one launch (start us, length us, event | category | flops | bytes accessed | tf_op | source)
XLA Modules:
  0.0 109.7 jit_solution(18095234454224994412)
XLA Ops:
  0.6 1.5 %shard_map.77.other = f32[160,1024]{1,0:T(8,128)S(1)} custom-call(s32[1]{0:T(128)} %bitcast.at_ref, f32[320,1024]{1,0:T(8,128)} %base_in.5, bf16[1,320,1024]{2,1,0:T(8,128)(2,1)} %local_in.3, f32[1,320,1024]{2,1,0:T(8,128)} %error_in.3), custom_call_target="tpu_custom_call" | custom-call | flops 1000000 | bytes 1048576 | tf_op jit(solution)/shard_map/pallas_call | solution.py:315
  2.1 3.3 %collective-permute-start = (f32[160,1024]{1,0:T(8,128)S(1)}, f32[160,1024]{1,0:T(8,128)S(1)}, u32[]{:S(2)}, u32[]{:S(2)}) collective-permute-start(f32[160,1024]{1,0:T(8,128)S(1)} %shard_map.77.other), channel_id=1, source_target_pairs={{0,16},{16,0},{1,17},{17,1},{2,18},{18,2},{3,19},{19,3},{4,20},{20... | collective-permute-start | bytes 1966088 | tf_op jit(solution)/shard_map/ppermute | solution.py:306
  5.5 1.5 %shard_map.76.mine_ref.own = f32[160,1024]{1,0:T(8,128)S(1)} custom-call(s32[1]{0:T(128)} %bitcast.at_ref, f32[320,1024]{1,0:T(8,128)} %base_in.5, bf16[1,320,1024]{2,1,0:T(8,128)(2,1)} %local_in.3, f32[1,320,1024]{2,1,0:T(8,128)} %error_in.3), custom_call_target="tpu_custom_call" | custom-call | flops 1000000 | bytes 1048576 | tf_op jit(solution)/shard_map/pallas_call | solution.py:315
  8.1 4.6 %collective-permute-start.2 = (f32[360,128]{1,0:T(8,128)S(1)}, f32[360,128]{1,0:T(8,128)S(1)}, u32[]{:S(2)}, u32[]{:S(2)}) collective-permute-start(f32[360,128]{1,0:T(8,128)S(1)} %get-tuple-element.23), channel_id=1, source_target_pairs={{0,224},{32,64},{64,32},{96,128},{128,96},{160,192},{192,160},{224... | collective-permute-start | bytes 552968 | tf_op jit(solution)/shard_map/ppermute | solution.py:329
  12.7 1.3 %collective-permute-done.1.first_ref = f32[360,128]{1,0:T(8,128)S(1)} collective-permute-done((f32[360,128]{1,0:T(8,128)S(1)}, f32[360,128]{1,0:T(8,128)S(1)}, u32[]{:S(2)}, u32[]{:S(2)}) %collective-permute-start.1) | collective-permute-done | bytes 184352 | tf_op jit(solution)/shard_map/ppermute | solution.py:328
  14.0 3.1 %collective-permute-done.2.second_ref = f32[360,128]{1,0:T(8,128)S(1)} collective-permute-done((f32[360,128]{1,0:T(8,128)S(1)}, f32[360,128]{1,0:T(8,128)S(1)}, u32[]{:S(2)}, u32[]{:S(2)}) %collective-permute-start.2) | collective-permute-done | bytes 184352 | tf_op jit(solution)/shard_map/ppermute | solution.py:329
  17.1 18.3 %all_to_all.25.got_ref = f32[4,240,128]{2,1,0:T(8,128)S(1)} all-to-all(f32[4,240,128]{2,1,0:T(8,128)S(1)} %shard_map.79), channel_id=1, replica_groups=mesh['h'=4,'l'=2,'c'=2,'x'=4,'y'=4] {'h'}, dimensions={0} | all-to-all | bytes 983040 | tf_op jit(solution)/shard_map/all_to_all | solution.py:294
  35.4 2.7 %collective-permute-start.3 = (f32[240,128]{1,0:T(8,128)S(1)}, f32[240,128]{1,0:T(8,128)S(1)}, u32[]{:S(2)}, u32[]{:S(2)}) collective-permute-start(f32[240,128]{1,0:T(8,128)S(1)} %shard_map.80.mine_ref), channel_id=1, source_target_pairs={{0,16},{16,0},{1,17},{17,1},{2,18},{18,2},{3,19},{19,3},{4,20},{20... | collective-permute-start | bytes 368648 | tf_op jit(solution)/shard_map/ppermute | solution.py:306
  38.2 1.0 collective-permute-done.3.theirs_ref
  39.2 0.9 shard_map.81
  40.0 15.8 %all_to_all.26.got_ref = f32[16,48,128]{2,1,0:T(8,128)S(1)} all-to-all(f32[16,48,128]{2,1,0:T(8,128)S(1)} %get-tuple-element.24), channel_id=1, replica_groups=mesh['h'=4,'l'=2,'c'=2,'x'=4,'y'=4] {'x','y'}, dimensions={0} | all-to-all | bytes 786432 | tf_op jit(solution)/shard_map/all_to_all | solution.py:294
  55.8 1.1 shard_map.82
  56.9 3.4 %all-to-all-start.2 = ((f32[8,80,128]{2,1,0:T(8,128)}), f32[8,80,128]{2,1,0:T(8,128)S(1)}, u32[]{:S(2)}, u32[]{:S(2)}) async-start(f32[8,80,128]{2,1,0:T(8,128)} %get-tuple-element.26), calls=%async_computation.2 | async-start | bytes 655360 | tf_op jit(solution)/shard_map/all_to_all | solution.py:294
  60.4 1.6 %collective-permute-start.4 = (f32[16,128]{1,0:T(8,128)S(1)}, f32[16,128]{1,0:T(8,128)S(1)}, u32[]{:S(2)}, u32[]{:S(2)}) collective-permute-start(f32[16,128]{1,0:T(8,128)S(1)} %get-tuple-element.27.mine_ref), channel_id=1, source_target_pairs={{0,16},{16,0},{1,17},{17,1},{2,18},{18,2},{3,19},{19,3},{4,20},{20... | collective-permute-start | bytes 24584 | tf_op jit(solution)/shard_map/ppermute | solution.py:306
  62.8 2.1 %shard_map.83.inv_ref = f32[64,64]{1,0:T(8,128)S(1)} custom-call(s32[1]{0:T(128)} %bitcast.at_ref, f32[16,128]{1,0:T(8,128)S(1)} %get-tuple-element.27.mine_ref, f32[16,128]{1,0:T(8,128)S(1)} %collective-permute-done.4.theirs_ref), custom_call_target="tpu_custom_call" | custom-call | flops 1000000000 | bytes 1048576 | tf_op jit(solution)/shard_map/pallas_call | solution.py:340
  64.9 6.5 %all-to-all-done.2.got_ref = f32[8,80,128]{2,1,0:T(8,128)S(1)} async-done(((f32[8,80,128]{2,1,0:T(8,128)}), f32[8,80,128]{2,1,0:T(8,128)S(1)}, u32[]{:S(2)}, u32[]{:S(2)}) %all-to-all-start.2) | async-done | bytes 327712 | tf_op jit(solution)/shard_map/all_to_all | solution.py:294
  71.4 3.2 %collective-permute-start.5 = (f32[80,128]{1,0:T(8,128)S(1)}, f32[80,128]{1,0:T(8,128)S(1)}, u32[]{:S(2)}, u32[]{:S(2)}) collective-permute-start(f32[80,128]{1,0:T(8,128)S(1)} %shard_map.84.mine_ref), channel_id=1, source_target_pairs={{0,16},{16,0},{1,17},{17,1},{2,18},{18,2},{3,19},{19,3},{4,20},{20... | collective-permute-start | bytes 122888 | tf_op jit(solution)/shard_map/ppermute | solution.py:306
  74.6 0.9 collective-permute-done.5.theirs_ref
  76.4 12.5 %all_to_all.27.got_ref = f32[16,48,128]{2,1,0:T(8,128)S(1)} all-to-all(f32[16,48,128]{2,1,0:T(8,128)S(1)} %get-tuple-element.28), channel_id=1, replica_groups=mesh['h'=4,'l'=2,'c'=2,'x'=4,'y'=4] {'x','y'}, dimensions={0} | all-to-all | bytes 786432 | tf_op jit(solution)/shard_map/all_to_all | solution.py:294
  89.6 4.8 %all-to-all-start.4 = ((f32[16,32,128]{2,1,0:T(8,128)}), f32[16,32,128]{2,1,0:T(8,128)S(1)}, u32[]{:S(2)}, u32[]{:S(2)}) async-start(f32[16,32,128]{2,1,0:T(8,128)} %get-tuple-element.29), calls=%async_computation.4 | async-start | bytes 524288 | tf_op jit(solution)/shard_map/all_to_all | solution.py:294
  94.8 0.9 collective-permute-done.6.theirs_ref
  95.6 4.0 %shard_map.87 = (f32[320,64]{1,0:T(8,128)S(1)}, f32[320,1024]{1,0:T(8,128)S(1)}) custom-call(s32[1]{0:T(128)} %bitcast.at_ref, f32[16,128]{1,0:T(8,128)S(1)} %get-tuple-element.30.mine_ref, f32[16,128]{1,0:T(8,128)S(1)} %collective-permute-done.6.theirs_ref, f32[64,320]{1,0:T(8,128)S(1)} %get-tuple-element.31.left_ref, f32[320,1024]{1,0:T(8,128)} %base_in.5, ...), custom_call_target="tpu_custom_call" | custom-call | flops 1000000000 | bytes 1048576 | tf_op jit(solution)/shard_map/pallas_call | solution.py:351
  99.6 6.7 %all-to-all-done.4.full_ref = f32[16,32,128]{2,1,0:T(8,128)S(1)} async-done(((f32[16,32,128]{2,1,0:T(8,128)}), f32[16,32,128]{2,1,0:T(8,128)S(1)}, u32[]{:S(2)}, u32[]{:S(2)}) %all-to-all-start.4) | async-done | bytes 262176 | tf_op jit(solution)/shard_map/all_to_all | solution.py:294
  106.3 3.4 %shard_map.88 = (f32[320,1024]{1,0:T(8,128)}, f32[320,1024]{1,0:T(8,128)}, f32[320,1024]{1,0:T(8,128)}) custom-call(s32[1]{0:T(128)} %bitcast.at_ref, f32[16,32,128]{2,1,0:T(8,128)S(1)} %all-to-all-done.4.full_ref, f32[320,64]{1,0:T(8,128)S(1)} %get-tuple-element.32.coef_ref, f32[160,1024]{1,0:T(8,128)S(1)} %shard_map.76.mine_ref.own, ...), custom_call_target="tpu_custom_call" | custom-call | tf_op jit(solution)/shard_map/pallas_call | solution.py:358
  (12 shorter events, 3.9 us)
Async XLA Ops:
  2.1 5.1 %collective-permute-start = (f32[160,1024]{1,0:T(8,128)S(1)}, f32[160,1024]{1,0:T(8,128)S(1)}, u32[]{:S(2)}, u32[]{:S(2)}) collective-permute-start(f32[160,1024]{1,0:T(8,128)S(1)} %shard_map.77.other), channel_id=1, source_target_pairs={{0,16},{16,0},{1,17},{17,1},{2,18},{18,2},{3,19},{19,3},{4,20},{20... | collective-permute-start | bytes 1966088 | tf_op jit(solution)/shard_map/ppermute | solution.py:306
  5.5 1.7 %copy-start = (f32[1024,64]{0,1:T(8,128)S(1)}, f32[1024,64]{0,1:T(8,128)}, u32[]{:S(2)}) copy-start(f32[1024,64]{0,1:T(8,128)} %param.9) | copy-start | bytes 786436
  8.0 5.9 %collective-permute-start.1 = (f32[360,128]{1,0:T(8,128)S(1)}, f32[360,128]{1,0:T(8,128)S(1)}, u32[]{:S(2)}, u32[]{:S(2)}) collective-permute-start(f32[360,128]{1,0:T(8,128)S(1)} %get-tuple-element.22), channel_id=1, source_target_pairs={{0,32},{32,0},{64,96},{96,64},{128,160},{160,128},{192,224},{224,1... | collective-permute-start | bytes 552968 | tf_op jit(solution)/shard_map/ppermute | solution.py:328
  8.1 8.9 %collective-permute-start.2 = (f32[360,128]{1,0:T(8,128)S(1)}, f32[360,128]{1,0:T(8,128)S(1)}, u32[]{:S(2)}, u32[]{:S(2)}) collective-permute-start(f32[360,128]{1,0:T(8,128)S(1)} %get-tuple-element.23), channel_id=1, source_target_pairs={{0,224},{32,64},{64,32},{96,128},{128,96},{160,192},{192,160},{224... | collective-permute-start | bytes 552968 | tf_op jit(solution)/shard_map/ppermute | solution.py:329
  35.4 3.7 %collective-permute-start.3 = (f32[240,128]{1,0:T(8,128)S(1)}, f32[240,128]{1,0:T(8,128)S(1)}, u32[]{:S(2)}, u32[]{:S(2)}) collective-permute-start(f32[240,128]{1,0:T(8,128)S(1)} %shard_map.80.mine_ref), channel_id=1, source_target_pairs={{0,16},{16,0},{1,17},{17,1},{2,18},{18,2},{3,19},{19,3},{4,20},{20... | collective-permute-start | bytes 368648 | tf_op jit(solution)/shard_map/ppermute | solution.py:306
  56.9 14.5 %all-to-all-start.2 = ((f32[8,80,128]{2,1,0:T(8,128)}), f32[8,80,128]{2,1,0:T(8,128)S(1)}, u32[]{:S(2)}, u32[]{:S(2)}) async-start(f32[8,80,128]{2,1,0:T(8,128)} %get-tuple-element.26), calls=%async_computation.2 | async-start | bytes 655360 | tf_op jit(solution)/shard_map/all_to_all | solution.py:294
  60.4 2.4 %collective-permute-start.4 = (f32[16,128]{1,0:T(8,128)S(1)}, f32[16,128]{1,0:T(8,128)S(1)}, u32[]{:S(2)}, u32[]{:S(2)}) collective-permute-start(f32[16,128]{1,0:T(8,128)S(1)} %get-tuple-element.27.mine_ref), channel_id=1, source_target_pairs={{0,16},{16,0},{1,17},{17,1},{2,18},{18,2},{3,19},{19,3},{4,20},{20... | collective-permute-start | bytes 24584 | tf_op jit(solution)/shard_map/ppermute | solution.py:306
  71.4 4.1 %collective-permute-start.5 = (f32[80,128]{1,0:T(8,128)S(1)}, f32[80,128]{1,0:T(8,128)S(1)}, u32[]{:S(2)}, u32[]{:S(2)}) collective-permute-start(f32[80,128]{1,0:T(8,128)S(1)} %shard_map.84.mine_ref), channel_id=1, source_target_pairs={{0,16},{16,0},{1,17},{17,1},{2,18},{18,2},{3,19},{19,3},{4,20},{20... | collective-permute-start | bytes 122888 | tf_op jit(solution)/shard_map/ppermute | solution.py:306
  89.6 16.7 %all-to-all-start.4 = ((f32[16,32,128]{2,1,0:T(8,128)}), f32[16,32,128]{2,1,0:T(8,128)S(1)}, u32[]{:S(2)}, u32[]{:S(2)}) async-start(f32[16,32,128]{2,1,0:T(8,128)} %get-tuple-element.29), calls=%async_computation.4 | async-start | bytes 524288 | tf_op jit(solution)/shard_map/all_to_all | solution.py:294
  94.5 1.2 %collective-permute-start.6 = (f32[16,128]{1,0:T(8,128)S(1)}, f32[16,128]{1,0:T(8,128)S(1)}, u32[]{:S(2)}, u32[]{:S(2)}) collective-permute-start(f32[16,128]{1,0:T(8,128)S(1)} %get-tuple-element.30.mine_ref), channel_id=1, source_target_pairs={{0,16},{16,0},{1,17},{17,1},{2,18},{18,2},{3,19},{19,3},{4,20},{20... | collective-permute-start | bytes 24584 | tf_op jit(solution)/shard_map/ppermute | solution.py:306

commit v8 on v7

--- a/solution.py
+++ b/solution.py
@@ -163,19 +163,32 @@
         left_ref[i * n : (i + 1) * n] = packed
 
 
-def fold(keep_ref, left_ref, first_ref, second_ref, out_ref):
+def fold(high_ref, keep_ref, left_ref, first_ref, second_ref, mine_ref, *out_refs):
+    out_ref = out_refs[-1]
+    out_refs = (mine_ref,) + out_refs[:-1]
     n = PAIRED // 2
     for i, ref in enumerate((first_ref, second_ref)):
         rows = slice(i * PAIRED, (i + 1) * PAIRED)
         for h in range(NH):
             out_ref[h, rows] = keep_ref[h, rows] + ref[h * PAIRED : (h + 1) * PAIRED]
         packed = left_ref[i * n : (i + 1) * n] + ref[NH * PAIRED :]
-        for h in range(NH):
-            out_ref[h, HALF + i * n : HALF + (i + 1) * n] = packed
-
-
-def mean_over_z(got_ref, out_ref):
-    out_ref[...] = add_up(got_ref) * (1.0 / REPLICAS)
+        for ref in out_refs:
+            ref[HALF + i * n : HALF + (i + 1) * n] = packed
+    for k, ref in enumerate(out_refs):
+        ref[:HALF] = out_ref[lax.rem(high_ref[0] + k, NH)]
+
+
+def sum_of_four(refs):
+    own, across, one, three = [ref[...] for ref in refs]
+    return (own + across) + (one + three)
+
+
+def mean_over_z(*refs):
+    refs[-1][...] = sum_of_four(refs[:-1]) * (1.0 / REPLICAS)
+
+
+def total_of_four(*refs):
+    refs[-1][...] = sum_of_four(refs[:-1])
 
 
 def first_message(at_ref, mine_ref, theirs_ref, out_ref, piece_ref, left_ref):
@@ -302,6 +315,10 @@
     return pltpu.with_memory_space_constraint(x, pltpu.VMEM)
 
 
+def ring(sends, axis):
+    return [lax.ppermute(sends[k - 1], axis, [(i, (i + k) % 4) for i in range(4)]) for k in (2, 1, 3)]
+
+
 def swap(x):
     return lax.ppermute(x, "c", SWAP)
 
@@ -327,8 +344,12 @@
     )(low, own, theirs, query.T)
     first = lax.ppermute(first, Z, PAIRS[0])
     second = lax.ppermute(second, Z, PAIRS[1])
-    send = call(fold, shape(NH, HALF + HALF // 2, 128), [VMEM] * 4)(keep, left, first, second)
-    mean = call(mean_over_z, shape(HALF + HALF // 2, 128), [VMEM])(exchange(send, "h"))
+    high = lax.axis_index("h").astype(jnp.int32)[None]
+    chunk = shape(HALF + HALF // 2, 128)
+    mine, *sends = call(fold, [chunk] * NH, [SMEM] + [VMEM] * 4, [pltpu.VMEM((NH, HALF, SLICE), F32)])(
+        high, keep, left, first, second
+    )
+    mean = call(mean_over_z, chunk, [VMEM] * NH)(mine, *ring(sends, "h"))
     send, piece, left = call(
         first_message, [shape(XY, PACK, 128), shape(ROWS, SLICE), shape(RANK, ROWS)], [SMEM] + [VMEM] * 2
     )(at, mean, swap(mean))
@@ -345,7 +366,7 @@
     send, gram = call(right_parts, [shape(ZC, PART, 128), shape(GRAM, 128)], [VMEM])(
         exchange(send, ("x", "y"))
     )
-    full = exchange(send, Z + ("c",))
+    full = exchange(in_vmem(send), Z + ("c",))
     whole = shape(ROWS, KV)
     big = pltpu.VMEM((ROWS, KV), F32)
     coef, partial_base = call(

time: 110 us -> 107 us (0.973)
  blocking collectives: 46.6 us -> 28.3 us
  waiting for transfers between devices: 21.3 us -> 29.4 us
  starting transfers between devices: 24.1 us -> 30.8 us
    all_to_all x3 -> x2, blocking collectives: 46.6 us -> 28.3 us  [exchange(): return lax.all_to_all(operand, axes, 0, 0, tiled=True)]
    ppermute x0 -> x3, waiting for transfers between devices: none -> 8.48 us  [ring(): lax.ppermute(sends[k - 1], axis, [(i, (i + k) % 4) for i in range(4)])]
    ppermute x0 -> x3, starting transfers between devices: none -> 7.35 us  [ring(): lax.ppermute(sends[k - 1], axis, [(i, (i + k) % 4) for i in range(4)])]
    ppermute x5, starting transfers between devices: 11.2 us -> 9.44 us  [swap(): return lax.ppermute(x, 'c', SWAP)]
    all_to_all x2, starting transfers between devices: 8.28 us -> 9.41 us  [exchange(): return lax.all_to_all(operand, axes, 0, 0, tiled=True)]
  transfers between devices with their start and end apart: 9 -> 12, of which waited for: 9 -> 12; matrix products, arithmetic and copies ran while one was open for 0% -> 0% of each run, Pallas kernels for 7% -> 7%
where the time goes in v8:
time: 107 us; the launch traced here: 106 us
  starting transfers between devices  30.8 us (29%)
  waiting for transfers between devices  29.4 us (27%)
  blocking collectives  28.3 us (26%)
  Pallas kernels  17.1 us (16%)
    all_to_all x2, blocking collectives, exchange(): return lax.all_to_all(operand, axes, 0, 0, tiled=True)  28.3 us
    all_to_all x2, waiting for transfers between devices, exchange(): return lax.all_to_all(operand, axes, 0, 0, tiled=True)  12.9 us
    ppermute x5, starting transfers between devices, swap(): return lax.ppermute(x, 'c', SWAP)  9.44 us
    all_to_all x2, starting transfers between devices, exchange(): return lax.all_to_all(operand, axes, 0, 0, tiled=True)  9.41 us
    ppermute x3, waiting for transfers between devices, ring(): lax.ppermute(sends[k - 1], axis, [(i, (i + k) % 4) for i in range(4)])  8.48 us
    ppermute x3, starting transfers between devices, ring(): lax.ppermute(sends[k - 1], axis, [(i, (i + k) % 4) for i in range(4)])  7.35 us
    ppermute x1, starting transfers between devices, body(): second = lax.ppermute(second, Z, PAIRS[1])  4.55 us
    pallas_call x1, Pallas kernels, body(): call(coefficients, [shape(ROWS, RANK), whole], [SMEM] + [VMEM] * 3 + [HBM...  3.97 us
  transfers between devices with their start and end apart: 12, of which 12 were waited for; matrix products, arithmetic and copies ran while one was open for 0% of the time, Pallas kernels for 7%

profile of v8, /device:TPU:1, one launch (start us, length us, event | category | flops | bytes accessed | tf_op | source)
XLA Modules:
  0.0 106.5 jit_solution(3299904950512676959)
XLA Ops:
  0.6 1.5 %shard_map.77.other = f32[160,1024]{1,0:T(8,128)S(1)} custom-call(s32[1]{0:T(128)} %bitcast.at_ref, f32[320,1024]{1,0:T(8,128)} %base_in.5, bf16[1,320,1024]{2,1,0:T(8,128)(2,1)} %local_in.3, f32[1,320,1024]{2,1,0:T(8,128)} %error_in.3), custom_call_target="tpu_custom_call" | custom-call | flops 1000000 | bytes 1048576 | tf_op jit(solution)/shard_map/pallas_call | solution.py:332
  2.1 3.3 %collective-permute-start = (f32[160,1024]{1,0:T(8,128)S(1)}, f32[160,1024]{1,0:T(8,128)S(1)}, u32[]{:S(2)}, u32[]{:S(2)}) collective-permute-start(f32[160,1024]{1,0:T(8,128)S(1)} %shard_map.77.other), channel_id=1, source_target_pairs={{0,16},{16,0},{1,17},{17,1},{2,18},{18,2},{3,19},{19,3},{4,20},{20... | collective-permute-start | bytes 1966088 | tf_op jit(solution)/shard_map/ppermute | solution.py:323
  5.5 1.5 %shard_map.76.mine_ref.own = f32[160,1024]{1,0:T(8,128)S(1)} custom-call(s32[1]{0:T(128)} %bitcast.at_ref, f32[320,1024]{1,0:T(8,128)} %base_in.5, bf16[1,320,1024]{2,1,0:T(8,128)(2,1)} %local_in.3, f32[1,320,1024]{2,1,0:T(8,128)} %error_in.3), custom_call_target="tpu_custom_call" | custom-call | flops 1000000 | bytes 1048576 | tf_op jit(solution)/shard_map/pallas_call | solution.py:332
  8.1 4.6 %collective-permute-start.2 = (f32[360,128]{1,0:T(8,128)S(1)}, f32[360,128]{1,0:T(8,128)S(1)}, u32[]{:S(2)}, u32[]{:S(2)}) collective-permute-start(f32[360,128]{1,0:T(8,128)S(1)} %get-tuple-element.27), channel_id=1, source_target_pairs={{0,224},{32,64},{64,32},{96,128},{128,96},{160,192},{192,160},{224... | collective-permute-start | bytes 552968 | tf_op jit(solution)/shard_map/ppermute | solution.py:346
  12.7 1.3 %collective-permute-done.1.first_ref = f32[360,128]{1,0:T(8,128)S(1)} collective-permute-done((f32[360,128]{1,0:T(8,128)S(1)}, f32[360,128]{1,0:T(8,128)S(1)}, u32[]{:S(2)}, u32[]{:S(2)}) %collective-permute-start.1) | collective-permute-done | bytes 184352 | tf_op jit(solution)/shard_map/ppermute | solution.py:345
  14.0 3.1 %collective-permute-done.2.second_ref = f32[360,128]{1,0:T(8,128)S(1)} collective-permute-done((f32[360,128]{1,0:T(8,128)S(1)}, f32[360,128]{1,0:T(8,128)S(1)}, u32[]{:S(2)}, u32[]{:S(2)}) %collective-permute-start.2) | collective-permute-done | bytes 184352 | tf_op jit(solution)/shard_map/ppermute | solution.py:346
  17.1 3.8 %collective-permute-start.3 = (f32[240,128]{1,0:T(8,128)S(1)}, f32[240,128]{1,0:T(8,128)S(1)}, u32[]{:S(2)}, u32[]{:S(2)}) collective-permute-start(f32[240,128]{1,0:T(8,128)S(1)} %get-tuple-element.29), channel_id=1, source_target_pairs={{0,128},{64,192},{128,0},{192,64},{1,129},{65,193},{129,1},{193,65... | collective-permute-start | bytes 368648 | tf_op jit(solution)/shard_map/ppermute | solution.py:319
  20.9 3.6 %collective-permute-start.5 = (f32[240,128]{1,0:T(8,128)S(1)}, f32[240,128]{1,0:T(8,128)S(1)}, u32[]{:S(2)}, u32[]{:S(2)}) collective-permute-start(f32[240,128]{1,0:T(8,128)S(1)} %get-tuple-element.31), channel_id=1, source_target_pairs={{0,192},{64,0},{128,64},{192,128},{1,193},{65,1},{129,65},{193,129... | collective-permute-start | bytes 368648 | tf_op jit(solution)/shard_map/ppermute | solution.py:319
  25.1 3.2 %collective-permute-done.4.refs_2_ = f32[240,128]{1,0:T(8,128)S(1)} collective-permute-done((f32[240,128]{1,0:T(8,128)S(1)}, f32[240,128]{1,0:T(8,128)S(1)}, u32[]{:S(2)}, u32[]{:S(2)}) %collective-permute-start.4) | collective-permute-done | bytes 122912 | tf_op jit(solution)/shard_map/ppermute | solution.py:319
  28.3 4.7 %collective-permute-done.5.refs_3_ = f32[240,128]{1,0:T(8,128)S(1)} collective-permute-done((f32[240,128]{1,0:T(8,128)S(1)}, f32[240,128]{1,0:T(8,128)S(1)}, u32[]{:S(2)}, u32[]{:S(2)}) %collective-permute-start.5) | collective-permute-done | bytes 122912 | tf_op jit(solution)/shard_map/ppermute | solution.py:319
  33.6 1.0 collective-permute-done.6.theirs_ref
  34.6 0.9 shard_map.81
  35.4 15.8 %all_to_all.20.got_ref = f32[16,48,128]{2,1,0:T(8,128)S(1)} all-to-all(f32[16,48,128]{2,1,0:T(8,128)S(1)} %get-tuple-element.32), channel_id=1, replica_groups=mesh['h'=4,'l'=2,'c'=2,'x'=4,'y'=4] {'x','y'}, dimensions={0} | all-to-all | bytes 786432 | tf_op jit(solution)/shard_map/all_to_all | solution.py:307
  51.2 1.1 %shard_map.82 = (f32[8,80,128]{2,1,0:T(8,128)}, f32[16,128]{1,0:T(8,128)S(1)}) custom-call(f32[16,48,128]{2,1,0:T(8,128)S(1)} %all_to_all.20.got_ref, f32[320,128]{1,0:T(8,128)S(1)} %get-tuple-element.33.piece_ref), custom_call_target="tpu_custom_call" | custom-call | flops 1000000 | bytes 1048576 | tf_op jit(solution)/shard_map/pallas_call | solution.py:357
  52.3 4.6 %all-to-all-start.1 = ((f32[8,80,128]{2,1,0:T(8,128)}), f32[8,80,128]{2,1,0:T(8,128)S(1)}, u32[]{:S(2)}, u32[]{:S(2)}) async-start(f32[8,80,128]{2,1,0:T(8,128)} %get-tuple-element.34), calls=%async_computation.1 | async-start | bytes 655360 | tf_op jit(solution)/shard_map/all_to_all | solution.py:307
  56.9 1.8 %collective-permute-start.7 = (f32[16,128]{1,0:T(8,128)S(1)}, f32[16,128]{1,0:T(8,128)S(1)}, u32[]{:S(2)}, u32[]{:S(2)}) collective-permute-start(f32[16,128]{1,0:T(8,128)S(1)} %get-tuple-element.35.mine_ref), channel_id=1, source_target_pairs={{0,16},{16,0},{1,17},{17,1},{2,18},{18,2},{3,19},{19,3},{4,20},{20... | collective-permute-start | bytes 24584 | tf_op jit(solution)/shard_map/ppermute | solution.py:323
  59.5 2.1 %shard_map.83.inv_ref = f32[64,64]{1,0:T(8,128)S(1)} custom-call(s32[1]{0:T(128)} %bitcast.at_ref, f32[16,128]{1,0:T(8,128)S(1)} %get-tuple-element.35.mine_ref, f32[16,128]{1,0:T(8,128)S(1)} %collective-permute-done.7.theirs_ref), custom_call_target="tpu_custom_call" | custom-call | flops 1000000000 | bytes 1048576 | tf_op jit(solution)/shard_map/pallas_call | solution.py:361
  61.6 6.3 %all-to-all-done.1.got_ref = f32[8,80,128]{2,1,0:T(8,128)S(1)} async-done(((f32[8,80,128]{2,1,0:T(8,128)}), f32[8,80,128]{2,1,0:T(8,128)S(1)}, u32[]{:S(2)}, u32[]{:S(2)}) %all-to-all-start.1) | async-done | bytes 327712 | tf_op jit(solution)/shard_map/all_to_all | solution.py:307
  68.0 3.2 %collective-permute-start.8 = (f32[80,128]{1,0:T(8,128)S(1)}, f32[80,128]{1,0:T(8,128)S(1)}, u32[]{:S(2)}, u32[]{:S(2)}) collective-permute-start(f32[80,128]{1,0:T(8,128)S(1)} %shard_map.84.mine_ref), channel_id=1, source_target_pairs={{0,16},{16,0},{1,17},{17,1},{2,18},{18,2},{3,19},{19,3},{4,20},{20... | collective-permute-start | bytes 122888 | tf_op jit(solution)/shard_map/ppermute | solution.py:323
  72.9 12.5 %all_to_all.21.got_ref = f32[16,48,128]{2,1,0:T(8,128)S(1)} all-to-all(f32[16,48,128]{2,1,0:T(8,128)S(1)} %get-tuple-element.36), channel_id=1, replica_groups=mesh['h'=4,'l'=2,'c'=2,'x'=4,'y'=4] {'x','y'}, dimensions={0} | all-to-all | bytes 786432 | tf_op jit(solution)/shard_map/all_to_all | solution.py:307
  86.2 4.8 %all-to-all-start.3 = ((f32[16,32,128]{2,1,0:T(8,128)}), f32[16,32,128]{2,1,0:T(8,128)S(1)}, u32[]{:S(2)}, u32[]{:S(2)}) async-start(f32[16,32,128]{2,1,0:T(8,128)} %get-tuple-element.37), calls=%async_computation.3 | async-start | bytes 524288 | tf_op jit(solution)/shard_map/all_to_all | solution.py:307
  92.4 4.0 %shard_map.87 = (f32[320,64]{1,0:T(8,128)S(1)}, f32[320,1024]{1,0:T(8,128)S(1)}) custom-call(s32[1]{0:T(128)} %bitcast.at_ref, f32[16,128]{1,0:T(8,128)S(1)} %get-tuple-element.38.mine_ref, f32[16,128]{1,0:T(8,128)S(1)} %collective-permute-done.9.theirs_ref, f32[64,320]{1,0:T(8,128)S(1)} %get-tuple-element.39.left_ref, f32[320,1024]{1,0:T(8,128)} %base_in.5, ...), custom_call_target="tpu_custom_call" | custom-call | flops 1000000000 | bytes 1048576 | tf_op jit(solution)/shard_map/pallas_call | solution.py:372
  96.3 6.6 %all-to-all-done.3.full_ref = f32[16,32,128]{2,1,0:T(8,128)S(1)} async-done(((f32[16,32,128]{2,1,0:T(8,128)}), f32[16,32,128]{2,1,0:T(8,128)S(1)}, u32[]{:S(2)}, u32[]{:S(2)}) %all-to-all-start.3) | async-done | bytes 262176 | tf_op jit(solution)/shard_map/all_to_all | solution.py:307
  102.9 3.4 %shard_map.88 = (f32[320,1024]{1,0:T(8,128)}, f32[320,1024]{1,0:T(8,128)}, f32[320,1024]{1,0:T(8,128)}) custom-call(s32[1]{0:T(128)} %bitcast.at_ref, f32[16,32,128]{2,1,0:T(8,128)S(1)} %all-to-all-done.3.full_ref, f32[320,64]{1,0:T(8,128)S(1)} %get-tuple-element.40.coef_ref, f32[160,1024]{1,0:T(8,128)S(1)} %shard_map.76.mine_ref.own, ...), custom_call_target="tpu_custom_call" | custom-call | tf_op jit(solution)/shard_map/pallas_call | solution.py:379
  (17 shorter events, 7.0 us)
Async XLA Ops:
  2.1 5.1 %collective-permute-start = (f32[160,1024]{1,0:T(8,128)S(1)}, f32[160,1024]{1,0:T(8,128)S(1)}, u32[]{:S(2)}, u32[]{:S(2)}) collective-permute-start(f32[160,1024]{1,0:T(8,128)S(1)} %shard_map.77.other), channel_id=1, source_target_pairs={{0,16},{16,0},{1,17},{17,1},{2,18},{18,2},{3,19},{19,3},{4,20},{20... | collective-permute-start | bytes 1966088 | tf_op jit(solution)/shard_map/ppermute | solution.py:323
  5.5 1.7 %copy-start = (f32[1024,64]{0,1:T(8,128)S(1)}, f32[1024,64]{0,1:T(8,128)}, u32[]{:S(2)}) copy-start(f32[1024,64]{0,1:T(8,128)} %param.9) | copy-start | bytes 786436
  8.0 5.9 %collective-permute-start.1 = (f32[360,128]{1,0:T(8,128)S(1)}, f32[360,128]{1,0:T(8,128)S(1)}, u32[]{:S(2)}, u32[]{:S(2)}) collective-permute-start(f32[360,128]{1,0:T(8,128)S(1)} %get-tuple-element.26), channel_id=1, source_target_pairs={{0,32},{32,0},{64,96},{96,64},{128,160},{160,128},{192,224},{224,1... | collective-permute-start | bytes 552968 | tf_op jit(solution)/shard_map/ppermute | solution.py:345
  8.1 8.9 %collective-permute-start.2 = (f32[360,128]{1,0:T(8,128)S(1)}, f32[360,128]{1,0:T(8,128)S(1)}, u32[]{:S(2)}, u32[]{:S(2)}) collective-permute-start(f32[360,128]{1,0:T(8,128)S(1)} %get-tuple-element.27), channel_id=1, source_target_pairs={{0,224},{32,64},{64,32},{96,128},{128,96},{160,192},{192,160},{224... | collective-permute-start | bytes 552968 | tf_op jit(solution)/shard_map/ppermute | solution.py:346
  17.1 7.9 %collective-permute-start.3 = (f32[240,128]{1,0:T(8,128)S(1)}, f32[240,128]{1,0:T(8,128)S(1)}, u32[]{:S(2)}, u32[]{:S(2)}) collective-permute-start(f32[240,128]{1,0:T(8,128)S(1)} %get-tuple-element.29), channel_id=1, source_target_pairs={{0,128},{64,192},{128,0},{192,64},{1,129},{65,193},{129,1},{193,65... | collective-permute-start | bytes 368648 | tf_op jit(solution)/shard_map/ppermute | solution.py:319
  20.9 7.4 %collective-permute-start.4 = (f32[240,128]{1,0:T(8,128)S(1)}, f32[240,128]{1,0:T(8,128)S(1)}, u32[]{:S(2)}, u32[]{:S(2)}) collective-permute-start(f32[240,128]{1,0:T(8,128)S(1)} %get-tuple-element.30), channel_id=1, source_target_pairs={{0,64},{64,128},{128,192},{192,0},{1,65},{65,129},{129,193},{193,1... | collective-permute-start | bytes 368648 | tf_op jit(solution)/shard_map/ppermute | solution.py:319
  20.9 12.1 %collective-permute-start.5 = (f32[240,128]{1,0:T(8,128)S(1)}, f32[240,128]{1,0:T(8,128)S(1)}, u32[]{:S(2)}, u32[]{:S(2)}) collective-permute-start(f32[240,128]{1,0:T(8,128)S(1)} %get-tuple-element.31), channel_id=1, source_target_pairs={{0,192},{64,0},{128,64},{192,128},{1,193},{65,1},{129,65},{193,129... | collective-permute-start | bytes 368648 | tf_op jit(solution)/shard_map/ppermute | solution.py:319
  33.0 1.6 %collective-permute-start.6 = (f32[240,128]{1,0:T(8,128)S(1)}, f32[240,128]{1,0:T(8,128)S(1)}, u32[]{:S(2)}, u32[]{:S(2)}) collective-permute-start(f32[240,128]{1,0:T(8,128)S(1)} %shard_map.80.mine_ref), channel_id=1, source_target_pairs={{0,16},{16,0},{1,17},{17,1},{2,18},{18,2},{3,19},{19,3},{4,20},{20... | collective-permute-start | bytes 368648 | tf_op jit(solution)/shard_map/ppermute | solution.py:323
  52.3 15.6 %all-to-all-start.1 = ((f32[8,80,128]{2,1,0:T(8,128)}), f32[8,80,128]{2,1,0:T(8,128)S(1)}, u32[]{:S(2)}, u32[]{:S(2)}) async-start(f32[8,80,128]{2,1,0:T(8,128)} %get-tuple-element.34), calls=%async_computation.1 | async-start | bytes 655360 | tf_op jit(solution)/shard_map/all_to_all | solution.py:307
  56.9 2.6 %collective-permute-start.7 = (f32[16,128]{1,0:T(8,128)S(1)}, f32[16,128]{1,0:T(8,128)S(1)}, u32[]{:S(2)}, u32[]{:S(2)}) collective-permute-start(f32[16,128]{1,0:T(8,128)S(1)} %get-tuple-element.35.mine_ref), channel_id=1, source_target_pairs={{0,16},{16,0},{1,17},{17,1},{2,18},{18,2},{3,19},{19,3},{4,20},{20... | collective-permute-start | bytes 24584 | tf_op jit(solution)/shard_map/ppermute | solution.py:323
  68.0 4.1 %collective-permute-start.8 = (f32[80,128]{1,0:T(8,128)S(1)}, f32[80,128]{1,0:T(8,128)S(1)}, u32[]{:S(2)}, u32[]{:S(2)}) collective-permute-start(f32[80,128]{1,0:T(8,128)S(1)} %shard_map.84.mine_ref), channel_id=1, source_target_pairs={{0,16},{16,0},{1,17},{17,1},{2,18},{18,2},{3,19},{19,3},{4,20},{20... | collective-permute-start | bytes 122888 | tf_op jit(solution)/shard_map/ppermute | solution.py:323
  86.2 16.7 %all-to-all-start.3 = ((f32[16,32,128]{2,1,0:T(8,128)}), f32[16,32,128]{2,1,0:T(8,128)S(1)}, u32[]{:S(2)}, u32[]{:S(2)}) async-start(f32[16,32,128]{2,1,0:T(8,128)} %get-tuple-element.37), calls=%async_computation.3 | async-start | bytes 524288 | tf_op jit(solution)/shard_map/all_to_all | solution.py:307
  91.0 1.3 %collective-permute-start.9 = (f32[16,128]{1,0:T(8,128)S(1)}, f32[16,128]{1,0:T(8,128)S(1)}, u32[]{:S(2)}, u32[]{:S(2)}) collective-permute-start(f32[16,128]{1,0:T(8,128)S(1)} %get-tuple-element.38.mine_ref), channel_id=1, source_target_pairs={{0,16},{16,0},{1,17},{17,1},{2,18},{18,2},{3,19},{19,3},{4,20},{20... | collective-permute-start | bytes 24584 | tf_op jit(solution)/shard_map/ppermute | solution.py:323

commit v9 on v8

--- a/solution.py
+++ b/solution.py
@@ -56,6 +56,17 @@
 
 def dot(a, b, ca, cb):
     return lax.dot_general(a, b, (((ca,), (cb,)), ((), ())), precision=HI, preferred_element_type=F32)
+
+
+def split(x):
+    high = x.astype(jnp.bfloat16)
+    return high, (x - high.astype(F32)).astype(jnp.bfloat16)
+
+
+def dot3(a, b, ca, cb):
+    (ah, al), (bh, bl) = split(a), split(b)
+    one = lambda x, y: lax.dot_general(x, y, (((ca,), (cb,)), ((), ())), preferred_element_type=F32)
+    return one(ah, bh) + (one(al, bh) + one(ah, bl))
 
 
 def add_up(ref):
@@ -113,7 +124,7 @@
 
 def put_message(c, left_ref, piece, out_ref):
     own = left_ref[pl.ds(pl.multiple_of(c * PART, PART), PART)]
-    wt = dot(own, piece, 1, 0)
+    wt = dot3(own, piece, 1, 0)
     gram = dot(own, left_ref[...], 1, 1)
     gram = jnp.concatenate([gram[:GRAM], gram[GRAM:]], axis=1)
     for i in range(XY):
@@ -154,7 +165,7 @@
         keep_ref[h] = pair_ref[:, slices[0]]
         for i, ref in enumerate((first_ref, second_ref)):
             ref[pl.ds(h * PAIRED, PAIRED)] = pair_ref[pl.ds(i * PAIRED, PAIRED), slices[1]]
-    left = dot(pair_ref[...], query_ref[...], 1, 1)
+    left = dot3(pair_ref[...], query_ref[...], 1, 1)
     n = PAIRED // 2
     for i, ref in enumerate((first_ref, second_ref)):
         at = i * PAIRED
@@ -213,18 +224,24 @@
 def left_parts(got_ref, piece_ref, out_ref, gram_ref):
     total = add_up(got_ref)
     gram_ref[...] = total[PART:]
-    left = dot(piece_ref[...], total[:PART], 1, 1)
+    left = dot3(piece_ref[...], total[:PART], 1, 1)
     packed = jnp.concatenate([left[i * LEFT : (i + 1) * LEFT] for i in range(128 // PART)], axis=1)
-    for z in range(NZ):
-        out_ref[z] = packed
+    out_ref[...] = packed
 
 
 def factor(at_ref, mine_ref, theirs_ref, out_ref):
     out_ref[...] = inverse_factor(gram_of(at_ref[0], mine_ref[...], theirs_ref[...]))
 
 
-def total_of(got_ref, inv_ref, out_ref):
-    out_ref[...] = add_up(got_ref)
+def add_halves(own_ref, first_ref, second_ref, inv_ref, *out_refs):
+    n = first_ref.shape[0]
+    for ref in out_refs:
+        ref[:n] = own_ref[:n] + first_ref[...]
+        ref[n:] = own_ref[n:] + second_ref[...]
+
+
+def total_of(own_ref, across_ref, one_ref, three_ref, out_ref):
+    out_ref[...] = sum_of_four((own_ref, across_ref, one_ref, three_ref))
 
 
 def next_message(at_ref, mine_ref, theirs_ref, inv_ref, piece_ref, out_ref, left_ref):
@@ -257,7 +274,8 @@
         load.start()
     inv = inverse_factor(gram_of(at_ref[0], mine_ref[...], theirs_ref[...]))
     basis = dot(inv, left_ref[...], 1, 0)
-    coef_ref[...] = dot(basis, inv, 0, 0)
+    high, low = split(dot(basis, inv, 0, 0))
+    coef_ref[...] = jnp.concatenate([high, low, high], axis=1)
     for load in loads:
         load.wait()
     base_ref[...] = base[...] - (outer_rate * momentum_decay * momentum_decay) * mom[...]
@@ -282,6 +300,8 @@
     wt = jnp.concatenate(
         [jnp.concatenate([full_ref[z * NC + k] for k in range(NC)], axis=0) for z in range(NZ)], axis=1
     )
+    high, low = split(wt)
+    wt = jnp.concatenate([high, high, low], axis=0)
     stores = []
 
     def store(j, i, src, dst):
@@ -291,7 +311,7 @@
 
     for i in range(count):
         field = own if i < count // 2 else other
-        approx = dot(coef_ref[rows[i]], wt, 1, 0)
+        approx = jnp.dot(coef_ref[rows[i]], wt, preferred_element_type=F32)
         nerr[here[i]] = field[pl.ds(at[i], part)] - approx
         store(0, i, nerr, err_out)
         nbase[here[i]] = base[rows[i]] - (outer_rate * (1.0 + momentum_decay)) * approx
@@ -354,12 +374,14 @@
         first_message, [shape(XY, PACK, 128), shape(ROWS, SLICE), shape(RANK, ROWS)], [SMEM] + [VMEM] * 2
     )(at, mean, swap(mean))
     for step in range(1, ITERS):
-        send, gram = call(left_parts, [shape(NZ, LEFT, 128), shape(GRAM, 128)], [VMEM] * 2)(
+        send, gram = call(left_parts, [shape(LEFT, 128), shape(GRAM, 128)], [VMEM] * 2)(
             exchange(send, ("x", "y")), piece
         )
-        got = exchange(send, Z)
+        n = LEFT // 2
+        pairs = [lax.ppermute(send[i * n : (i + 1) * n], Z, PAIRS[i]) for i in range(2)]
         inv = call(factor, shape(RANK, RANK), [SMEM] + [VMEM] * 2, flops=10**9)(at, gram, swap(gram))
-        part = call(total_of, shape(LEFT, 128), [VMEM, HBM])(got, inv)
+        mine, *sends = call(add_halves, [shape(LEFT, 128)] * NH, [VMEM] * 3 + [HBM])(send, *pairs, inv)
+        part = call(total_of, shape(LEFT, 128), [VMEM] * 4)(mine, *ring(sends, "h"))
         send, left = call(
             next_message, [shape(XY, PACK, 128), shape(RANK, ROWS)], [SMEM] + [VMEM] * 4
         )(at, part, swap(part), inv, piece)
@@ -371,7 +393,7 @@
     big = pltpu.VMEM((ROWS, KV), F32)
     coef, partial_base = call(
         coefficients,
-        [shape(ROWS, RANK), whole],
+        [jax.ShapeDtypeStruct((ROWS, 3 * RANK), jnp.bfloat16), whole],
         [SMEM] + [VMEM] * 3 + [HBM] * 2,
         [big] * 2 + [pltpu.SemaphoreType.DMA((2,))],
         flops=10**9,

time: 107 us -> 105 us (0.981)
  starting transfers between devices: 30.8 us -> 34.7 us
  waiting for transfers between devices: 29.4 us -> 25.9 us
  Pallas kernels: 17.1 us -> 15.1 us
    ppermute x3 -> x6, starting transfers between devices: 7.35 us -> 14.3 us  [ring(): lax.ppermute(sends[k - 1], axis, [(i, (i + k) % 4) for i in range(4)])]
    all_to_all x2 -> x1, waiting for transfers between devices: 12.9 us -> 6.99 us  [exchange(): return lax.all_to_all(operand, axes, 0, 0, tiled=True)]
    all_to_all x2 -> x1, starting transfers between devices: 9.41 us -> 6.67 us  [exchange(): return lax.all_to_all(operand, axes, 0, 0, tiled=True)]
    ppermute x3 -> x6, waiting for transfers between devices: 8.48 us -> 10.7 us  [ring(): lax.ppermute(sends[k - 1], axis, [(i, (i + k) % 4) for i in range(4)])]
    ppermute x5, starting transfers between devices: 9.44 us -> 7.47 us  [swap(): return lax.ppermute(x, 'c', SWAP)]
    ppermute x0 -> x2, starting transfers between devices: none -> 1.68 us  [body(): lax.ppermute(send[i * n:(i + 1) * n], Z, PAIRS[i])]
    pallas_call x3 -> x4, Pallas kernels: 5.08 us -> 3.86 us  [the longest x1 3.54 us: body(): call(coefficients, [jax.ShapeDtypeStruct((ROWS, 3 * RANK), jnp.bfloat16),...]
  transfers between devices with their start and end apart: 12 -> 16, of which waited for: 12 -> 14; matrix products, arithmetic and copies ran while one was open for 0% -> 0% of each run, Pallas kernels for 7% -> 7%
where the time goes in v9:
time: 105 us
  starting transfers between devices  34.7 us (33%)
  blocking collectives  28.3 us (27%)
  waiting for transfers between devices  25.9 us (25%)
  Pallas kernels  15.1 us (14%)
    all_to_all x2, blocking collectives, exchange(): return lax.all_to_all(operand, axes, 0, 0, tiled=True)  28.3 us
    ppermute x6, starting transfers between devices, ring(): lax.ppermute(sends[k - 1], axis, [(i, (i + k) % 4) for i in range(4)])  14.3 us
    ppermute x6, waiting for transfers between devices, ring(): lax.ppermute(sends[k - 1], axis, [(i, (i + k) % 4) for i in range(4)])  10.7 us
    ppermute x5, starting transfers between devices, swap(): return lax.ppermute(x, 'c', SWAP)  7.47 us
    all_to_all x1, waiting for transfers between devices, exchange(): return lax.all_to_all(operand, axes, 0, 0, tiled=True)  6.99 us
    all_to_all x1, starting transfers between devices, exchange(): return lax.all_to_all(operand, axes, 0, 0, tiled=True)  6.67 us
    ppermute x1, starting transfers between devices, body(): second = lax.ppermute(second, Z, PAIRS[1])  4.55 us
    pallas_call x1, Pallas kernels, body(): call(coefficients, [jax.ShapeDtypeStruct((ROWS, 3 * RANK), jnp.bfloat16),...  3.54 us
  transfers between devices with their start and end apart: 16, of which 14 were waited for; matrix products, arithmetic and copies ran while one was open for 0% of the time, Pallas kernels for 7%

profile of v9, /device:TPU:1, one launch (start us, length us, event | category | flops | bytes accessed | tf_op | source)
XLA Modules:
  0.0 104.8 jit_solution(6351179589201977127)
XLA Ops:
  0.6 1.5 %shard_map.77.other = f32[160,1024]{1,0:T(8,128)S(1)} custom-call(s32[1]{0:T(128)} %bitcast.at_ref, f32[320,1024]{1,0:T(8,128)} %base_in.5, bf16[1,320,1024]{2,1,0:T(8,128)(2,1)} %local_in.3, f32[1,320,1024]{2,1,0:T(8,128)} %error_in.3), custom_call_target="tpu_custom_call" | custom-call | flops 1000000 | bytes 1048576 | tf_op jit(solution)/shard_map/pallas_call | solution.py:352
  2.1 3.3 %collective-permute-start = (f32[160,1024]{1,0:T(8,128)S(1)}, f32[160,1024]{1,0:T(8,128)S(1)}, u32[]{:S(2)}, u32[]{:S(2)}) collective-permute-start(f32[160,1024]{1,0:T(8,128)S(1)} %shard_map.77.other), channel_id=1, source_target_pairs={{0,16},{16,0},{1,17},{17,1},{2,18},{18,2},{3,19},{19,3},{4,20},{20... | collective-permute-start | bytes 1966088 | tf_op jit(solution)/shard_map/ppermute | solution.py:343
  5.5 1.5 %shard_map.76.mine_ref.own = f32[160,1024]{1,0:T(8,128)S(1)} custom-call(s32[1]{0:T(128)} %bitcast.at_ref, f32[320,1024]{1,0:T(8,128)} %base_in.5, bf16[1,320,1024]{2,1,0:T(8,128)(2,1)} %local_in.3, f32[1,320,1024]{2,1,0:T(8,128)} %error_in.3), custom_call_target="tpu_custom_call" | custom-call | flops 1000000 | bytes 1048576 | tf_op jit(solution)/shard_map/pallas_call | solution.py:352
  7.9 4.6 %collective-permute-start.2 = (f32[360,128]{1,0:T(8,128)S(1)}, f32[360,128]{1,0:T(8,128)S(1)}, u32[]{:S(2)}, u32[]{:S(2)}) collective-permute-start(f32[360,128]{1,0:T(8,128)S(1)} %get-tuple-element.31), channel_id=1, source_target_pairs={{0,224},{32,64},{64,32},{96,128},{128,96},{160,192},{192,160},{224... | collective-permute-start | bytes 552968 | tf_op jit(solution)/shard_map/ppermute | solution.py:366
  12.4 1.3 %collective-permute-done.1.first_ref = f32[360,128]{1,0:T(8,128)S(1)} collective-permute-done((f32[360,128]{1,0:T(8,128)S(1)}, f32[360,128]{1,0:T(8,128)S(1)}, u32[]{:S(2)}, u32[]{:S(2)}) %collective-permute-start.1) | collective-permute-done | bytes 184352 | tf_op jit(solution)/shard_map/ppermute | solution.py:365
  13.7 3.1 %collective-permute-done.2.second_ref = f32[360,128]{1,0:T(8,128)S(1)} collective-permute-done((f32[360,128]{1,0:T(8,128)S(1)}, f32[360,128]{1,0:T(8,128)S(1)}, u32[]{:S(2)}, u32[]{:S(2)}) %collective-permute-start.2) | collective-permute-done | bytes 184352 | tf_op jit(solution)/shard_map/ppermute | solution.py:366
  16.9 3.8 %collective-permute-start.3 = (f32[240,128]{1,0:T(8,128)S(1)}, f32[240,128]{1,0:T(8,128)S(1)}, u32[]{:S(2)}, u32[]{:S(2)}) collective-permute-start(f32[240,128]{1,0:T(8,128)S(1)} %get-tuple-element.33), channel_id=1, source_target_pairs={{0,128},{64,192},{128,0},{192,64},{1,129},{65,193},{129,1},{193,65... | collective-permute-start | bytes 368648 | tf_op jit(solution)/shard_map/ppermute | solution.py:339
  20.7 3.6 %collective-permute-start.5 = (f32[240,128]{1,0:T(8,128)S(1)}, f32[240,128]{1,0:T(8,128)S(1)}, u32[]{:S(2)}, u32[]{:S(2)}) collective-permute-start(f32[240,128]{1,0:T(8,128)S(1)} %get-tuple-element.35), channel_id=1, source_target_pairs={{0,192},{64,0},{128,64},{192,128},{1,193},{65,1},{129,65},{193,129... | collective-permute-start | bytes 368648 | tf_op jit(solution)/shard_map/ppermute | solution.py:339
  24.8 3.2 %collective-permute-done.4.refs_2_ = f32[240,128]{1,0:T(8,128)S(1)} collective-permute-done((f32[240,128]{1,0:T(8,128)S(1)}, f32[240,128]{1,0:T(8,128)S(1)}, u32[]{:S(2)}, u32[]{:S(2)}) %collective-permute-start.4) | collective-permute-done | bytes 122912 | tf_op jit(solution)/shard_map/ppermute | solution.py:339
  28.0 4.7 %collective-permute-done.5.refs_3_ = f32[240,128]{1,0:T(8,128)S(1)} collective-permute-done((f32[240,128]{1,0:T(8,128)S(1)}, f32[240,128]{1,0:T(8,128)S(1)}, u32[]{:S(2)}, u32[]{:S(2)}) %collective-permute-start.5) | collective-permute-done | bytes 122912 | tf_op jit(solution)/shard_map/ppermute | solution.py:339
  35.1 15.8 %all_to_all.15.got_ref = f32[16,48,128]{2,1,0:T(8,128)S(1)} all-to-all(f32[16,48,128]{2,1,0:T(8,128)S(1)} %get-tuple-element.36), channel_id=1, replica_groups=mesh['h'=4,'l'=2,'c'=2,'x'=4,'y'=4] {'x','y'}, dimensions={0} | all-to-all | bytes 786432 | tf_op jit(solution)/shard_map/all_to_all | solution.py:327
  51.2 1.6 %collective-permute-start.9 = (f32[16,128]{1,0:T(8,128)S(1)}, f32[16,128]{1,0:T(8,128)S(1)}, u32[]{:S(2)}, u32[]{:S(2)}) collective-permute-start(f32[16,128]{1,0:T(8,128)S(1)} %get-tuple-element.39.mine_ref), channel_id=1, source_target_pairs={{0,16},{16,0},{1,17},{17,1},{2,18},{18,2},{3,19},{19,3},{4,20},{20... | collective-permute-start | bytes 24584 | tf_op jit(solution)/shard_map/ppermute | solution.py:343
  52.8 1.7 %collective-permute-start.8 = (f32[40,128]{1,0:T(8,128)S(1)}, f32[40,128]{1,0:T(8,128)S(1)}, u32[]{:S(2)}, u32[]{:S(2)}) collective-permute-start(f32[40,128]{1,0:T(8,128)S(1)} %get-tuple-element.53), channel_id=1, source_target_pairs={{0,224},{32,64},{64,32},{96,128},{128,96},{160,192},{192,160},{224... | collective-permute-start | bytes 61448 | tf_op jit(solution)/shard_map/ppermute | solution.py:381
  54.5 2.1 %shard_map.83.inv_ref = f32[64,64]{1,0:T(8,128)S(1)} custom-call(s32[1]{0:T(128)} %bitcast.at_ref, f32[16,128]{1,0:T(8,128)S(1)} %get-tuple-element.39.mine_ref, f32[16,128]{1,0:T(8,128)S(1)} %collective-permute-done.9.theirs_ref), custom_call_target="tpu_custom_call" | custom-call | flops 1000000000 | bytes 1048576 | tf_op jit(solution)/shard_map/pallas_call | solution.py:382
  57.4 3.3 %collective-permute-start.10 = (f32[80,128]{1,0:T(8,128)S(1)}, f32[80,128]{1,0:T(8,128)S(1)}, u32[]{:S(2)}, u32[]{:S(2)}) collective-permute-start(f32[80,128]{1,0:T(8,128)S(1)} %get-tuple-element.41), channel_id=1, source_target_pairs={{0,128},{64,192},{128,0},{192,64},{1,129},{65,193},{129,1},{193,65... | collective-permute-start | bytes 122888 | tf_op jit(solution)/shard_map/ppermute | solution.py:339
  61.3 3.1 %collective-permute-start.12 = (f32[80,128]{1,0:T(8,128)S(1)}, f32[80,128]{1,0:T(8,128)S(1)}, u32[]{:S(2)}, u32[]{:S(2)}) collective-permute-start(f32[80,128]{1,0:T(8,128)S(1)} %get-tuple-element.43), channel_id=1, source_target_pairs={{0,192},{64,0},{128,64},{192,128},{1,193},{65,1},{129,65},{193,129... | collective-permute-start | bytes 122888 | tf_op jit(solution)/shard_map/ppermute | solution.py:339
  64.3 1.7 %collective-permute-done.11.one_ref = f32[80,128]{1,0:T(8,128)S(1)} collective-permute-done((f32[80,128]{1,0:T(8,128)S(1)}, f32[80,128]{1,0:T(8,128)S(1)}, u32[]{:S(2)}, u32[]{:S(2)}) %collective-permute-start.11) | collective-permute-done | bytes 40992 | tf_op jit(solution)/shard_map/ppermute | solution.py:339
  66.6 1.8 %collective-permute-start.13 = (f32[80,128]{1,0:T(8,128)S(1)}, f32[80,128]{1,0:T(8,128)S(1)}, u32[]{:S(2)}, u32[]{:S(2)}) collective-permute-start(f32[80,128]{1,0:T(8,128)S(1)} %shard_map.85.mine_ref), channel_id=1, source_target_pairs={{0,16},{16,0},{1,17},{17,1},{2,18},{18,2},{3,19},{19,3},{4,20},{20... | collective-permute-start | bytes 122888 | tf_op jit(solution)/shard_map/ppermute | solution.py:343
  70.0 12.5 %all_to_all.16.got_ref = f32[16,48,128]{2,1,0:T(8,128)S(1)} all-to-all(f32[16,48,128]{2,1,0:T(8,128)S(1)} %get-tuple-element.44), channel_id=1, replica_groups=mesh['h'=4,'l'=2,'c'=2,'x'=4,'y'=4] {'x','y'}, dimensions={0} | all-to-all | bytes 786432 | tf_op jit(solution)/shard_map/all_to_all | solution.py:327
  83.3 6.7 %all-to-all-start.2 = ((f32[16,32,128]{2,1,0:T(8,128)}), f32[16,32,128]{2,1,0:T(8,128)S(1)}, u32[]{:S(2)}, u32[]{:S(2)}) async-start(f32[16,32,128]{2,1,0:T(8,128)} %get-tuple-element.45), calls=%async_computation.2 | async-start | bytes 524288 | tf_op jit(solution)/shard_map/all_to_all | solution.py:327
  90.1 1.0 collective-permute-done.14.theirs_ref
  91.1 3.5 %shard_map.88 = (bf16[320,192]{1,0:T(8,128)(2,1)S(1)}, f32[320,1024]{1,0:T(8,128)S(1)}) custom-call(s32[1]{0:T(128)} %bitcast.at_ref, f32[16,128]{1,0:T(8,128)S(1)} %get-tuple-element.46.mine_ref, f32[16,128]{1,0:T(8,128)S(1)} %collective-permute-done.14.theirs_ref, f32[64,320]{1,0:T(8,128)S(1)} %get-tuple-element.47.left_ref, f32[320,1024]{1,0:T(8,128)} %base_in.5, ...), custom_call_target="tpu_custom_call" | custom-call | flops 1000000000 | bytes 1048576 | tf_op jit(solution)/shard_map/pallas_call | solution.py:394
  94.6 7.0 %all-to-all-done.2.full_ref = f32[16,32,128]{2,1,0:T(8,128)S(1)} async-done(((f32[16,32,128]{2,1,0:T(8,128)}), f32[16,32,128]{2,1,0:T(8,128)S(1)}, u32[]{:S(2)}, u32[]{:S(2)}) %all-to-all-start.2) | async-done | bytes 262176 | tf_op jit(solution)/shard_map/all_to_all | solution.py:327
  101.6 3.0 %shard_map.89 = (f32[320,1024]{1,0:T(8,128)}, f32[320,1024]{1,0:T(8,128)}, f32[320,1024]{1,0:T(8,128)}) custom-call(s32[1]{0:T(128)} %bitcast.at_ref, f32[16,32,128]{2,1,0:T(8,128)S(1)} %all-to-all-done.2.full_ref, bf16[320,192]{1,0:T(8,128)(2,1)S(1)} %get-tuple-element.48.coef_ref, f32[160,1024]{1,0:T(8,128)S(1)} %shard_map.76.mine_ref.own, ...), custom_call_target="tpu_custom_call" | custom-call | tf_op jit(solution)/shard_map/pallas_call | solution.py:401
  (27 shorter events, 8.7 us)
Async XLA Ops:
  2.1 5.1 %collective-permute-start = (f32[160,1024]{1,0:T(8,128)S(1)}, f32[160,1024]{1,0:T(8,128)S(1)}, u32[]{:S(2)}, u32[]{:S(2)}) collective-permute-start(f32[160,1024]{1,0:T(8,128)S(1)} %shard_map.77.other), channel_id=1, source_target_pairs={{0,16},{16,0},{1,17},{17,1},{2,18},{18,2},{3,19},{19,3},{4,20},{20... | collective-permute-start | bytes 1966088 | tf_op jit(solution)/shard_map/ppermute | solution.py:343
  5.5 1.7 %copy-start = (f32[1024,64]{0,1:T(8,128)S(1)}, f32[1024,64]{0,1:T(8,128)}, u32[]{:S(2)}) copy-start(f32[1024,64]{0,1:T(8,128)} %param.9) | copy-start | bytes 786436
  7.8 5.9 %collective-permute-start.1 = (f32[360,128]{1,0:T(8,128)S(1)}, f32[360,128]{1,0:T(8,128)S(1)}, u32[]{:S(2)}, u32[]{:S(2)}) collective-permute-start(f32[360,128]{1,0:T(8,128)S(1)} %get-tuple-element.30), channel_id=1, source_target_pairs={{0,32},{32,0},{64,96},{96,64},{128,160},{160,128},{192,224},{224,1... | collective-permute-start | bytes 552968 | tf_op jit(solution)/shard_map/ppermute | solution.py:365
  7.9 8.9 %collective-permute-start.2 = (f32[360,128]{1,0:T(8,128)S(1)}, f32[360,128]{1,0:T(8,128)S(1)}, u32[]{:S(2)}, u32[]{:S(2)}) collective-permute-start(f32[360,128]{1,0:T(8,128)S(1)} %get-tuple-element.31), channel_id=1, source_target_pairs={{0,224},{32,64},{64,32},{96,128},{128,96},{160,192},{192,160},{224... | collective-permute-start | bytes 552968 | tf_op jit(solution)/shard_map/ppermute | solution.py:366
  16.9 7.9 %collective-permute-start.3 = (f32[240,128]{1,0:T(8,128)S(1)}, f32[240,128]{1,0:T(8,128)S(1)}, u32[]{:S(2)}, u32[]{:S(2)}) collective-permute-start(f32[240,128]{1,0:T(8,128)S(1)} %get-tuple-element.33), channel_id=1, source_target_pairs={{0,128},{64,192},{128,0},{192,64},{1,129},{65,193},{129,1},{193,65... | collective-permute-start | bytes 368648 | tf_op jit(solution)/shard_map/ppermute | solution.py:339
  20.7 7.4 %collective-permute-start.4 = (f32[240,128]{1,0:T(8,128)S(1)}, f32[240,128]{1,0:T(8,128)S(1)}, u32[]{:S(2)}, u32[]{:S(2)}) collective-permute-start(f32[240,128]{1,0:T(8,128)S(1)} %get-tuple-element.34), channel_id=1, source_target_pairs={{0,64},{64,128},{128,192},{192,0},{1,65},{65,129},{129,193},{193,1... | collective-permute-start | bytes 368648 | tf_op jit(solution)/shard_map/ppermute | solution.py:339
  20.7 12.0 %collective-permute-start.5 = (f32[240,128]{1,0:T(8,128)S(1)}, f32[240,128]{1,0:T(8,128)S(1)}, u32[]{:S(2)}, u32[]{:S(2)}) collective-permute-start(f32[240,128]{1,0:T(8,128)S(1)} %get-tuple-element.35), channel_id=1, source_target_pairs={{0,192},{64,0},{128,64},{192,128},{1,193},{65,1},{129,65},{193,129... | collective-permute-start | bytes 368648 | tf_op jit(solution)/shard_map/ppermute | solution.py:339
  32.7 1.6 %collective-permute-start.6 = (f32[240,128]{1,0:T(8,128)S(1)}, f32[240,128]{1,0:T(8,128)S(1)}, u32[]{:S(2)}, u32[]{:S(2)}) collective-permute-start(f32[240,128]{1,0:T(8,128)S(1)} %shard_map.80.mine_ref), channel_id=1, source_target_pairs={{0,16},{16,0},{1,17},{17,1},{2,18},{18,2},{3,19},{19,3},{4,20},{20... | collective-permute-start | bytes 368648 | tf_op jit(solution)/shard_map/ppermute | solution.py:343
  51.2 3.3 %collective-permute-start.9 = (f32[16,128]{1,0:T(8,128)S(1)}, f32[16,128]{1,0:T(8,128)S(1)}, u32[]{:S(2)}, u32[]{:S(2)}) collective-permute-start(f32[16,128]{1,0:T(8,128)S(1)} %get-tuple-element.39.mine_ref), channel_id=1, source_target_pairs={{0,16},{16,0},{1,17},{17,1},{2,18},{18,2},{3,19},{19,3},{4,20},{20... | collective-permute-start | bytes 24584 | tf_op jit(solution)/shard_map/ppermute | solution.py:343
  52.8 3.9 %collective-permute-start.8 = (f32[40,128]{1,0:T(8,128)S(1)}, f32[40,128]{1,0:T(8,128)S(1)}, u32[]{:S(2)}, u32[]{:S(2)}) collective-permute-start(f32[40,128]{1,0:T(8,128)S(1)} %get-tuple-element.53), channel_id=1, source_target_pairs={{0,224},{32,64},{64,32},{96,128},{128,96},{160,192},{192,160},{224... | collective-permute-start | bytes 61448 | tf_op jit(solution)/shard_map/ppermute | solution.py:381
  54.5 2.9 %collective-permute-start.7 = (f32[40,128]{1,0:T(8,128)S(1)}, f32[40,128]{1,0:T(8,128)S(1)}, u32[]{:S(2)}, u32[]{:S(2)}) collective-permute-start(f32[40,128]{1,0:T(8,128)S(1)} %get-tuple-element.54), channel_id=1, source_target_pairs={{0,32},{32,0},{64,96},{96,64},{128,160},{160,128},{192,224},{224,1... | collective-permute-start | bytes 61448 | tf_op jit(solution)/shard_map/ppermute | solution.py:381
  57.4 6.9 %collective-permute-start.10 = (f32[80,128]{1,0:T(8,128)S(1)}, f32[80,128]{1,0:T(8,128)S(1)}, u32[]{:S(2)}, u32[]{:S(2)}) collective-permute-start(f32[80,128]{1,0:T(8,128)S(1)} %get-tuple-element.41), channel_id=1, source_target_pairs={{0,128},{64,192},{128,0},{192,64},{1,129},{65,193},{129,1},{193,65... | collective-permute-start | bytes 122888 | tf_op jit(solution)/shard_map/ppermute | solution.py:339
  60.8 5.3 %collective-permute-start.11 = (f32[80,128]{1,0:T(8,128)S(1)}, f32[80,128]{1,0:T(8,128)S(1)}, u32[]{:S(2)}, u32[]{:S(2)}) collective-permute-start(f32[80,128]{1,0:T(8,128)S(1)} %get-tuple-element.42), channel_id=1, source_target_pairs={{0,64},{64,128},{128,192},{192,0},{1,65},{65,129},{129,193},{193,1... | collective-permute-start | bytes 122888 | tf_op jit(solution)/shard_map/ppermute | solution.py:339
  61.3 5.3 %collective-permute-start.12 = (f32[80,128]{1,0:T(8,128)S(1)}, f32[80,128]{1,0:T(8,128)S(1)}, u32[]{:S(2)}, u32[]{:S(2)}) collective-permute-start(f32[80,128]{1,0:T(8,128)S(1)} %get-tuple-element.43), channel_id=1, source_target_pairs={{0,192},{64,0},{128,64},{192,128},{1,193},{65,1},{129,65},{193,129... | collective-permute-start | bytes 122888 | tf_op jit(solution)/shard_map/ppermute | solution.py:339
  66.6 2.6 %collective-permute-start.13 = (f32[80,128]{1,0:T(8,128)S(1)}, f32[80,128]{1,0:T(8,128)S(1)}, u32[]{:S(2)}, u32[]{:S(2)}) collective-permute-start(f32[80,128]{1,0:T(8,128)S(1)} %shard_map.85.mine_ref), channel_id=1, source_target_pairs={{0,16},{16,0},{1,17},{17,1},{2,18},{18,2},{3,19},{19,3},{4,20},{20... | collective-permute-start | bytes 122888 | tf_op jit(solution)/shard_map/ppermute | solution.py:343
  83.3 18.4 %all-to-all-start.2 = ((f32[16,32,128]{2,1,0:T(8,128)}), f32[16,32,128]{2,1,0:T(8,128)S(1)}, u32[]{:S(2)}, u32[]{:S(2)}) async-start(f32[16,32,128]{2,1,0:T(8,128)} %get-tuple-element.45), calls=%async_computation.2 | async-start | bytes 524288 | tf_op jit(solution)/shard_map/all_to_all | solution.py:327
  89.9 1.2 %collective-permute-start.14 = (f32[16,128]{1,0:T(8,128)S(1)}, f32[16,128]{1,0:T(8,128)S(1)}, u32[]{:S(2)}, u32[]{:S(2)}) collective-permute-start(f32[16,128]{1,0:T(8,128)S(1)} %get-tuple-element.46.mine_ref), channel_id=1, source_target_pairs={{0,16},{16,0},{1,17},{17,1},{2,18},{18,2},{3,19},{19,3},{4,20},{20... | collective-permute-start | bytes 24584 | tf_op jit(solution)/shard_map/ppermute | solution.py:343

commit v10 on v9

--- a/solution.py
+++ b/solution.py
@@ -32,6 +32,7 @@
     [(i, (i + 1 if i % 2 else i - 1) % NZ) for i in range(NZ)],
 )
 PAIRED = HALF // 2
+DISTANCES = (0, 2, 1, 3)
 F32 = jnp.float32
 VMEM = pl.BlockSpec(memory_space=pltpu.VMEM)
 SMEM = pl.BlockSpec(memory_space=pltpu.SMEM)
@@ -261,8 +262,13 @@
 def right_parts(got_ref, out_ref, gram_ref):
     total = add_up(got_ref)
     gram_ref[...] = total[PART:]
-    for i in range(ZC):
-        out_ref[i] = total[:PART]
+    out_ref[...] = total[:PART]
+
+
+def pair_up(own_ref, theirs_ref, *out_refs):
+    for ref in out_refs:
+        ref[:PART] = own_ref[...]
+        ref[PART:] = theirs_ref[...]
 
 
 def coefficients(at_ref, mine_ref, theirs_ref, left_ref, base_in, mom_in, coef_ref, base_ref, base, mom, sem):
@@ -281,8 +287,21 @@
     base_ref[...] = base[...] - (outer_rate * momentum_decay * momentum_decay) * mom[...]
 
 
-def finish(at_ref, full_ref, coef_ref, own, other, base, mom_in, base_out, err_out, mom_out,
-           mom, nbase, nerr, nmom, in_sem, out_sem):
+def finish(at_ref, low_ref, high_ref, *refs):
+    slices, refs = refs[: 2 * NH], refs[2 * NH :]
+    wt_ref = refs[-1]
+    for i, ref in enumerate(slices):
+        core = at_ref[0] if i < NH else 1 - at_ref[0]
+        ranks = pl.ds(pl.multiple_of(core * PART, PART), PART)
+        h = lax.rem(high_ref[0] + NH - DISTANCES[i % NH], NH)
+        for j in range(2):
+            l = low_ref[0] if j == 0 else 1 - low_ref[0]
+            wt_ref[2 * h + l, ranks] = ref[j * PART : (j + 1) * PART]
+    write_outputs(at_ref, *refs)
+
+
+def write_outputs(at_ref, coef_ref, own, other, base, mom_in, base_out, err_out, mom_out,
+           mom, nbase, nerr, nmom, in_sem, out_sem, wt_ref):
     c = at_ref[0]
     part = HALF // 2
     count = ROWS // part
@@ -297,9 +316,7 @@
     ]
     for load in loads:
         load.start()
-    wt = jnp.concatenate(
-        [jnp.concatenate([full_ref[z * NC + k] for k in range(NC)], axis=0) for z in range(NZ)], axis=1
-    )
+    wt = jnp.concatenate([wt_ref[z] for z in range(NZ)], axis=1)
     high, low = split(wt)
     wt = jnp.concatenate([high, high, low], axis=0)
     stores = []
@@ -336,7 +353,7 @@
 
 
 def ring(sends, axis):
-    return [lax.ppermute(sends[k - 1], axis, [(i, (i + k) % 4) for i in range(4)]) for k in (2, 1, 3)]
+    return [lax.ppermute(sends[k - 1], axis, [(i, (i + k) % 4) for i in range(4)]) for k in DISTANCES[1:]]
 
 
 def swap(x):
@@ -385,10 +402,10 @@
         send, left = call(
             next_message, [shape(XY, PACK, 128), shape(RANK, ROWS)], [SMEM] + [VMEM] * 4
         )(at, part, swap(part), inv, piece)
-    send, gram = call(right_parts, [shape(ZC, PART, 128), shape(GRAM, 128)], [VMEM])(
+    send, gram = call(right_parts, [shape(PART, 128), shape(GRAM, 128)], [VMEM])(
         exchange(send, ("x", "y"))
     )
-    full = exchange(in_vmem(send), Z + ("c",))
+    other_parity = lax.ppermute(send, Z, PAIRS[0])
     whole = shape(ROWS, KV)
     big = pltpu.VMEM((ROWS, KV), F32)
     coef, partial_base = call(
@@ -398,14 +415,18 @@
         [big] * 2 + [pltpu.SemaphoreType.DMA((2,))],
         flops=10**9,
     )(at, gram, swap(gram), left, in_hbm(base), in_hbm(momentum))
+    mine, *sends = call(pair_up, [shape(2 * PART, 128)] * NH, [VMEM] * 2)(send, other_parity)
+    *got, coef = lax.optimization_barrier((*ring(sends, "h"), coef))
+    slices = [mine, *got, swap(mine)] + [swap(x) for x in got]
     new_base, new_error, new_momentum = pl.pallas_call(
         finish,
         out_shape=[whole] * 3,
-        in_specs=[SMEM] + [VMEM] * 5 + [HBM],
+        in_specs=[SMEM] * 3 + [VMEM] * (2 * NH + 4) + [HBM],
         out_specs=[HBM] * 3,
-        scratch_shapes=[big] * 4 + [pltpu.SemaphoreType.DMA((4,)), pltpu.SemaphoreType.DMA((3, 4))],
+        scratch_shapes=[big] * 4 + [pltpu.SemaphoreType.DMA((4,)), pltpu.SemaphoreType.DMA((3, 4))]
+        + [pltpu.VMEM((NZ, RANK, SLICE), F32)],
         compiler_params=pltpu.CompilerParams(vmem_limit_bytes=16 * 2**20),
-    )(at, full, coef, in_vmem(own), in_vmem(other), in_vmem(partial_base), in_hbm(momentum))
+    )(at, low, high, *slices, coef, in_vmem(own), in_vmem(other), in_vmem(partial_base), in_hbm(momentum))
     return new_base, new_error[None], new_momentum
 
 

time: 105 us -> 104 us (level)
  waiting for transfers between devices: 25.9 us -> 19 us
  starting transfers between devices: 34.7 us -> 41.3 us
    all_to_all x1 -> x0, waiting for transfers between devices: 6.99 us -> none  [exchange(): return lax.all_to_all(operand, axes, 0, 0, tiled=True)]
    all_to_all x1 -> x0, starting transfers between devices: 6.67 us -> none  [exchange(): return lax.all_to_all(operand, axes, 0, 0, tiled=True)]
    ppermute x6 -> x9, starting transfers between devices: 14.3 us -> 20.3 us  [ring(): lax.ppermute(sends[k - 1], axis, [(i, (i + k) % 4) for i in range(4)])]
    ppermute x5 -> x9, starting transfers between devices: 7.47 us -> 13.2 us  [swap(): return lax.ppermute(x, 'c', SWAP)]
    ppermute x0 -> x1, starting transfers between devices: none -> 1.49 us  [body(): other_parity = lax.ppermute(send, Z, PAIRS[0])]
    pallas_call x2 -> x3, Pallas kernels: 3.74 us -> 3.06 us  [the longest x1 3.02 us: body(): pl.pallas_call(finish, out_shape=[whole] * 3, in_specs=[SMEM] * 3 + [VMEM...]
    ppermute x5 -> x9, waiting for transfers between devices: 3.02 us -> 3.14 us  [swap(): return lax.ppermute(x, 'c', SWAP)]
    ppermute x6 -> x9, waiting for transfers between devices: 10.7 us -> 10.7 us  [ring(): lax.ppermute(sends[k - 1], axis, [(i, (i + k) % 4) for i in range(4)])]
  transfers between devices with their start and end apart: 16 -> 23, of which waited for: 14 -> 16; matrix products, arithmetic and copies ran while one was open for 0% -> 0% of each run, Pallas kernels for 7% -> 7%
where the time goes in v10:
time: 104 us
  starting transfers between devices  41.3 us (40%)
  blocking collectives  28.3 us (27%)
  waiting for transfers between devices  19 us (18%)
  Pallas kernels  14.4 us (14%)
    all_to_all x2, blocking collectives, exchange(): return lax.all_to_all(operand, axes, 0, 0, tiled=True)  28.3 us
    ppermute x9, starting transfers between devices, ring(): lax.ppermute(sends[k - 1], axis, [(i, (i + k) % 4) for i in range(4)])  20.3 us
    ppermute x9, starting transfers between devices, swap(): return lax.ppermute(x, 'c', SWAP)  13.2 us
    ppermute x9, waiting for transfers between devices, ring(): lax.ppermute(sends[k - 1], axis, [(i, (i + k) % 4) for i in range(4)])  10.7 us
    ppermute x1, starting transfers between devices, body(): second = lax.ppermute(second, Z, PAIRS[1])  4.55 us
    pallas_call x1, Pallas kernels, body(): call(coefficients, [jax.ShapeDtypeStruct((ROWS, 3 * RANK), jnp.bfloat16),...  3.54 us
    ppermute x9, waiting for transfers between devices, swap(): return lax.ppermute(x, 'c', SWAP)  3.14 us
    ppermute x1, waiting for transfers between devices, body(): second = lax.ppermute(second, Z, PAIRS[1])  3.11 us
  transfers between devices with their start and end apart: 23, of which 16 were waited for; matrix products, arithmetic and copies ran while one was open for 0% of the time, Pallas kernels for 7%

profile of v10, /device:TPU:1, one launch (start us, length us, event | category | flops | bytes accessed | tf_op | source)
XLA Modules:
  0.0 103.8 jit_solution(7073818818289696208)
XLA Ops:
  0.6 1.5 %shard_map.77.refs_10_ = f32[160,1024]{1,0:T(8,128)S(1)} custom-call(s32[1]{0:T(128)} %bitcast.at_ref, f32[320,1024]{1,0:T(8,128)} %base_in.5, bf16[1,320,1024]{2,1,0:T(8,128)(2,1)} %local_in.3, f32[1,320,1024]{2,1,0:T(8,128)} %error_in.3), custom_call_target="tpu_custom_call" | custom-call | flops 1000000 | bytes 1048576 | tf_op jit(solution)/shard_map/pallas_call | solution.py:369
  2.1 3.3 %collective-permute-start = (f32[160,1024]{1,0:T(8,128)S(1)}, f32[160,1024]{1,0:T(8,128)S(1)}, u32[]{:S(2)}, u32[]{:S(2)}) collective-permute-start(f32[160,1024]{1,0:T(8,128)S(1)} %shard_map.77.refs_10_), channel_id=1, source_target_pairs={{0,16},{16,0},{1,17},{17,1},{2,18},{18,2},{3,19},{19,3},{4,20},{20... | collective-permute-start | bytes 1966088 | tf_op jit(solution)/shard_map/ppermute | solution.py:360
  5.5 1.5 %shard_map.76.mine_ref.refs_9_ = f32[160,1024]{1,0:T(8,128)S(1)} custom-call(s32[1]{0:T(128)} %bitcast.at_ref, f32[320,1024]{1,0:T(8,128)} %base_in.5, bf16[1,320,1024]{2,1,0:T(8,128)(2,1)} %local_in.3, f32[1,320,1024]{2,1,0:T(8,128)} %error_in.3), custom_call_target="tpu_custom_call" | custom-call | flops 1000000 | bytes 1048576 | tf_op jit(solution)/shard_map/pallas_call | solution.py:369
  7.9 4.6 %collective-permute-start.2 = (f32[360,128]{1,0:T(8,128)S(1)}, f32[360,128]{1,0:T(8,128)S(1)}, u32[]{:S(2)}, u32[]{:S(2)}) collective-permute-start(f32[360,128]{1,0:T(8,128)S(1)} %get-tuple-element.39), channel_id=1, source_target_pairs={{0,224},{32,64},{64,32},{96,128},{128,96},{160,192},{192,160},{224... | collective-permute-start | bytes 552968 | tf_op jit(solution)/shard_map/ppermute | solution.py:383
  13.7 3.1 %collective-permute-done.2.second_ref = f32[360,128]{1,0:T(8,128)S(1)} collective-permute-done((f32[360,128]{1,0:T(8,128)S(1)}, f32[360,128]{1,0:T(8,128)S(1)}, u32[]{:S(2)}, u32[]{:S(2)}) %collective-permute-start.2) | collective-permute-done | bytes 184352 | tf_op jit(solution)/shard_map/ppermute | solution.py:383
  16.9 3.8 %collective-permute-start.3 = (f32[240,128]{1,0:T(8,128)S(1)}, f32[240,128]{1,0:T(8,128)S(1)}, u32[]{:S(2)}, u32[]{:S(2)}) collective-permute-start(f32[240,128]{1,0:T(8,128)S(1)} %get-tuple-element.41), channel_id=1, source_target_pairs={{0,128},{64,192},{128,0},{192,64},{1,129},{65,193},{129,1},{193,65... | collective-permute-start | bytes 368648 | tf_op jit(solution)/shard_map/ppermute | solution.py:356
  20.7 3.6 %collective-permute-start.5 = (f32[240,128]{1,0:T(8,128)S(1)}, f32[240,128]{1,0:T(8,128)S(1)}, u32[]{:S(2)}, u32[]{:S(2)}) collective-permute-start(f32[240,128]{1,0:T(8,128)S(1)} %get-tuple-element.43), channel_id=1, source_target_pairs={{0,192},{64,0},{128,64},{192,128},{1,193},{65,1},{129,65},{193,129... | collective-permute-start | bytes 368648 | tf_op jit(solution)/shard_map/ppermute | solution.py:356
  24.8 3.2 %collective-permute-done.4.refs_2_ = f32[240,128]{1,0:T(8,128)S(1)} collective-permute-done((f32[240,128]{1,0:T(8,128)S(1)}, f32[240,128]{1,0:T(8,128)S(1)}, u32[]{:S(2)}, u32[]{:S(2)}) %collective-permute-start.4) | collective-permute-done | bytes 122912 | tf_op jit(solution)/shard_map/ppermute | solution.py:356
  28.0 4.7 %collective-permute-done.5.refs_3_ = f32[240,128]{1,0:T(8,128)S(1)} collective-permute-done((f32[240,128]{1,0:T(8,128)S(1)}, f32[240,128]{1,0:T(8,128)S(1)}, u32[]{:S(2)}, u32[]{:S(2)}) %collective-permute-start.5) | collective-permute-done | bytes 122912 | tf_op jit(solution)/shard_map/ppermute | solution.py:356
  35.1 15.8 %all_to_all.10.got_ref = f32[16,48,128]{2,1,0:T(8,128)S(1)} all-to-all(f32[16,48,128]{2,1,0:T(8,128)S(1)} %get-tuple-element.44), channel_id=1, replica_groups=mesh['h'=4,'l'=2,'c'=2,'x'=4,'y'=4] {'x','y'}, dimensions={0} | all-to-all | bytes 786432 | tf_op jit(solution)/shard_map/all_to_all | solution.py:344
  51.2 1.6 %collective-permute-start.9 = (f32[16,128]{1,0:T(8,128)S(1)}, f32[16,128]{1,0:T(8,128)S(1)}, u32[]{:S(2)}, u32[]{:S(2)}) collective-permute-start(f32[16,128]{1,0:T(8,128)S(1)} %get-tuple-element.47.mine_ref), channel_id=1, source_target_pairs={{0,16},{16,0},{1,17},{17,1},{2,18},{18,2},{3,19},{19,3},{4,20},{20... | collective-permute-start | bytes 24584 | tf_op jit(solution)/shard_map/ppermute | solution.py:360
  52.8 1.7 %collective-permute-start.8 = (f32[40,128]{1,0:T(8,128)S(1)}, f32[40,128]{1,0:T(8,128)S(1)}, u32[]{:S(2)}, u32[]{:S(2)}) collective-permute-start(f32[40,128]{1,0:T(8,128)S(1)} %get-tuple-element.69), channel_id=1, source_target_pairs={{0,224},{32,64},{64,32},{96,128},{128,96},{160,192},{192,160},{224... | collective-permute-start | bytes 61448 | tf_op jit(solution)/shard_map/ppermute | solution.py:398
  54.5 2.1 %shard_map.83.inv_ref = f32[64,64]{1,0:T(8,128)S(1)} custom-call(s32[1]{0:T(128)} %bitcast.at_ref, f32[16,128]{1,0:T(8,128)S(1)} %get-tuple-element.47.mine_ref, f32[16,128]{1,0:T(8,128)S(1)} %collective-permute-done.9.theirs_ref), custom_call_target="tpu_custom_call" | custom-call | flops 1000000000 | bytes 1048576 | tf_op jit(solution)/shard_map/pallas_call | solution.py:399
  57.4 3.3 %collective-permute-start.10 = (f32[80,128]{1,0:T(8,128)S(1)}, f32[80,128]{1,0:T(8,128)S(1)}, u32[]{:S(2)}, u32[]{:S(2)}) collective-permute-start(f32[80,128]{1,0:T(8,128)S(1)} %get-tuple-element.49), channel_id=1, source_target_pairs={{0,128},{64,192},{128,0},{192,64},{1,129},{65,193},{129,1},{193,65... | collective-permute-start | bytes 122888 | tf_op jit(solution)/shard_map/ppermute | solution.py:356
  61.3 3.1 %collective-permute-start.12 = (f32[80,128]{1,0:T(8,128)S(1)}, f32[80,128]{1,0:T(8,128)S(1)}, u32[]{:S(2)}, u32[]{:S(2)}) collective-permute-start(f32[80,128]{1,0:T(8,128)S(1)} %get-tuple-element.51), channel_id=1, source_target_pairs={{0,192},{64,0},{128,64},{192,128},{1,193},{65,1},{129,65},{193,129... | collective-permute-start | bytes 122888 | tf_op jit(solution)/shard_map/ppermute | solution.py:356
  64.3 1.7 %collective-permute-done.11.one_ref = f32[80,128]{1,0:T(8,128)S(1)} collective-permute-done((f32[80,128]{1,0:T(8,128)S(1)}, f32[80,128]{1,0:T(8,128)S(1)}, u32[]{:S(2)}, u32[]{:S(2)}) %collective-permute-start.11) | collective-permute-done | bytes 40992 | tf_op jit(solution)/shard_map/ppermute | solution.py:356
  66.6 1.8 %collective-permute-start.13 = (f32[80,128]{1,0:T(8,128)S(1)}, f32[80,128]{1,0:T(8,128)S(1)}, u32[]{:S(2)}, u32[]{:S(2)}) collective-permute-start(f32[80,128]{1,0:T(8,128)S(1)} %shard_map.85.mine_ref), channel_id=1, source_target_pairs={{0,16},{16,0},{1,17},{17,1},{2,18},{18,2},{3,19},{19,3},{4,20},{20... | collective-permute-start | bytes 122888 | tf_op jit(solution)/shard_map/ppermute | solution.py:360
  70.0 12.5 %all_to_all.11.got_ref = f32[16,48,128]{2,1,0:T(8,128)S(1)} all-to-all(f32[16,48,128]{2,1,0:T(8,128)S(1)} %get-tuple-element.52), channel_id=1, replica_groups=mesh['h'=4,'l'=2,'c'=2,'x'=4,'y'=4] {'x','y'}, dimensions={0} | all-to-all | bytes 786432 | tf_op jit(solution)/shard_map/all_to_all | solution.py:344
  84.0 1.8 %collective-permute-start.18 = (f32[16,128]{1,0:T(8,128)S(1)}, f32[16,128]{1,0:T(8,128)S(1)}, u32[]{:S(2)}, u32[]{:S(2)}) collective-permute-start(f32[16,128]{1,0:T(8,128)S(1)} %get-tuple-element.58.mine_ref), channel_id=1, source_target_pairs={{0,16},{16,0},{1,17},{17,1},{2,18},{18,2},{3,19},{19,3},{4,20},{20... | collective-permute-start | bytes 24584 | tf_op jit(solution)/shard_map/ppermute | solution.py:360
  85.8 2.4 %collective-permute-start.15 = (f32[64,128]{1,0:T(8,128)S(1)}, f32[64,128]{1,0:T(8,128)S(1)}, u32[]{:S(2)}, u32[]{:S(2)}) collective-permute-start(f32[64,128]{1,0:T(8,128)S(1)} %get-tuple-element.55), channel_id=1, source_target_pairs={{0,128},{64,192},{128,0},{192,64},{1,129},{65,193},{129,1},{193,65... | collective-permute-start | bytes 98312 | tf_op jit(solution)/shard_map/ppermute | solution.py:356
  88.2 3.3 %collective-permute-start.16 = (f32[64,128]{1,0:T(8,128)S(1)}, f32[64,128]{1,0:T(8,128)S(1)}, u32[]{:S(2)}, u32[]{:S(2)}) collective-permute-start(f32[64,128]{1,0:T(8,128)S(1)} %get-tuple-element.56), channel_id=1, source_target_pairs={{0,64},{64,128},{128,192},{192,0},{1,65},{65,129},{129,193},{193,1... | collective-permute-start | bytes 98312 | tf_op jit(solution)/shard_map/ppermute | solution.py:356
  91.9 3.5 %shard_map.89 = (bf16[320,192]{1,0:T(8,128)(2,1)S(1)}, f32[320,1024]{1,0:T(8,128)S(1)}) custom-call(s32[1]{0:T(128)} %bitcast.at_ref, f32[16,128]{1,0:T(8,128)S(1)} %get-tuple-element.58.mine_ref, f32[16,128]{1,0:T(8,128)S(1)} %collective-permute-done.18.theirs_ref, f32[64,320]{1,0:T(8,128)S(1)} %get-tuple-element.59.left_ref, f32[320,1024]{1,0:T(8,128)} %base_in.5, ...), custom_call_target="tpu_custom_call" | custom-call | flops 1000000000 | bytes 1048576 | tf_op jit(solution)/shard_map/pallas_call | solution.py:411
  95.5 3.4 %collective-permute-start.19 = (f32[64,128]{1,0:T(8,128)S(1)}, f32[64,128]{1,0:T(8,128)S(1)}, u32[]{:S(2)}, u32[]{:S(2)}) collective-permute-start(f32[64,128]{1,0:T(8,128)S(1)} %get-tuple-element.54.refs_0_), channel_id=1, source_target_pairs={{0,16},{16,0},{1,17},{17,1},{2,18},{18,2},{3,19},{19,3},{4,20},{20... | collective-permute-start | bytes 98312 | tf_op jit(solution)/shard_map/ppermute | solution.py:360
  100.7 3.0 %shard_map.90 = (f32[320,1024]{1,0:T(8,128)}, f32[320,1024]{1,0:T(8,128)}, f32[320,1024]{1,0:T(8,128)}) custom-call(s32[1]{0:T(128)} %bitcast.at_ref, s32[1]{0:T(128)} %bitcast.1.low_ref, s32[1]{0:T(128)} %bitcast.2.high_ref, f32[64,128]{1,0:T(8,128)S(1)} %get-tuple-element.54.refs_0_, f32[64,128]{1,0:T(8,128)S(1)} %collective-permute-done.15.refs_1_, ...), custom_call_target="tpu_custom_call" | custom-call | tf_op jit(solution)/shard_map/pallas_call | solution.py:421
  (42 shorter events, 12.7 us)
Async XLA Ops:
  2.1 5.1 %collective-permute-start = (f32[160,1024]{1,0:T(8,128)S(1)}, f32[160,1024]{1,0:T(8,128)S(1)}, u32[]{:S(2)}, u32[]{:S(2)}) collective-permute-start(f32[160,1024]{1,0:T(8,128)S(1)} %shard_map.77.refs_10_), channel_id=1, source_target_pairs={{0,16},{16,0},{1,17},{17,1},{2,18},{18,2},{3,19},{19,3},{4,20},{20... | collective-permute-start | bytes 1966088 | tf_op jit(solution)/shard_map/ppermute | solution.py:360
  5.5 1.7 %copy-start = (f32[1024,64]{0,1:T(8,128)S(1)}, f32[1024,64]{0,1:T(8,128)}, u32[]{:S(2)}) copy-start(f32[1024,64]{0,1:T(8,128)} %param.9) | copy-start | bytes 786436
  7.8 5.9 %collective-permute-start.1 = (f32[360,128]{1,0:T(8,128)S(1)}, f32[360,128]{1,0:T(8,128)S(1)}, u32[]{:S(2)}, u32[]{:S(2)}) collective-permute-start(f32[360,128]{1,0:T(8,128)S(1)} %get-tuple-element.38), channel_id=1, source_target_pairs={{0,32},{32,0},{64,96},{96,64},{128,160},{160,128},{192,224},{224,1... | collective-permute-start | bytes 552968 | tf_op jit(solution)/shard_map/ppermute | solution.py:382
  7.9 8.9 %collective-permute-start.2 = (f32[360,128]{1,0:T(8,128)S(1)}, f32[360,128]{1,0:T(8,128)S(1)}, u32[]{:S(2)}, u32[]{:S(2)}) collective-permute-start(f32[360,128]{1,0:T(8,128)S(1)} %get-tuple-element.39), channel_id=1, source_target_pairs={{0,224},{32,64},{64,32},{96,128},{128,96},{160,192},{192,160},{224... | collective-permute-start | bytes 552968 | tf_op jit(solution)/shard_map/ppermute | solution.py:383
  16.9 7.9 %collective-permute-start.3 = (f32[240,128]{1,0:T(8,128)S(1)}, f32[240,128]{1,0:T(8,128)S(1)}, u32[]{:S(2)}, u32[]{:S(2)}) collective-permute-start(f32[240,128]{1,0:T(8,128)S(1)} %get-tuple-element.41), channel_id=1, source_target_pairs={{0,128},{64,192},{128,0},{192,64},{1,129},{65,193},{129,1},{193,65... | collective-permute-start | bytes 368648 | tf_op jit(solution)/shard_map/ppermute | solution.py:356
  20.7 7.4 %collective-permute-start.4 = (f32[240,128]{1,0:T(8,128)S(1)}, f32[240,128]{1,0:T(8,128)S(1)}, u32[]{:S(2)}, u32[]{:S(2)}) collective-permute-start(f32[240,128]{1,0:T(8,128)S(1)} %get-tuple-element.42), channel_id=1, source_target_pairs={{0,64},{64,128},{128,192},{192,0},{1,65},{65,129},{129,193},{193,1... | collective-permute-start | bytes 368648 | tf_op jit(solution)/shard_map/ppermute | solution.py:356
  20.7 12.0 %collective-permute-start.5 = (f32[240,128]{1,0:T(8,128)S(1)}, f32[240,128]{1,0:T(8,128)S(1)}, u32[]{:S(2)}, u32[]{:S(2)}) collective-permute-start(f32[240,128]{1,0:T(8,128)S(1)} %get-tuple-element.43), channel_id=1, source_target_pairs={{0,192},{64,0},{128,64},{192,128},{1,193},{65,1},{129,65},{193,129... | collective-permute-start | bytes 368648 | tf_op jit(solution)/shard_map/ppermute | solution.py:356
  32.7 1.6 %collective-permute-start.6 = (f32[240,128]{1,0:T(8,128)S(1)}, f32[240,128]{1,0:T(8,128)S(1)}, u32[]{:S(2)}, u32[]{:S(2)}) collective-permute-start(f32[240,128]{1,0:T(8,128)S(1)} %shard_map.80.mine_ref), channel_id=1, source_target_pairs={{0,16},{16,0},{1,17},{17,1},{2,18},{18,2},{3,19},{19,3},{4,20},{20... | collective-permute-start | bytes 368648 | tf_op jit(solution)/shard_map/ppermute | solution.py:360
  51.2 3.3 %collective-permute-start.9 = (f32[16,128]{1,0:T(8,128)S(1)}, f32[16,128]{1,0:T(8,128)S(1)}, u32[]{:S(2)}, u32[]{:S(2)}) collective-permute-start(f32[16,128]{1,0:T(8,128)S(1)} %get-tuple-element.47.mine_ref), channel_id=1, source_target_pairs={{0,16},{16,0},{1,17},{17,1},{2,18},{18,2},{3,19},{19,3},{4,20},{20... | collective-permute-start | bytes 24584 | tf_op jit(solution)/shard_map/ppermute | solution.py:360
  52.8 3.9 %collective-permute-start.8 = (f32[40,128]{1,0:T(8,128)S(1)}, f32[40,128]{1,0:T(8,128)S(1)}, u32[]{:S(2)}, u32[]{:S(2)}) collective-permute-start(f32[40,128]{1,0:T(8,128)S(1)} %get-tuple-element.69), channel_id=1, source_target_pairs={{0,224},{32,64},{64,32},{96,128},{128,96},{160,192},{192,160},{224... | collective-permute-start | bytes 61448 | tf_op jit(solution)/shard_map/ppermute | solution.py:398
  54.5 2.9 %collective-permute-start.7 = (f32[40,128]{1,0:T(8,128)S(1)}, f32[40,128]{1,0:T(8,128)S(1)}, u32[]{:S(2)}, u32[]{:S(2)}) collective-permute-start(f32[40,128]{1,0:T(8,128)S(1)} %get-tuple-element.70), channel_id=1, source_target_pairs={{0,32},{32,0},{64,96},{96,64},{128,160},{160,128},{192,224},{224,1... | collective-permute-start | bytes 61448 | tf_op jit(solution)/shard_map/ppermute | solution.py:398
  57.4 6.9 %collective-permute-start.10 = (f32[80,128]{1,0:T(8,128)S(1)}, f32[80,128]{1,0:T(8,128)S(1)}, u32[]{:S(2)}, u32[]{:S(2)}) collective-permute-start(f32[80,128]{1,0:T(8,128)S(1)} %get-tuple-element.49), channel_id=1, source_target_pairs={{0,128},{64,192},{128,0},{192,64},{1,129},{65,193},{129,1},{193,65... | collective-permute-start | bytes 122888 | tf_op jit(solution)/shard_map/ppermute | solution.py:356
  60.8 5.3 %collective-permute-start.11 = (f32[80,128]{1,0:T(8,128)S(1)}, f32[80,128]{1,0:T(8,128)S(1)}, u32[]{:S(2)}, u32[]{:S(2)}) collective-permute-start(f32[80,128]{1,0:T(8,128)S(1)} %get-tuple-element.50), channel_id=1, source_target_pairs={{0,64},{64,128},{128,192},{192,0},{1,65},{65,129},{129,193},{193,1... | collective-permute-start | bytes 122888 | tf_op jit(solution)/shard_map/ppermute | solution.py:356
  61.3 5.3 %collective-permute-start.12 = (f32[80,128]{1,0:T(8,128)S(1)}, f32[80,128]{1,0:T(8,128)S(1)}, u32[]{:S(2)}, u32[]{:S(2)}) collective-permute-start(f32[80,128]{1,0:T(8,128)S(1)} %get-tuple-element.51), channel_id=1, source_target_pairs={{0,192},{64,0},{128,64},{192,128},{1,193},{65,1},{129,65},{193,129... | collective-permute-start | bytes 122888 | tf_op jit(solution)/shard_map/ppermute | solution.py:356
  66.6 2.6 %collective-permute-start.13 = (f32[80,128]{1,0:T(8,128)S(1)}, f32[80,128]{1,0:T(8,128)S(1)}, u32[]{:S(2)}, u32[]{:S(2)}) collective-permute-start(f32[80,128]{1,0:T(8,128)S(1)} %shard_map.85.mine_ref), channel_id=1, source_target_pairs={{0,16},{16,0},{1,17},{17,1},{2,18},{18,2},{3,19},{19,3},{4,20},{20... | collective-permute-start | bytes 122888 | tf_op jit(solution)/shard_map/ppermute | solution.py:360
  82.5 3.3 %collective-permute-start.14 = (f32[32,128]{1,0:T(8,128)S(1)}, f32[32,128]{1,0:T(8,128)S(1)}, u32[]{:S(2)}, u32[]{:S(2)}) collective-permute-start(f32[32,128]{1,0:T(8,128)S(1)} %get-tuple-element.53.own_ref), channel_id=1, source_target_pairs={{0,32},{32,0},{64,96},{96,64},{128,160},{160,128},{192,224},{224,1... | collective-permute-start | bytes 49160 | tf_op jit(solution)/shard_map/ppermute | solution.py:408
  84.0 7.9 %collective-permute-start.18 = (f32[16,128]{1,0:T(8,128)S(1)}, f32[16,128]{1,0:T(8,128)S(1)}, u32[]{:S(2)}, u32[]{:S(2)}) collective-permute-start(f32[16,128]{1,0:T(8,128)S(1)} %get-tuple-element.58.mine_ref), channel_id=1, source_target_pairs={{0,16},{16,0},{1,17},{17,1},{2,18},{18,2},{3,19},{19,3},{4,20},{20... | collective-permute-start | bytes 24584 | tf_op jit(solution)/shard_map/ppermute | solution.py:360
  85.8 13.0 %collective-permute-start.15 = (f32[64,128]{1,0:T(8,128)S(1)}, f32[64,128]{1,0:T(8,128)S(1)}, u32[]{:S(2)}, u32[]{:S(2)}) collective-permute-start(f32[64,128]{1,0:T(8,128)S(1)} %get-tuple-element.55), channel_id=1, source_target_pairs={{0,128},{64,192},{128,0},{192,64},{1,129},{65,193},{129,1},{193,65... | collective-permute-start | bytes 98312 | tf_op jit(solution)/shard_map/ppermute | solution.py:356
  88.2 10.6 %collective-permute-start.16 = (f32[64,128]{1,0:T(8,128)S(1)}, f32[64,128]{1,0:T(8,128)S(1)}, u32[]{:S(2)}, u32[]{:S(2)}) collective-permute-start(f32[64,128]{1,0:T(8,128)S(1)} %get-tuple-element.56), channel_id=1, source_target_pairs={{0,64},{64,128},{128,192},{192,0},{1,65},{65,129},{129,193},{193,1... | collective-permute-start | bytes 98312 | tf_op jit(solution)/shard_map/ppermute | solution.py:356
  91.6 7.3 %collective-permute-start.17 = (f32[64,128]{1,0:T(8,128)S(1)}, f32[64,128]{1,0:T(8,128)S(1)}, u32[]{:S(2)}, u32[]{:S(2)}) collective-permute-start(f32[64,128]{1,0:T(8,128)S(1)} %get-tuple-element.57), channel_id=1, source_target_pairs={{0,192},{64,0},{128,64},{192,128},{1,193},{65,1},{129,65},{193,129... | collective-permute-start | bytes 98312 | tf_op jit(solution)/shard_map/ppermute | solution.py:356
  95.5 4.2 %collective-permute-start.19 = (f32[64,128]{1,0:T(8,128)S(1)}, f32[64,128]{1,0:T(8,128)S(1)}, u32[]{:S(2)}, u32[]{:S(2)}) collective-permute-start(f32[64,128]{1,0:T(8,128)S(1)} %get-tuple-element.54.refs_0_), channel_id=1, source_target_pairs={{0,16},{16,0},{1,17},{17,1},{2,18},{18,2},{3,19},{19,3},{4,20},{20... | collective-permute-start | bytes 98312 | tf_op jit(solution)/shard_map/ppermute | solution.py:360
  98.9 1.3 %collective-permute-start.20 = (f32[64,128]{1,0:T(8,128)S(1)}, f32[64,128]{1,0:T(8,128)S(1)}, u32[]{:S(2)}, u32[]{:S(2)}) collective-permute-start(f32[64,128]{1,0:T(8,128)S(1)} %collective-permute-done.15.refs_1_), channel_id=1, source_target_pairs={{0,16},{16,0},{1,17},{17,1},{2,18},{18,2},{3,19},{19,3},{4,20},{20... | collective-permute-start | bytes 98312 | tf_op jit(solution)/shard_map/ppermute | solution.py:360
  99.0 1.3 %collective-permute-start.21 = (f32[64,128]{1,0:T(8,128)S(1)}, f32[64,128]{1,0:T(8,128)S(1)}, u32[]{:S(2)}, u32[]{:S(2)}) collective-permute-start(f32[64,128]{1,0:T(8,128)S(1)} %collective-permute-done.16.refs_2_), channel_id=1, source_target_pairs={{0,16},{16,0},{1,17},{17,1},{2,18},{18,2},{3,19},{19,3},{4,20},{20... | collective-permute-start | bytes 98312 | tf_op jit(solution)/shard_map/ppermute | solution.py:360
  99.5 1.2 %collective-permute-start.22 = (f32[64,128]{1,0:T(8,128)S(1)}, f32[64,128]{1,0:T(8,128)S(1)}, u32[]{:S(2)}, u32[]{:S(2)}) collective-permute-start(f32[64,128]{1,0:T(8,128)S(1)} %collective-permute-done.17.refs_3_), channel_id=1, source_target_pairs={{0,16},{16,0},{1,17},{17,1},{2,18},{18,2},{3,19},{19,3},{4,20},{20... | collective-permute-start | bytes 98312 | tf_op jit(solution)/shard_map/ppermute | solution.py:360

commit v11 on v10

--- a/solution.py
+++ b/solution.py
@@ -271,6 +271,12 @@
         ref[PART:] = theirs_ref[...]
 
 
+def join(*refs):
+    n = 2 * PART
+    for i, ref in enumerate(refs[:-1]):
+        refs[-1][i * n : (i + 1) * n] = ref[...]
+
+
 def coefficients(at_ref, mine_ref, theirs_ref, left_ref, base_in, mom_in, coef_ref, base_ref, base, mom, sem):
     loads = [
         pltpu.make_async_copy(src, dst, sem.at[i])
@@ -288,7 +294,9 @@
 
 
 def finish(at_ref, low_ref, high_ref, *refs):
-    slices, refs = refs[: 2 * NH], refs[2 * NH :]
+    n = 2 * PART
+    slices, joined, refs = refs[: NH + 1], refs[NH + 1], refs[NH + 2 :]
+    slices += tuple(joined.at[i * n : (i + 1) * n] for i in range(NH - 1))
     wt_ref = refs[-1]
     for i, ref in enumerate(slices):
         core = at_ref[0] if i < NH else 1 - at_ref[0]
@@ -417,11 +425,12 @@
     )(at, gram, swap(gram), left, in_hbm(base), in_hbm(momentum))
     mine, *sends = call(pair_up, [shape(2 * PART, 128)] * NH, [VMEM] * 2)(send, other_parity)
     *got, coef = lax.optimization_barrier((*ring(sends, "h"), coef))
-    slices = [mine, *got, swap(mine)] + [swap(x) for x in got]
+    joined = call(join, shape(2 * PART * (NH - 1), 128), [VMEM] * (NH - 1))(*got)
+    slices = [mine, *got, swap(mine), swap(joined)]
     new_base, new_error, new_momentum = pl.pallas_call(
         finish,
         out_shape=[whole] * 3,
-        in_specs=[SMEM] * 3 + [VMEM] * (2 * NH + 4) + [HBM],
+        in_specs=[SMEM] * 3 + [VMEM] * (NH + 6) + [HBM],
         out_specs=[HBM] * 3,
         scratch_shapes=[big] * 4 + [pltpu.SemaphoreType.DMA((4,)), pltpu.SemaphoreType.DMA((3, 4))]
         + [pltpu.VMEM((NZ, RANK, SLICE), F32)],

time: 104 us -> 104 us (level)
    ppermute x9 -> x7, starting transfers between devices: 13.2 us -> 12.8 us  [swap(): return lax.ppermute(x, 'c', SWAP)]
    ppermute x9 -> x7, waiting for transfers between devices: 3.14 us -> 3.14 us  [swap(): return lax.ppermute(x, 'c', SWAP)]
  transfers between devices with their start and end apart: 23 -> 21, of which waited for: 16 -> 13; matrix products, arithmetic and copies ran while one was open for 0% -> 0% of each run, Pallas kernels for 7% -> 7%
where the time goes in v11:
time: 104 us
  starting transfers between devices  40.9 us (39%)
  blocking collectives  28.3 us (27%)
  waiting for transfers between devices  19 us (18%)
  Pallas kernels  14.4 us (14%)
    all_to_all x2, blocking collectives, exchange(): return lax.all_to_all(operand, axes, 0, 0, tiled=True)  28.3 us
    ppermute x9, starting transfers between devices, ring(): lax.ppermute(sends[k - 1], axis, [(i, (i + k) % 4) for i in range(4)])  20.3 us
    ppermute x7, starting transfers between devices, swap(): return lax.ppermute(x, 'c', SWAP)  12.8 us
    ppermute x9, waiting for transfers between devices, ring(): lax.ppermute(sends[k - 1], axis, [(i, (i + k) % 4) for i in range(4)])  10.7 us
    ppermute x1, starting transfers between devices, body(): second = lax.ppermute(second, Z, PAIRS[1])  4.55 us
    pallas_call x1, Pallas kernels, body(): call(coefficients, [jax.ShapeDtypeStruct((ROWS, 3 * RANK), jnp.bfloat16),...  3.54 us
    ppermute x7, waiting for transfers between devices, swap(): return lax.ppermute(x, 'c', SWAP)  3.14 us
    ppermute x1, waiting for transfers between devices, body(): second = lax.ppermute(second, Z, PAIRS[1])  3.11 us
  transfers between devices with their start and end apart: 21, of which 13 were waited for; matrix products, arithmetic and copies ran while one was open for 0% of the time, Pallas kernels for 7%

profile of v11, /device:TPU:1, one launch (start us, length us, event | category | flops | bytes accessed | tf_op | source)
XLA Modules:
  0.0 103.5 jit_solution(15642305119075912419)
XLA Ops:
  0.6 1.5 %shard_map.77.refs_8_ = f32[160,1024]{1,0:T(8,128)S(1)} custom-call(s32[1]{0:T(128)} %bitcast.at_ref, f32[320,1024]{1,0:T(8,128)} %base_in.5, bf16[1,320,1024]{2,1,0:T(8,128)(2,1)} %local_in.3, f32[1,320,1024]{2,1,0:T(8,128)} %error_in.3), custom_call_target="tpu_custom_call" | custom-call | flops 1000000 | bytes 1048576 | tf_op jit(solution)/shard_map/pallas_call | solution.py:377
  2.1 3.3 %collective-permute-start = (f32[160,1024]{1,0:T(8,128)S(1)}, f32[160,1024]{1,0:T(8,128)S(1)}, u32[]{:S(2)}, u32[]{:S(2)}) collective-permute-start(f32[160,1024]{1,0:T(8,128)S(1)} %shard_map.77.refs_8_), channel_id=1, source_target_pairs={{0,16},{16,0},{1,17},{17,1},{2,18},{18,2},{3,19},{19,3},{4,20},{20... | collective-permute-start | bytes 1966088 | tf_op jit(solution)/shard_map/ppermute | solution.py:368
  5.5 1.5 %shard_map.76.mine_ref.refs_7_ = f32[160,1024]{1,0:T(8,128)S(1)} custom-call(s32[1]{0:T(128)} %bitcast.at_ref, f32[320,1024]{1,0:T(8,128)} %base_in.5, bf16[1,320,1024]{2,1,0:T(8,128)(2,1)} %local_in.3, f32[1,320,1024]{2,1,0:T(8,128)} %error_in.3), custom_call_target="tpu_custom_call" | custom-call | flops 1000000 | bytes 1048576 | tf_op jit(solution)/shard_map/pallas_call | solution.py:377
  7.9 4.6 %collective-permute-start.2 = (f32[360,128]{1,0:T(8,128)S(1)}, f32[360,128]{1,0:T(8,128)S(1)}, u32[]{:S(2)}, u32[]{:S(2)}) collective-permute-start(f32[360,128]{1,0:T(8,128)S(1)} %get-tuple-element.39), channel_id=1, source_target_pairs={{0,224},{32,64},{64,32},{96,128},{128,96},{160,192},{192,160},{224... | collective-permute-start | bytes 552968 | tf_op jit(solution)/shard_map/ppermute | solution.py:391
  13.7 3.1 %collective-permute-done.2.second_ref = f32[360,128]{1,0:T(8,128)S(1)} collective-permute-done((f32[360,128]{1,0:T(8,128)S(1)}, f32[360,128]{1,0:T(8,128)S(1)}, u32[]{:S(2)}, u32[]{:S(2)}) %collective-permute-start.2) | collective-permute-done | bytes 184352 | tf_op jit(solution)/shard_map/ppermute | solution.py:391
  16.9 3.8 %collective-permute-start.3 = (f32[240,128]{1,0:T(8,128)S(1)}, f32[240,128]{1,0:T(8,128)S(1)}, u32[]{:S(2)}, u32[]{:S(2)}) collective-permute-start(f32[240,128]{1,0:T(8,128)S(1)} %get-tuple-element.41), channel_id=1, source_target_pairs={{0,128},{64,192},{128,0},{192,64},{1,129},{65,193},{129,1},{193,65... | collective-permute-start | bytes 368648 | tf_op jit(solution)/shard_map/ppermute | solution.py:364
  20.7 3.6 %collective-permute-start.5 = (f32[240,128]{1,0:T(8,128)S(1)}, f32[240,128]{1,0:T(8,128)S(1)}, u32[]{:S(2)}, u32[]{:S(2)}) collective-permute-start(f32[240,128]{1,0:T(8,128)S(1)} %get-tuple-element.43), channel_id=1, source_target_pairs={{0,192},{64,0},{128,64},{192,128},{1,193},{65,1},{129,65},{193,129... | collective-permute-start | bytes 368648 | tf_op jit(solution)/shard_map/ppermute | solution.py:364
  24.8 3.2 %collective-permute-done.4.refs_2_ = f32[240,128]{1,0:T(8,128)S(1)} collective-permute-done((f32[240,128]{1,0:T(8,128)S(1)}, f32[240,128]{1,0:T(8,128)S(1)}, u32[]{:S(2)}, u32[]{:S(2)}) %collective-permute-start.4) | collective-permute-done | bytes 122912 | tf_op jit(solution)/shard_map/ppermute | solution.py:364
  28.0 4.7 %collective-permute-done.5.refs_3_ = f32[240,128]{1,0:T(8,128)S(1)} collective-permute-done((f32[240,128]{1,0:T(8,128)S(1)}, f32[240,128]{1,0:T(8,128)S(1)}, u32[]{:S(2)}, u32[]{:S(2)}) %collective-permute-start.5) | collective-permute-done | bytes 122912 | tf_op jit(solution)/shard_map/ppermute | solution.py:364
  35.1 15.8 %all_to_all.10.got_ref = f32[16,48,128]{2,1,0:T(8,128)S(1)} all-to-all(f32[16,48,128]{2,1,0:T(8,128)S(1)} %get-tuple-element.44), channel_id=1, replica_groups=mesh['h'=4,'l'=2,'c'=2,'x'=4,'y'=4] {'x','y'}, dimensions={0} | all-to-all | bytes 786432 | tf_op jit(solution)/shard_map/all_to_all | solution.py:352
  51.2 1.6 %collective-permute-start.9 = (f32[16,128]{1,0:T(8,128)S(1)}, f32[16,128]{1,0:T(8,128)S(1)}, u32[]{:S(2)}, u32[]{:S(2)}) collective-permute-start(f32[16,128]{1,0:T(8,128)S(1)} %get-tuple-element.47.mine_ref), channel_id=1, source_target_pairs={{0,16},{16,0},{1,17},{17,1},{2,18},{18,2},{3,19},{19,3},{4,20},{20... | collective-permute-start | bytes 24584 | tf_op jit(solution)/shard_map/ppermute | solution.py:368
  52.8 1.7 %collective-permute-start.8 = (f32[40,128]{1,0:T(8,128)S(1)}, f32[40,128]{1,0:T(8,128)S(1)}, u32[]{:S(2)}, u32[]{:S(2)}) collective-permute-start(f32[40,128]{1,0:T(8,128)S(1)} %get-tuple-element.69), channel_id=1, source_target_pairs={{0,224},{32,64},{64,32},{96,128},{128,96},{160,192},{192,160},{224... | collective-permute-start | bytes 61448 | tf_op jit(solution)/shard_map/ppermute | solution.py:406
  54.5 2.1 %shard_map.83.inv_ref = f32[64,64]{1,0:T(8,128)S(1)} custom-call(s32[1]{0:T(128)} %bitcast.at_ref, f32[16,128]{1,0:T(8,128)S(1)} %get-tuple-element.47.mine_ref, f32[16,128]{1,0:T(8,128)S(1)} %collective-permute-done.9.theirs_ref), custom_call_target="tpu_custom_call" | custom-call | flops 1000000000 | bytes 1048576 | tf_op jit(solution)/shard_map/pallas_call | solution.py:407
  57.4 3.3 %collective-permute-start.10 = (f32[80,128]{1,0:T(8,128)S(1)}, f32[80,128]{1,0:T(8,128)S(1)}, u32[]{:S(2)}, u32[]{:S(2)}) collective-permute-start(f32[80,128]{1,0:T(8,128)S(1)} %get-tuple-element.49), channel_id=1, source_target_pairs={{0,128},{64,192},{128,0},{192,64},{1,129},{65,193},{129,1},{193,65... | collective-permute-start | bytes 122888 | tf_op jit(solution)/shard_map/ppermute | solution.py:364
  61.3 3.1 %collective-permute-start.12 = (f32[80,128]{1,0:T(8,128)S(1)}, f32[80,128]{1,0:T(8,128)S(1)}, u32[]{:S(2)}, u32[]{:S(2)}) collective-permute-start(f32[80,128]{1,0:T(8,128)S(1)} %get-tuple-element.51), channel_id=1, source_target_pairs={{0,192},{64,0},{128,64},{192,128},{1,193},{65,1},{129,65},{193,129... | collective-permute-start | bytes 122888 | tf_op jit(solution)/shard_map/ppermute | solution.py:364
  64.3 1.7 %collective-permute-done.11.one_ref = f32[80,128]{1,0:T(8,128)S(1)} collective-permute-done((f32[80,128]{1,0:T(8,128)S(1)}, f32[80,128]{1,0:T(8,128)S(1)}, u32[]{:S(2)}, u32[]{:S(2)}) %collective-permute-start.11) | collective-permute-done | bytes 40992 | tf_op jit(solution)/shard_map/ppermute | solution.py:364
  66.6 1.8 %collective-permute-start.13 = (f32[80,128]{1,0:T(8,128)S(1)}, f32[80,128]{1,0:T(8,128)S(1)}, u32[]{:S(2)}, u32[]{:S(2)}) collective-permute-start(f32[80,128]{1,0:T(8,128)S(1)} %shard_map.85.mine_ref), channel_id=1, source_target_pairs={{0,16},{16,0},{1,17},{17,1},{2,18},{18,2},{3,19},{19,3},{4,20},{20... | collective-permute-start | bytes 122888 | tf_op jit(solution)/shard_map/ppermute | solution.py:368
  70.0 12.5 %all_to_all.11.got_ref = f32[16,48,128]{2,1,0:T(8,128)S(1)} all-to-all(f32[16,48,128]{2,1,0:T(8,128)S(1)} %get-tuple-element.52), channel_id=1, replica_groups=mesh['h'=4,'l'=2,'c'=2,'x'=4,'y'=4] {'x','y'}, dimensions={0} | all-to-all | bytes 786432 | tf_op jit(solution)/shard_map/all_to_all | solution.py:352
  84.0 1.8 %collective-permute-start.18 = (f32[16,128]{1,0:T(8,128)S(1)}, f32[16,128]{1,0:T(8,128)S(1)}, u32[]{:S(2)}, u32[]{:S(2)}) collective-permute-start(f32[16,128]{1,0:T(8,128)S(1)} %get-tuple-element.58.mine_ref), channel_id=1, source_target_pairs={{0,16},{16,0},{1,17},{17,1},{2,18},{18,2},{3,19},{19,3},{4,20},{20... | collective-permute-start | bytes 24584 | tf_op jit(solution)/shard_map/ppermute | solution.py:368
  85.8 2.4 %collective-permute-start.15 = (f32[64,128]{1,0:T(8,128)S(1)}, f32[64,128]{1,0:T(8,128)S(1)}, u32[]{:S(2)}, u32[]{:S(2)}) collective-permute-start(f32[64,128]{1,0:T(8,128)S(1)} %get-tuple-element.55), channel_id=1, source_target_pairs={{0,128},{64,192},{128,0},{192,64},{1,129},{65,193},{129,1},{193,65... | collective-permute-start | bytes 98312 | tf_op jit(solution)/shard_map/ppermute | solution.py:364
  88.2 3.3 %collective-permute-start.16 = (f32[64,128]{1,0:T(8,128)S(1)}, f32[64,128]{1,0:T(8,128)S(1)}, u32[]{:S(2)}, u32[]{:S(2)}) collective-permute-start(f32[64,128]{1,0:T(8,128)S(1)} %get-tuple-element.56), channel_id=1, source_target_pairs={{0,64},{64,128},{128,192},{192,0},{1,65},{65,129},{129,193},{193,1... | collective-permute-start | bytes 98312 | tf_op jit(solution)/shard_map/ppermute | solution.py:364
  91.9 3.5 %shard_map.89 = (bf16[320,192]{1,0:T(8,128)(2,1)S(1)}, f32[320,1024]{1,0:T(8,128)S(1)}) custom-call(s32[1]{0:T(128)} %bitcast.at_ref, f32[16,128]{1,0:T(8,128)S(1)} %get-tuple-element.58.mine_ref, f32[16,128]{1,0:T(8,128)S(1)} %collective-permute-done.18.theirs_ref, f32[64,320]{1,0:T(8,128)S(1)} %get-tuple-element.59.left_ref, f32[320,1024]{1,0:T(8,128)} %base_in.5, ...), custom_call_target="tpu_custom_call" | custom-call | flops 1000000000 | bytes 1048576 | tf_op jit(solution)/shard_map/pallas_call | solution.py:419
  95.5 3.6 %collective-permute-start.20 = (f32[192,128]{1,0:T(8,128)S(1)}, f32[192,128]{1,0:T(8,128)S(1)}, u32[]{:S(2)}, u32[]{:S(2)}) collective-permute-start(f32[192,128]{1,0:T(8,128)S(1)} %shard_map.90), channel_id=1, source_target_pairs={{0,16},{16,0},{1,17},{17,1},{2,18},{18,2},{3,19},{19,3},{4,20},{20... | collective-permute-start | bytes 294920 | tf_op jit(solution)/shard_map/ppermute | solution.py:368
  100.4 3.0 %shard_map.91 = (f32[320,1024]{1,0:T(8,128)}, f32[320,1024]{1,0:T(8,128)}, f32[320,1024]{1,0:T(8,128)}) custom-call(s32[1]{0:T(128)} %bitcast.at_ref, s32[1]{0:T(128)} %bitcast.1.low_ref, s32[1]{0:T(128)} %bitcast.2.high_ref, f32[64,128]{1,0:T(8,128)S(1)} %get-tuple-element.54.refs_0_, f32[64,128]{1,0:T(8,128)S(1)} %collective-permute-done.15.refs_0_.refs_1_, ...), custom_call_target="tpu_custom_call" | custom-call | tf_op jit(solution)/shard_map/pallas_call | solution.py:430
  (39 shorter events, 12.2 us)
Async XLA Ops:
  2.1 5.1 %collective-permute-start = (f32[160,1024]{1,0:T(8,128)S(1)}, f32[160,1024]{1,0:T(8,128)S(1)}, u32[]{:S(2)}, u32[]{:S(2)}) collective-permute-start(f32[160,1024]{1,0:T(8,128)S(1)} %shard_map.77.refs_8_), channel_id=1, source_target_pairs={{0,16},{16,0},{1,17},{17,1},{2,18},{18,2},{3,19},{19,3},{4,20},{20... | collective-permute-start | bytes 1966088 | tf_op jit(solution)/shard_map/ppermute | solution.py:368
  5.5 1.7 %copy-start = (f32[1024,64]{0,1:T(8,128)S(1)}, f32[1024,64]{0,1:T(8,128)}, u32[]{:S(2)}) copy-start(f32[1024,64]{0,1:T(8,128)} %param.9) | copy-start | bytes 786436
  7.8 5.9 %collective-permute-start.1 = (f32[360,128]{1,0:T(8,128)S(1)}, f32[360,128]{1,0:T(8,128)S(1)}, u32[]{:S(2)}, u32[]{:S(2)}) collective-permute-start(f32[360,128]{1,0:T(8,128)S(1)} %get-tuple-element.38), channel_id=1, source_target_pairs={{0,32},{32,0},{64,96},{96,64},{128,160},{160,128},{192,224},{224,1... | collective-permute-start | bytes 552968 | tf_op jit(solution)/shard_map/ppermute | solution.py:390
  7.9 8.9 %collective-permute-start.2 = (f32[360,128]{1,0:T(8,128)S(1)}, f32[360,128]{1,0:T(8,128)S(1)}, u32[]{:S(2)}, u32[]{:S(2)}) collective-permute-start(f32[360,128]{1,0:T(8,128)S(1)} %get-tuple-element.39), channel_id=1, source_target_pairs={{0,224},{32,64},{64,32},{96,128},{128,96},{160,192},{192,160},{224... | collective-permute-start | bytes 552968 | tf_op jit(solution)/shard_map/ppermute | solution.py:391
  16.9 7.9 %collective-permute-start.3 = (f32[240,128]{1,0:T(8,128)S(1)}, f32[240,128]{1,0:T(8,128)S(1)}, u32[]{:S(2)}, u32[]{:S(2)}) collective-permute-start(f32[240,128]{1,0:T(8,128)S(1)} %get-tuple-element.41), channel_id=1, source_target_pairs={{0,128},{64,192},{128,0},{192,64},{1,129},{65,193},{129,1},{193,65... | collective-permute-start | bytes 368648 | tf_op jit(solution)/shard_map/ppermute | solution.py:364
  20.7 7.4 %collective-permute-start.4 = (f32[240,128]{1,0:T(8,128)S(1)}, f32[240,128]{1,0:T(8,128)S(1)}, u32[]{:S(2)}, u32[]{:S(2)}) collective-permute-start(f32[240,128]{1,0:T(8,128)S(1)} %get-tuple-element.42), channel_id=1, source_target_pairs={{0,64},{64,128},{128,192},{192,0},{1,65},{65,129},{129,193},{193,1... | collective-permute-start | bytes 368648 | tf_op jit(solution)/shard_map/ppermute | solution.py:364
  20.7 12.0 %collective-permute-start.5 = (f32[240,128]{1,0:T(8,128)S(1)}, f32[240,128]{1,0:T(8,128)S(1)}, u32[]{:S(2)}, u32[]{:S(2)}) collective-permute-start(f32[240,128]{1,0:T(8,128)S(1)} %get-tuple-element.43), channel_id=1, source_target_pairs={{0,192},{64,0},{128,64},{192,128},{1,193},{65,1},{129,65},{193,129... | collective-permute-start | bytes 368648 | tf_op jit(solution)/shard_map/ppermute | solution.py:364
  32.7 1.6 %collective-permute-start.6 = (f32[240,128]{1,0:T(8,128)S(1)}, f32[240,128]{1,0:T(8,128)S(1)}, u32[]{:S(2)}, u32[]{:S(2)}) collective-permute-start(f32[240,128]{1,0:T(8,128)S(1)} %shard_map.80.mine_ref), channel_id=1, source_target_pairs={{0,16},{16,0},{1,17},{17,1},{2,18},{18,2},{3,19},{19,3},{4,20},{20... | collective-permute-start | bytes 368648 | tf_op jit(solution)/shard_map/ppermute | solution.py:368
  51.2 3.3 %collective-permute-start.9 = (f32[16,128]{1,0:T(8,128)S(1)}, f32[16,128]{1,0:T(8,128)S(1)}, u32[]{:S(2)}, u32[]{:S(2)}) collective-permute-start(f32[16,128]{1,0:T(8,128)S(1)} %get-tuple-element.47.mine_ref), channel_id=1, source_target_pairs={{0,16},{16,0},{1,17},{17,1},{2,18},{18,2},{3,19},{19,3},{4,20},{20... | collective-permute-start | bytes 24584 | tf_op jit(solution)/shard_map/ppermute | solution.py:368
  52.8 3.9 %collective-permute-start.8 = (f32[40,128]{1,0:T(8,128)S(1)}, f32[40,128]{1,0:T(8,128)S(1)}, u32[]{:S(2)}, u32[]{:S(2)}) collective-permute-start(f32[40,128]{1,0:T(8,128)S(1)} %get-tuple-element.69), channel_id=1, source_target_pairs={{0,224},{32,64},{64,32},{96,128},{128,96},{160,192},{192,160},{224... | collective-permute-start | bytes 61448 | tf_op jit(solution)/shard_map/ppermute | solution.py:406
  54.5 2.9 %collective-permute-start.7 = (f32[40,128]{1,0:T(8,128)S(1)}, f32[40,128]{1,0:T(8,128)S(1)}, u32[]{:S(2)}, u32[]{:S(2)}) collective-permute-start(f32[40,128]{1,0:T(8,128)S(1)} %get-tuple-element.70), channel_id=1, source_target_pairs={{0,32},{32,0},{64,96},{96,64},{128,160},{160,128},{192,224},{224,1... | collective-permute-start | bytes 61448 | tf_op jit(solution)/shard_map/ppermute | solution.py:406
  57.4 6.9 %collective-permute-start.10 = (f32[80,128]{1,0:T(8,128)S(1)}, f32[80,128]{1,0:T(8,128)S(1)}, u32[]{:S(2)}, u32[]{:S(2)}) collective-permute-start(f32[80,128]{1,0:T(8,128)S(1)} %get-tuple-element.49), channel_id=1, source_target_pairs={{0,128},{64,192},{128,0},{192,64},{1,129},{65,193},{129,1},{193,65... | collective-permute-start | bytes 122888 | tf_op jit(solution)/shard_map/ppermute | solution.py:364
  60.8 5.3 %collective-permute-start.11 = (f32[80,128]{1,0:T(8,128)S(1)}, f32[80,128]{1,0:T(8,128)S(1)}, u32[]{:S(2)}, u32[]{:S(2)}) collective-permute-start(f32[80,128]{1,0:T(8,128)S(1)} %get-tuple-element.50), channel_id=1, source_target_pairs={{0,64},{64,128},{128,192},{192,0},{1,65},{65,129},{129,193},{193,1... | collective-permute-start | bytes 122888 | tf_op jit(solution)/shard_map/ppermute | solution.py:364
  61.3 5.3 %collective-permute-start.12 = (f32[80,128]{1,0:T(8,128)S(1)}, f32[80,128]{1,0:T(8,128)S(1)}, u32[]{:S(2)}, u32[]{:S(2)}) collective-permute-start(f32[80,128]{1,0:T(8,128)S(1)} %get-tuple-element.51), channel_id=1, source_target_pairs={{0,192},{64,0},{128,64},{192,128},{1,193},{65,1},{129,65},{193,129... | collective-permute-start | bytes 122888 | tf_op jit(solution)/shard_map/ppermute | solution.py:364
  66.6 2.6 %collective-permute-start.13 = (f32[80,128]{1,0:T(8,128)S(1)}, f32[80,128]{1,0:T(8,128)S(1)}, u32[]{:S(2)}, u32[]{:S(2)}) collective-permute-start(f32[80,128]{1,0:T(8,128)S(1)} %shard_map.85.mine_ref), channel_id=1, source_target_pairs={{0,16},{16,0},{1,17},{17,1},{2,18},{18,2},{3,19},{19,3},{4,20},{20... | collective-permute-start | bytes 122888 | tf_op jit(solution)/shard_map/ppermute | solution.py:368
  82.5 3.3 %collective-permute-start.14 = (f32[32,128]{1,0:T(8,128)S(1)}, f32[32,128]{1,0:T(8,128)S(1)}, u32[]{:S(2)}, u32[]{:S(2)}) collective-permute-start(f32[32,128]{1,0:T(8,128)S(1)} %get-tuple-element.53.own_ref), channel_id=1, source_target_pairs={{0,32},{32,0},{64,96},{96,64},{128,160},{160,128},{192,224},{224,1... | collective-permute-start | bytes 49160 | tf_op jit(solution)/shard_map/ppermute | solution.py:416
  84.0 7.9 %collective-permute-start.18 = (f32[16,128]{1,0:T(8,128)S(1)}, f32[16,128]{1,0:T(8,128)S(1)}, u32[]{:S(2)}, u32[]{:S(2)}) collective-permute-start(f32[16,128]{1,0:T(8,128)S(1)} %get-tuple-element.58.mine_ref), channel_id=1, source_target_pairs={{0,16},{16,0},{1,17},{17,1},{2,18},{18,2},{3,19},{19,3},{4,20},{20... | collective-permute-start | bytes 24584 | tf_op jit(solution)/shard_map/ppermute | solution.py:368
  85.8 9.6 %collective-permute-start.15 = (f32[64,128]{1,0:T(8,128)S(1)}, f32[64,128]{1,0:T(8,128)S(1)}, u32[]{:S(2)}, u32[]{:S(2)}) collective-permute-start(f32[64,128]{1,0:T(8,128)S(1)} %get-tuple-element.55), channel_id=1, source_target_pairs={{0,128},{64,192},{128,0},{192,64},{1,129},{65,193},{129,1},{193,65... | collective-permute-start | bytes 98312 | tf_op jit(solution)/shard_map/ppermute | solution.py:364
  88.2 7.3 %collective-permute-start.16 = (f32[64,128]{1,0:T(8,128)S(1)}, f32[64,128]{1,0:T(8,128)S(1)}, u32[]{:S(2)}, u32[]{:S(2)}) collective-permute-start(f32[64,128]{1,0:T(8,128)S(1)} %get-tuple-element.56), channel_id=1, source_target_pairs={{0,64},{64,128},{128,192},{192,0},{1,65},{65,129},{129,193},{193,1... | collective-permute-start | bytes 98312 | tf_op jit(solution)/shard_map/ppermute | solution.py:364
  91.6 4.0 %collective-permute-start.17 = (f32[64,128]{1,0:T(8,128)S(1)}, f32[64,128]{1,0:T(8,128)S(1)}, u32[]{:S(2)}, u32[]{:S(2)}) collective-permute-start(f32[64,128]{1,0:T(8,128)S(1)} %get-tuple-element.57), channel_id=1, source_target_pairs={{0,192},{64,0},{128,64},{192,128},{1,193},{65,1},{129,65},{193,129... | collective-permute-start | bytes 98312 | tf_op jit(solution)/shard_map/ppermute | solution.py:364
  95.5 4.8 %collective-permute-start.20 = (f32[192,128]{1,0:T(8,128)S(1)}, f32[192,128]{1,0:T(8,128)S(1)}, u32[]{:S(2)}, u32[]{:S(2)}) collective-permute-start(f32[192,128]{1,0:T(8,128)S(1)} %shard_map.90), channel_id=1, source_target_pairs={{0,16},{16,0},{1,17},{17,1},{2,18},{18,2},{3,19},{19,3},{4,20},{20... | collective-permute-start | bytes 294920 | tf_op jit(solution)/shard_map/ppermute | solution.py:368
  99.1 1.2 %collective-permute-start.19 = (f32[64,128]{1,0:T(8,128)S(1)}, f32[64,128]{1,0:T(8,128)S(1)}, u32[]{:S(2)}, u32[]{:S(2)}) collective-permute-start(f32[64,128]{1,0:T(8,128)S(1)} %get-tuple-element.54.refs_0_), channel_id=1, source_target_pairs={{0,16},{16,0},{1,17},{17,1},{2,18},{18,2},{3,19},{19,3},{4,20},{20... | collective-permute-start | bytes 98312 | tf_op jit(solution)/shard_map/ppermute | solution.py:368

commit v12 on v11

--- a/solution.py
+++ b/solution.py
@@ -311,7 +311,7 @@
 def write_outputs(at_ref, coef_ref, own, other, base, mom_in, base_out, err_out, mom_out,
            mom, nbase, nerr, nmom, in_sem, out_sem, wt_ref):
     c = at_ref[0]
-    part = HALF // 2
+    part = HALF // 5
     count = ROWS // part
     at = [i * part if i < count // 2 else (i - count // 2) * part for i in range(count)]
     here = [pl.ds(i * part, part) for i in range(count)]
@@ -432,7 +432,7 @@
         out_shape=[whole] * 3,
         in_specs=[SMEM] * 3 + [VMEM] * (NH + 6) + [HBM],
         out_specs=[HBM] * 3,
-        scratch_shapes=[big] * 4 + [pltpu.SemaphoreType.DMA((4,)), pltpu.SemaphoreType.DMA((3, 4))]
+        scratch_shapes=[big] * 4 + [pltpu.SemaphoreType.DMA((10,)), pltpu.SemaphoreType.DMA((3, 10))]
         + [pltpu.VMEM((NZ, RANK, SLICE), F32)],
         compiler_params=pltpu.CompilerParams(vmem_limit_bytes=16 * 2**20),
     )(at, low, high, *slices, coef, in_vmem(own), in_vmem(other), in_vmem(partial_base), in_hbm(momentum))

time: 104 us -> 104 us (level)
  no operation moved by 1% of the time
where the time goes in v12:
time: 104 us
  starting transfers between devices  40.9 us (39%)
  blocking collectives  28.3 us (27%)
  waiting for transfers between devices  19 us (18%)
  Pallas kernels  15.1 us (15%)
    all_to_all x2, blocking collectives, exchange(): return lax.all_to_all(operand, axes, 0, 0, tiled=True)  28.3 us
    ppermute x9, starting transfers between devices, ring(): lax.ppermute(sends[k - 1], axis, [(i, (i + k) % 4) for i in range(4)])  20.3 us
    ppermute x7, starting transfers between devices, swap(): return lax.ppermute(x, 'c', SWAP)  12.8 us
    ppermute x9, waiting for transfers between devices, ring(): lax.ppermute(sends[k - 1], axis, [(i, (i + k) % 4) for i in range(4)])  10.7 us
    ppermute x1, starting transfers between devices, body(): second = lax.ppermute(second, Z, PAIRS[1])  4.55 us
    pallas_call x1, Pallas kernels, body(): pl.pallas_call(finish, out_shape=[whole] * 3, in_specs=[SMEM] * 3 + [VMEM...  3.71 us
    pallas_call x1, Pallas kernels, body(): call(coefficients, [jax.ShapeDtypeStruct((ROWS, 3 * RANK), jnp.bfloat16),...  3.54 us
    ppermute x7, waiting for transfers between devices, swap(): return lax.ppermute(x, 'c', SWAP)  3.14 us
  transfers between devices with their start and end apart: 21, of which 13 were waited for; matrix products, arithmetic and copies ran while one was open for 0% of the time, Pallas kernels for 7%

profile of v12, /device:TPU:1, one launch (start us, length us, event | category | flops | bytes accessed | tf_op | source)
XLA Modules:
  0.0 104.2 jit_solution(8739367898092308050)
XLA Ops:
  0.6 1.5 %shard_map.77.refs_8_ = f32[160,1024]{1,0:T(8,128)S(1)} custom-call(s32[1]{0:T(128)} %bitcast.at_ref, f32[320,1024]{1,0:T(8,128)} %base_in.5, bf16[1,320,1024]{2,1,0:T(8,128)(2,1)} %local_in.3, f32[1,320,1024]{2,1,0:T(8,128)} %error_in.3), custom_call_target="tpu_custom_call" | custom-call | flops 1000000 | bytes 1048576 | tf_op jit(solution)/shard_map/pallas_call | solution.py:377
  2.1 3.3 %collective-permute-start = (f32[160,1024]{1,0:T(8,128)S(1)}, f32[160,1024]{1,0:T(8,128)S(1)}, u32[]{:S(2)}, u32[]{:S(2)}) collective-permute-start(f32[160,1024]{1,0:T(8,128)S(1)} %shard_map.77.refs_8_), channel_id=1, source_target_pairs={{0,16},{16,0},{1,17},{17,1},{2,18},{18,2},{3,19},{19,3},{4,20},{20... | collective-permute-start | bytes 1966088 | tf_op jit(solution)/shard_map/ppermute | solution.py:368
  5.5 1.5 %shard_map.76.mine_ref.refs_7_ = f32[160,1024]{1,0:T(8,128)S(1)} custom-call(s32[1]{0:T(128)} %bitcast.at_ref, f32[320,1024]{1,0:T(8,128)} %base_in.5, bf16[1,320,1024]{2,1,0:T(8,128)(2,1)} %local_in.3, f32[1,320,1024]{2,1,0:T(8,128)} %error_in.3), custom_call_target="tpu_custom_call" | custom-call | flops 1000000 | bytes 1048576 | tf_op jit(solution)/shard_map/pallas_call | solution.py:377
  7.9 4.6 %collective-permute-start.2 = (f32[360,128]{1,0:T(8,128)S(1)}, f32[360,128]{1,0:T(8,128)S(1)}, u32[]{:S(2)}, u32[]{:S(2)}) collective-permute-start(f32[360,128]{1,0:T(8,128)S(1)} %get-tuple-element.39), channel_id=1, source_target_pairs={{0,224},{32,64},{64,32},{96,128},{128,96},{160,192},{192,160},{224... | collective-permute-start | bytes 552968 | tf_op jit(solution)/shard_map/ppermute | solution.py:391
  13.7 3.1 %collective-permute-done.2.second_ref = f32[360,128]{1,0:T(8,128)S(1)} collective-permute-done((f32[360,128]{1,0:T(8,128)S(1)}, f32[360,128]{1,0:T(8,128)S(1)}, u32[]{:S(2)}, u32[]{:S(2)}) %collective-permute-start.2) | collective-permute-done | bytes 184352 | tf_op jit(solution)/shard_map/ppermute | solution.py:391
  16.9 3.8 %collective-permute-start.3 = (f32[240,128]{1,0:T(8,128)S(1)}, f32[240,128]{1,0:T(8,128)S(1)}, u32[]{:S(2)}, u32[]{:S(2)}) collective-permute-start(f32[240,128]{1,0:T(8,128)S(1)} %get-tuple-element.41), channel_id=1, source_target_pairs={{0,128},{64,192},{128,0},{192,64},{1,129},{65,193},{129,1},{193,65... | collective-permute-start | bytes 368648 | tf_op jit(solution)/shard_map/ppermute | solution.py:364
  20.7 3.6 %collective-permute-start.5 = (f32[240,128]{1,0:T(8,128)S(1)}, f32[240,128]{1,0:T(8,128)S(1)}, u32[]{:S(2)}, u32[]{:S(2)}) collective-permute-start(f32[240,128]{1,0:T(8,128)S(1)} %get-tuple-element.43), channel_id=1, source_target_pairs={{0,192},{64,0},{128,64},{192,128},{1,193},{65,1},{129,65},{193,129... | collective-permute-start | bytes 368648 | tf_op jit(solution)/shard_map/ppermute | solution.py:364
  24.8 3.2 %collective-permute-done.4.refs_2_ = f32[240,128]{1,0:T(8,128)S(1)} collective-permute-done((f32[240,128]{1,0:T(8,128)S(1)}, f32[240,128]{1,0:T(8,128)S(1)}, u32[]{:S(2)}, u32[]{:S(2)}) %collective-permute-start.4) | collective-permute-done | bytes 122912 | tf_op jit(solution)/shard_map/ppermute | solution.py:364
  28.0 4.7 %collective-permute-done.5.refs_3_ = f32[240,128]{1,0:T(8,128)S(1)} collective-permute-done((f32[240,128]{1,0:T(8,128)S(1)}, f32[240,128]{1,0:T(8,128)S(1)}, u32[]{:S(2)}, u32[]{:S(2)}) %collective-permute-start.5) | collective-permute-done | bytes 122912 | tf_op jit(solution)/shard_map/ppermute | solution.py:364
  35.1 15.8 %all_to_all.10.got_ref = f32[16,48,128]{2,1,0:T(8,128)S(1)} all-to-all(f32[16,48,128]{2,1,0:T(8,128)S(1)} %get-tuple-element.44), channel_id=1, replica_groups=mesh['h'=4,'l'=2,'c'=2,'x'=4,'y'=4] {'x','y'}, dimensions={0} | all-to-all | bytes 786432 | tf_op jit(solution)/shard_map/all_to_all | solution.py:352
  51.2 1.6 %collective-permute-start.9 = (f32[16,128]{1,0:T(8,128)S(1)}, f32[16,128]{1,0:T(8,128)S(1)}, u32[]{:S(2)}, u32[]{:S(2)}) collective-permute-start(f32[16,128]{1,0:T(8,128)S(1)} %get-tuple-element.47.mine_ref), channel_id=1, source_target_pairs={{0,16},{16,0},{1,17},{17,1},{2,18},{18,2},{3,19},{19,3},{4,20},{20... | collective-permute-start | bytes 24584 | tf_op jit(solution)/shard_map/ppermute | solution.py:368
  52.8 1.7 %collective-permute-start.8 = (f32[40,128]{1,0:T(8,128)S(1)}, f32[40,128]{1,0:T(8,128)S(1)}, u32[]{:S(2)}, u32[]{:S(2)}) collective-permute-start(f32[40,128]{1,0:T(8,128)S(1)} %get-tuple-element.69), channel_id=1, source_target_pairs={{0,224},{32,64},{64,32},{96,128},{128,96},{160,192},{192,160},{224... | collective-permute-start | bytes 61448 | tf_op jit(solution)/shard_map/ppermute | solution.py:406
  54.5 2.1 %shard_map.83.inv_ref = f32[64,64]{1,0:T(8,128)S(1)} custom-call(s32[1]{0:T(128)} %bitcast.at_ref, f32[16,128]{1,0:T(8,128)S(1)} %get-tuple-element.47.mine_ref, f32[16,128]{1,0:T(8,128)S(1)} %collective-permute-done.9.theirs_ref), custom_call_target="tpu_custom_call" | custom-call | flops 1000000000 | bytes 1048576 | tf_op jit(solution)/shard_map/pallas_call | solution.py:407
  57.4 3.3 %collective-permute-start.10 = (f32[80,128]{1,0:T(8,128)S(1)}, f32[80,128]{1,0:T(8,128)S(1)}, u32[]{:S(2)}, u32[]{:S(2)}) collective-permute-start(f32[80,128]{1,0:T(8,128)S(1)} %get-tuple-element.49), channel_id=1, source_target_pairs={{0,128},{64,192},{128,0},{192,64},{1,129},{65,193},{129,1},{193,65... | collective-permute-start | bytes 122888 | tf_op jit(solution)/shard_map/ppermute | solution.py:364
  61.3 3.1 %collective-permute-start.12 = (f32[80,128]{1,0:T(8,128)S(1)}, f32[80,128]{1,0:T(8,128)S(1)}, u32[]{:S(2)}, u32[]{:S(2)}) collective-permute-start(f32[80,128]{1,0:T(8,128)S(1)} %get-tuple-element.51), channel_id=1, source_target_pairs={{0,192},{64,0},{128,64},{192,128},{1,193},{65,1},{129,65},{193,129... | collective-permute-start | bytes 122888 | tf_op jit(solution)/shard_map/ppermute | solution.py:364
  64.3 1.7 %collective-permute-done.11.one_ref = f32[80,128]{1,0:T(8,128)S(1)} collective-permute-done((f32[80,128]{1,0:T(8,128)S(1)}, f32[80,128]{1,0:T(8,128)S(1)}, u32[]{:S(2)}, u32[]{:S(2)}) %collective-permute-start.11) | collective-permute-done | bytes 40992 | tf_op jit(solution)/shard_map/ppermute | solution.py:364
  66.6 1.8 %collective-permute-start.13 = (f32[80,128]{1,0:T(8,128)S(1)}, f32[80,128]{1,0:T(8,128)S(1)}, u32[]{:S(2)}, u32[]{:S(2)}) collective-permute-start(f32[80,128]{1,0:T(8,128)S(1)} %shard_map.85.mine_ref), channel_id=1, source_target_pairs={{0,16},{16,0},{1,17},{17,1},{2,18},{18,2},{3,19},{19,3},{4,20},{20... | collective-permute-start | bytes 122888 | tf_op jit(solution)/shard_map/ppermute | solution.py:368
  70.0 12.5 %all_to_all.11.got_ref = f32[16,48,128]{2,1,0:T(8,128)S(1)} all-to-all(f32[16,48,128]{2,1,0:T(8,128)S(1)} %get-tuple-element.52), channel_id=1, replica_groups=mesh['h'=4,'l'=2,'c'=2,'x'=4,'y'=4] {'x','y'}, dimensions={0} | all-to-all | bytes 786432 | tf_op jit(solution)/shard_map/all_to_all | solution.py:352
  84.0 1.8 %collective-permute-start.18 = (f32[16,128]{1,0:T(8,128)S(1)}, f32[16,128]{1,0:T(8,128)S(1)}, u32[]{:S(2)}, u32[]{:S(2)}) collective-permute-start(f32[16,128]{1,0:T(8,128)S(1)} %get-tuple-element.58.mine_ref), channel_id=1, source_target_pairs={{0,16},{16,0},{1,17},{17,1},{2,18},{18,2},{3,19},{19,3},{4,20},{20... | collective-permute-start | bytes 24584 | tf_op jit(solution)/shard_map/ppermute | solution.py:368
  85.8 2.4 %collective-permute-start.15 = (f32[64,128]{1,0:T(8,128)S(1)}, f32[64,128]{1,0:T(8,128)S(1)}, u32[]{:S(2)}, u32[]{:S(2)}) collective-permute-start(f32[64,128]{1,0:T(8,128)S(1)} %get-tuple-element.55), channel_id=1, source_target_pairs={{0,128},{64,192},{128,0},{192,64},{1,129},{65,193},{129,1},{193,65... | collective-permute-start | bytes 98312 | tf_op jit(solution)/shard_map/ppermute | solution.py:364
  88.2 3.3 %collective-permute-start.16 = (f32[64,128]{1,0:T(8,128)S(1)}, f32[64,128]{1,0:T(8,128)S(1)}, u32[]{:S(2)}, u32[]{:S(2)}) collective-permute-start(f32[64,128]{1,0:T(8,128)S(1)} %get-tuple-element.56), channel_id=1, source_target_pairs={{0,64},{64,128},{128,192},{192,0},{1,65},{65,129},{129,193},{193,1... | collective-permute-start | bytes 98312 | tf_op jit(solution)/shard_map/ppermute | solution.py:364
  91.9 3.5 %shard_map.89 = (bf16[320,192]{1,0:T(8,128)(2,1)S(1)}, f32[320,1024]{1,0:T(8,128)S(1)}) custom-call(s32[1]{0:T(128)} %bitcast.at_ref, f32[16,128]{1,0:T(8,128)S(1)} %get-tuple-element.58.mine_ref, f32[16,128]{1,0:T(8,128)S(1)} %collective-permute-done.18.theirs_ref, f32[64,320]{1,0:T(8,128)S(1)} %get-tuple-element.59.left_ref, f32[320,1024]{1,0:T(8,128)} %base_in.5, ...), custom_call_target="tpu_custom_call" | custom-call | flops 1000000000 | bytes 1048576 | tf_op jit(solution)/shard_map/pallas_call | solution.py:419
  95.5 3.6 %collective-permute-start.20 = (f32[192,128]{1,0:T(8,128)S(1)}, f32[192,128]{1,0:T(8,128)S(1)}, u32[]{:S(2)}, u32[]{:S(2)}) collective-permute-start(f32[192,128]{1,0:T(8,128)S(1)} %shard_map.90), channel_id=1, source_target_pairs={{0,16},{16,0},{1,17},{17,1},{2,18},{18,2},{3,19},{19,3},{4,20},{20... | collective-permute-start | bytes 294920 | tf_op jit(solution)/shard_map/ppermute | solution.py:368
  100.4 3.7 %shard_map.91 = (f32[320,1024]{1,0:T(8,128)}, f32[320,1024]{1,0:T(8,128)}, f32[320,1024]{1,0:T(8,128)}) custom-call(s32[1]{0:T(128)} %bitcast.at_ref, s32[1]{0:T(128)} %bitcast.1.low_ref, s32[1]{0:T(128)} %bitcast.2.high_ref, f32[64,128]{1,0:T(8,128)S(1)} %get-tuple-element.54.refs_0_, f32[64,128]{1,0:T(8,128)S(1)} %collective-permute-done.15.refs_0_.refs_1_, ...), custom_call_target="tpu_custom_call" | custom-call | tf_op jit(solution)/shard_map/pallas_call | solution.py:430
  (39 shorter events, 12.2 us)
Async XLA Ops:
  2.1 5.1 %collective-permute-start = (f32[160,1024]{1,0:T(8,128)S(1)}, f32[160,1024]{1,0:T(8,128)S(1)}, u32[]{:S(2)}, u32[]{:S(2)}) collective-permute-start(f32[160,1024]{1,0:T(8,128)S(1)} %shard_map.77.refs_8_), channel_id=1, source_target_pairs={{0,16},{16,0},{1,17},{17,1},{2,18},{18,2},{3,19},{19,3},{4,20},{20... | collective-permute-start | bytes 1966088 | tf_op jit(solution)/shard_map/ppermute | solution.py:368
  5.5 1.7 %copy-start = (f32[1024,64]{0,1:T(8,128)S(1)}, f32[1024,64]{0,1:T(8,128)}, u32[]{:S(2)}) copy-start(f32[1024,64]{0,1:T(8,128)} %param.9) | copy-start | bytes 786436
  7.8 5.9 %collective-permute-start.1 = (f32[360,128]{1,0:T(8,128)S(1)}, f32[360,128]{1,0:T(8,128)S(1)}, u32[]{:S(2)}, u32[]{:S(2)}) collective-permute-start(f32[360,128]{1,0:T(8,128)S(1)} %get-tuple-element.38), channel_id=1, source_target_pairs={{0,32},{32,0},{64,96},{96,64},{128,160},{160,128},{192,224},{224,1... | collective-permute-start | bytes 552968 | tf_op jit(solution)/shard_map/ppermute | solution.py:390
  7.9 8.9 %collective-permute-start.2 = (f32[360,128]{1,0:T(8,128)S(1)}, f32[360,128]{1,0:T(8,128)S(1)}, u32[]{:S(2)}, u32[]{:S(2)}) collective-permute-start(f32[360,128]{1,0:T(8,128)S(1)} %get-tuple-element.39), channel_id=1, source_target_pairs={{0,224},{32,64},{64,32},{96,128},{128,96},{160,192},{192,160},{224... | collective-permute-start | bytes 552968 | tf_op jit(solution)/shard_map/ppermute | solution.py:391
  16.9 7.9 %collective-permute-start.3 = (f32[240,128]{1,0:T(8,128)S(1)}, f32[240,128]{1,0:T(8,128)S(1)}, u32[]{:S(2)}, u32[]{:S(2)}) collective-permute-start(f32[240,128]{1,0:T(8,128)S(1)} %get-tuple-element.41), channel_id=1, source_target_pairs={{0,128},{64,192},{128,0},{192,64},{1,129},{65,193},{129,1},{193,65... | collective-permute-start | bytes 368648 | tf_op jit(solution)/shard_map/ppermute | solution.py:364
  20.7 7.4 %collective-permute-start.4 = (f32[240,128]{1,0:T(8,128)S(1)}, f32[240,128]{1,0:T(8,128)S(1)}, u32[]{:S(2)}, u32[]{:S(2)}) collective-permute-start(f32[240,128]{1,0:T(8,128)S(1)} %get-tuple-element.42), channel_id=1, source_target_pairs={{0,64},{64,128},{128,192},{192,0},{1,65},{65,129},{129,193},{193,1... | collective-permute-start | bytes 368648 | tf_op jit(solution)/shard_map/ppermute | solution.py:364
  20.7 12.0 %collective-permute-start.5 = (f32[240,128]{1,0:T(8,128)S(1)}, f32[240,128]{1,0:T(8,128)S(1)}, u32[]{:S(2)}, u32[]{:S(2)}) collective-permute-start(f32[240,128]{1,0:T(8,128)S(1)} %get-tuple-element.43), channel_id=1, source_target_pairs={{0,192},{64,0},{128,64},{192,128},{1,193},{65,1},{129,65},{193,129... | collective-permute-start | bytes 368648 | tf_op jit(solution)/shard_map/ppermute | solution.py:364
  32.7 1.6 %collective-permute-start.6 = (f32[240,128]{1,0:T(8,128)S(1)}, f32[240,128]{1,0:T(8,128)S(1)}, u32[]{:S(2)}, u32[]{:S(2)}) collective-permute-start(f32[240,128]{1,0:T(8,128)S(1)} %shard_map.80.mine_ref), channel_id=1, source_target_pairs={{0,16},{16,0},{1,17},{17,1},{2,18},{18,2},{3,19},{19,3},{4,20},{20... | collective-permute-start | bytes 368648 | tf_op jit(solution)/shard_map/ppermute | solution.py:368
  51.2 3.3 %collective-permute-start.9 = (f32[16,128]{1,0:T(8,128)S(1)}, f32[16,128]{1,0:T(8,128)S(1)}, u32[]{:S(2)}, u32[]{:S(2)}) collective-permute-start(f32[16,128]{1,0:T(8,128)S(1)} %get-tuple-element.47.mine_ref), channel_id=1, source_target_pairs={{0,16},{16,0},{1,17},{17,1},{2,18},{18,2},{3,19},{19,3},{4,20},{20... | collective-permute-start | bytes 24584 | tf_op jit(solution)/shard_map/ppermute | solution.py:368
  52.8 3.9 %collective-permute-start.8 = (f32[40,128]{1,0:T(8,128)S(1)}, f32[40,128]{1,0:T(8,128)S(1)}, u32[]{:S(2)}, u32[]{:S(2)}) collective-permute-start(f32[40,128]{1,0:T(8,128)S(1)} %get-tuple-element.69), channel_id=1, source_target_pairs={{0,224},{32,64},{64,32},{96,128},{128,96},{160,192},{192,160},{224... | collective-permute-start | bytes 61448 | tf_op jit(solution)/shard_map/ppermute | solution.py:406
  54.5 2.9 %collective-permute-start.7 = (f32[40,128]{1,0:T(8,128)S(1)}, f32[40,128]{1,0:T(8,128)S(1)}, u32[]{:S(2)}, u32[]{:S(2)}) collective-permute-start(f32[40,128]{1,0:T(8,128)S(1)} %get-tuple-element.70), channel_id=1, source_target_pairs={{0,32},{32,0},{64,96},{96,64},{128,160},{160,128},{192,224},{224,1... | collective-permute-start | bytes 61448 | tf_op jit(solution)/shard_map/ppermute | solution.py:406
  57.4 6.9 %collective-permute-start.10 = (f32[80,128]{1,0:T(8,128)S(1)}, f32[80,128]{1,0:T(8,128)S(1)}, u32[]{:S(2)}, u32[]{:S(2)}) collective-permute-start(f32[80,128]{1,0:T(8,128)S(1)} %get-tuple-element.49), channel_id=1, source_target_pairs={{0,128},{64,192},{128,0},{192,64},{1,129},{65,193},{129,1},{193,65... | collective-permute-start | bytes 122888 | tf_op jit(solution)/shard_map/ppermute | solution.py:364
  60.8 5.3 %collective-permute-start.11 = (f32[80,128]{1,0:T(8,128)S(1)}, f32[80,128]{1,0:T(8,128)S(1)}, u32[]{:S(2)}, u32[]{:S(2)}) collective-permute-start(f32[80,128]{1,0:T(8,128)S(1)} %get-tuple-element.50), channel_id=1, source_target_pairs={{0,64},{64,128},{128,192},{192,0},{1,65},{65,129},{129,193},{193,1... | collective-permute-start | bytes 122888 | tf_op jit(solution)/shard_map/ppermute | solution.py:364
  61.3 5.3 %collective-permute-start.12 = (f32[80,128]{1,0:T(8,128)S(1)}, f32[80,128]{1,0:T(8,128)S(1)}, u32[]{:S(2)}, u32[]{:S(2)}) collective-permute-start(f32[80,128]{1,0:T(8,128)S(1)} %get-tuple-element.51), channel_id=1, source_target_pairs={{0,192},{64,0},{128,64},{192,128},{1,193},{65,1},{129,65},{193,129... | collective-permute-start | bytes 122888 | tf_op jit(solution)/shard_map/ppermute | solution.py:364
  66.6 2.6 %collective-permute-start.13 = (f32[80,128]{1,0:T(8,128)S(1)}, f32[80,128]{1,0:T(8,128)S(1)}, u32[]{:S(2)}, u32[]{:S(2)}) collective-permute-start(f32[80,128]{1,0:T(8,128)S(1)} %shard_map.85.mine_ref), channel_id=1, source_target_pairs={{0,16},{16,0},{1,17},{17,1},{2,18},{18,2},{3,19},{19,3},{4,20},{20... | collective-permute-start | bytes 122888 | tf_op jit(solution)/shard_map/ppermute | solution.py:368
  82.5 3.3 %collective-permute-start.14 = (f32[32,128]{1,0:T(8,128)S(1)}, f32[32,128]{1,0:T(8,128)S(1)}, u32[]{:S(2)}, u32[]{:S(2)}) collective-permute-start(f32[32,128]{1,0:T(8,128)S(1)} %get-tuple-element.53.own_ref), channel_id=1, source_target_pairs={{0,32},{32,0},{64,96},{96,64},{128,160},{160,128},{192,224},{224,1... | collective-permute-start | bytes 49160 | tf_op jit(solution)/shard_map/ppermute | solution.py:416
  84.0 7.9 %collective-permute-start.18 = (f32[16,128]{1,0:T(8,128)S(1)}, f32[16,128]{1,0:T(8,128)S(1)}, u32[]{:S(2)}, u32[]{:S(2)}) collective-permute-start(f32[16,128]{1,0:T(8,128)S(1)} %get-tuple-element.58.mine_ref), channel_id=1, source_target_pairs={{0,16},{16,0},{1,17},{17,1},{2,18},{18,2},{3,19},{19,3},{4,20},{20... | collective-permute-start | bytes 24584 | tf_op jit(solution)/shard_map/ppermute | solution.py:368
  85.8 9.6 %collective-permute-start.15 = (f32[64,128]{1,0:T(8,128)S(1)}, f32[64,128]{1,0:T(8,128)S(1)}, u32[]{:S(2)}, u32[]{:S(2)}) collective-permute-start(f32[64,128]{1,0:T(8,128)S(1)} %get-tuple-element.55), channel_id=1, source_target_pairs={{0,128},{64,192},{128,0},{192,64},{1,129},{65,193},{129,1},{193,65... | collective-permute-start | bytes 98312 | tf_op jit(solution)/shard_map/ppermute | solution.py:364
  88.2 7.3 %collective-permute-start.16 = (f32[64,128]{1,0:T(8,128)S(1)}, f32[64,128]{1,0:T(8,128)S(1)}, u32[]{:S(2)}, u32[]{:S(2)}) collective-permute-start(f32[64,128]{1,0:T(8,128)S(1)} %get-tuple-element.56), channel_id=1, source_target_pairs={{0,64},{64,128},{128,192},{192,0},{1,65},{65,129},{129,193},{193,1... | collective-permute-start | bytes 98312 | tf_op jit(solution)/shard_map/ppermute | solution.py:364
  91.6 4.0 %collective-permute-start.17 = (f32[64,128]{1,0:T(8,128)S(1)}, f32[64,128]{1,0:T(8,128)S(1)}, u32[]{:S(2)}, u32[]{:S(2)}) collective-permute-start(f32[64,128]{1,0:T(8,128)S(1)} %get-tuple-element.57), channel_id=1, source_target_pairs={{0,192},{64,0},{128,64},{192,128},{1,193},{65,1},{129,65},{193,129... | collective-permute-start | bytes 98312 | tf_op jit(solution)/shard_map/ppermute | solution.py:364
  95.5 4.8 %collective-permute-start.20 = (f32[192,128]{1,0:T(8,128)S(1)}, f32[192,128]{1,0:T(8,128)S(1)}, u32[]{:S(2)}, u32[]{:S(2)}) collective-permute-start(f32[192,128]{1,0:T(8,128)S(1)} %shard_map.90), channel_id=1, source_target_pairs={{0,16},{16,0},{1,17},{17,1},{2,18},{18,2},{3,19},{19,3},{4,20},{20... | collective-permute-start | bytes 294920 | tf_op jit(solution)/shard_map/ppermute | solution.py:368
  99.1 1.2 %collective-permute-start.19 = (f32[64,128]{1,0:T(8,128)S(1)}, f32[64,128]{1,0:T(8,128)S(1)}, u32[]{:S(2)}, u32[]{:S(2)}) collective-permute-start(f32[64,128]{1,0:T(8,128)S(1)} %get-tuple-element.54.refs_0_), channel_id=1, source_target_pairs={{0,16},{16,0},{1,17},{17,1},{2,18},{18,2},{3,19},{19,3},{4,20},{20... | collective-permute-start | bytes 98312 | tf_op jit(solution)/shard_map/ppermute | solution.py:368
